TPU v7x, 1024 devices: a whole 4x8x16 slice. The times are simulated.
1024 devices in a mesh: dp: 64 (over z_lo, x, core), expert: 16 (over y, z_hi).
Axes of the slice: x: 4, y: 8, z: 16 (z_hi: 2, z_lo: 8; z = z_hi * 8 + z_lo), core: 2. Of those that a mesh axis runs over, the one named last changes fastest.
Arguments:
- hidden: bfloat16 [131072, 1024], P(('dp', 'expert')), may hold values from -24 to 24
- expert_ids: int32 [131072, 1], P(('dp', 'expert')), may hold values from 0 to 15; in each aligned block of 128 rows (0 to 127, 128 to 255, ...) at most 10 rows name the same one
- gate_weights: float32 [131072, 1], P(('dp', 'expert')), may hold values from 0.2 to 1
- down_weight: bfloat16 [16, 1024, 2048], P('expert'), may hold values from -0.1875 to 0.1875
- out_grad: bfloat16 [131072, 2048], P(('dp', 'expert')), may hold values from -6 to 6
Outputs:
- layer_out: bfloat16 [131072, 2048], P(('dp', 'expert'))
- hidden_grad: bfloat16 [131072, 1024], P(('dp', 'expert'))
- gate_grad: float32 [131072, 1], P(('dp', 'expert'))
- weight_grad: float32 [16, 1024, 2048], P('expert', 'dp')
Inputs may be any that keep to these rules, and one draw needn't show every extreme that they name: `expert_ids`: among the 128 rows of one device no expert is named more than 10 times, a bound that some block reaches.
All inputs are finite; a program needn't handle non-finite values.
Results may differ from a plain program's by a relative error of at most 0.0049.
Values may be sent and summed in bfloat16 or wider, within the bound.
No kernel may reach another device: no remote copies, remote signals or barrier semaphores. Data moves between devices by JAX's collectives and lax.ppermute only.
A program may use at most 64 MiB of HBM per device.

v0:
```python
import jax
import jax.numpy as jnp
from jax import lax
from jax.sharding import PartitionSpec as P


def shards(hidden, expert_ids, gate_weights, down_weight, out_grad):
    tok_rows = hidden.shape[0]
    hid_width = hidden.shape[1]
    out_width = out_grad.shape[1]
    expert_count = lax.axis_size("expert")
    capacity = 5 * tok_rows // (4 * expert_count)
    expert_list = expert_ids[:, 0]
    onehot = (expert_list[:, None] == jnp.arange(expert_count, dtype=jnp.int32)[None, :]).astype(
        jnp.int32
    )
    row_rank = jnp.sum(onehot * (jnp.cumsum(onehot, axis=0) - 1), axis=1)
    slot_index = expert_list * capacity + row_rank
    placer = (
        jnp.arange(expert_count * capacity, dtype=jnp.int32)[:, None] == slot_index[None, :]
    ).astype(jnp.bfloat16)
    outgoing = jnp.dot(placer, hidden, preferred_element_type=jnp.float32).astype(jnp.bfloat16)
    received = lax.all_to_all(
        outgoing.reshape(expert_count, capacity, hid_width),
        "expert",
        split_axis=0,
        concat_axis=0,
        tiled=True,
    )
    weight = down_weight[0]
    hid_rows = received.reshape(expert_count * capacity, hid_width)
    proj_rows = jnp.dot(hid_rows, weight, preferred_element_type=jnp.float32).astype(jnp.bfloat16)
    proj_slots = lax.all_to_all(
        proj_rows.reshape(expert_count, capacity, out_width),
        "expert",
        split_axis=0,
        concat_axis=0,
        tiled=True,
    )
    projected = lax.dot_general(
        placer,
        proj_slots.reshape(expert_count * capacity, out_width),
        (((0,), (0,)), ((), ())),
        preferred_element_type=jnp.float32,
    )
    layer_out = (gate_weights * projected).astype(jnp.bfloat16)
    gate_grad = jnp.sum(out_grad.astype(jnp.float32) * projected, axis=1, keepdims=True)
    grad_rows = (gate_weights * out_grad.astype(jnp.float32)).astype(jnp.bfloat16)
    grad_slots = jnp.dot(placer, grad_rows, preferred_element_type=jnp.float32).astype(jnp.bfloat16)
    grad_arrived = lax.all_to_all(
        grad_slots.reshape(expert_count, capacity, out_width),
        "expert",
        split_axis=0,
        concat_axis=0,
        tiled=True,
    )
    grad_flat = grad_arrived.reshape(expert_count * capacity, out_width)
    back_rows = lax.dot_general(
        grad_flat, weight, (((1,), (1,)), ((), ())), preferred_element_type=jnp.float32
    ).astype(jnp.bfloat16)
    back_slots = lax.all_to_all(
        back_rows.reshape(expert_count, capacity, hid_width),
        "expert",
        split_axis=0,
        concat_axis=0,
        tiled=True,
    )
    partial_grad = lax.dot_general(
        hid_rows, grad_flat, (((0,), (0,)), ((), ())), preferred_element_type=jnp.float32
    )
    weight_grad = lax.psum_scatter(partial_grad, "dp", scatter_dimension=0, tiled=True)
    hidden_grad = lax.dot_general(
        placer,
        back_slots.reshape(expert_count * capacity, hid_width),
        (((0,), (0,)), ((), ())),
        preferred_element_type=jnp.float32,
    ).astype(jnp.bfloat16)
    return (layer_out, hidden_grad, gate_grad, weight_grad[None])


def solution(mesh):
    return jax.shard_map(
        shards,
        mesh=mesh,
        in_specs=(
            P(("dp", "expert"), None),
            P(("dp", "expert"), None),
            P(("dp", "expert"), None),
            P("expert", None, None),
            P(("dp", "expert"), None),
        ),
        out_specs=(
            P(("dp", "expert"), None),
            P(("dp", "expert"), None),
            P(("dp", "expert"), None),
            P("expert", "dp", None),
        ),
        check_vma=False,
    )
```

profile of v0, /device:TPU:24, one launch (start us, length us, event | category | flops | bytes accessed | tf_op | source)
XLA Modules:
  0.0 648.7 jit_solution(1937862215883419804)
XLA Ops:
  7.2 0.0 copy-start
  7.2 0.8 fusion.15
  8.0 0.2 reduce_window_sum.11
  8.1 0.8 select_reduce_fusion
  9.0 0.7 multiply_add_fusion
  9.6 0.0 copy-done
  9.6 0.2 convolution_convert_fusion.1
  9.9 0.9 reshape.40
  10.8 24.2 %all-to-all-start = ((bf16[16,10,1024]{2,1,0:T(8,128)(2,1)}), bf16[16,10,1024]{2,1,0:T(8,128)(2,1)S(1)}, u32[]{:S(2)}, u32[]{:S(2)}) async-start(bf16[16,10,1024]{2,1,0:T(8,128)(2,1)} %reshape.40), calls=%async_computation | async-start | bytes 1048576 | tf_op jit(solution)/shard_map/all_to_all | solution.py:23
  35.0 0.0 reduce-scatter.2.cloned.1.call-start
  35.1 1.4 convolution_convert_fusion
  36.5 0.2 reshape.44
  36.7 18.0 %all-to-all-done = bf16[16,10,1024]{2,1,0:T(8,128)(2,1)S(1)} async-done(((bf16[16,10,1024]{2,1,0:T(8,128)(2,1)}), bf16[16,10,1024]{2,1,0:T(8,128)(2,1)S(1)}, u32[]{:S(2)}, u32[]{:S(2)}) %all-to-all-start) | async-done | bytes 327712 | tf_op jit(solution)/shard_map/all_to_all | solution.py:23
  54.7 34.7 %all_to_all.20 = bf16[16,10,2048]{2,1,0:T(8,128)(2,1)S(1)} all-to-all(bf16[16,10,2048]{2,1,0:T(8,128)(2,1)S(1)} %reshape.44), channel_id=1, replica_groups=mesh['dp'=64,'expert'=16] {'expert'}, dimensions={0} | all-to-all | bytes 1310720 | tf_op jit(solution)/shard_map/all_to_all | solution.py:50
  89.4 4.5 convolution_bitcast_fusion
  93.9 0.0 reduce-scatter.2.cloned.1.call-update
  93.9 0.1 reshape.41
  94.1 3.0 fusion.4
  97.1 1.3 reshape.42
  98.4 16.7 %all-to-all-start.1 = ((bf16[16,10,2048]{2,1,0:T(8,128)(2,1)}), bf16[16,10,2048]{2,1,0:T(8,128)(2,1)S(1)}, u32[]{:S(2)}, u32[]{:S(2)}) async-start(bf16[16,10,2048]{2,1,0:T(8,128)(2,1)} %reshape.42), calls=%async_computation.1 | async-start | bytes 2097152 | tf_op jit(solution)/shard_map/all_to_all | solution.py:33
  115.1 0.2 reshape.45
  115.3 0.0 copy-start.1
  115.3 0.0 copy-start.2
  115.3 3.8 fusion.7
  119.1 0.9 reshape.46
  120.0 28.1 %all-to-all-done.1 = bf16[16,10,2048]{2,1,0:T(8,128)(2,1)S(1)} async-done(((bf16[16,10,2048]{2,1,0:T(8,128)(2,1)}), bf16[16,10,2048]{2,1,0:T(8,128)(2,1)S(1)}, u32[]{:S(2)}, u32[]{:S(2)}) %all-to-all-start.1) | async-done | bytes 655392 | tf_op jit(solution)/shard_map/all_to_all | solution.py:33
  148.1 13.2 %all-to-all-start.3 = ((bf16[16,10,1024]{2,1,0:T(8,128)(2,1)}), bf16[16,10,1024]{2,1,0:T(8,128)(2,1)S(1)}, u32[]{:S(2)}, u32[]{:S(2)}) async-start(bf16[16,10,1024]{2,1,0:T(8,128)(2,1)} %reshape.46), calls=%async_computation.3 | async-start | bytes 1048576 | tf_op jit(solution)/shard_map/all_to_all | solution.py:61
  161.3 0.2 reshape.43
  161.6 38.3 %all-to-all-done.3 = bf16[16,10,1024]{2,1,0:T(8,128)(2,1)S(1)} async-done(((bf16[16,10,1024]{2,1,0:T(8,128)(2,1)}), bf16[16,10,1024]{2,1,0:T(8,128)(2,1)S(1)}, u32[]{:S(2)}, u32[]{:S(2)}) %all-to-all-start.3) | async-done | bytes 327712 | tf_op jit(solution)/shard_map/all_to_all | solution.py:61
  199.9 0.1 reshape.47
  200.0 1.0 convolution_convert_fusion.2
  201.0 0.0 copy-done.1
  201.0 0.0 copy-done.2
  201.0 1.8 fusion.11
  202.7 439.1 %reduce-scatter.2.cloned.1.call-done = f32[16,2048]{1,0:T(8,128)} async-done(((f32[1024,2048]{1,0:T(8,128)}), f32[16,2048]{1,0:T(8,128)}) %reduce-scatter.2.cloned.1.call-update) | async-done | bytes 131088 | tf_op jit(solution)/shard_map/reduce_scatter | solution.py:71
Async XLA Ops:
  7.2 2.5 copy-start
  10.8 43.9 %all-to-all-start = ((bf16[16,10,1024]{2,1,0:T(8,128)(2,1)}), bf16[16,10,1024]{2,1,0:T(8,128)(2,1)S(1)}, u32[]{:S(2)}, u32[]{:S(2)}) async-start(bf16[16,10,1024]{2,1,0:T(8,128)(2,1)} %reshape.40), calls=%async_computation | async-start | bytes 1048576 | tf_op jit(solution)/shard_map/all_to_all | solution.py:23
  35.0 606.8 %reduce-scatter.2.cloned.1.call-start = ((), (), s32[]{:S(2)}) async-start(), calls=%async_computation.5 | async-start | bytes 8519680 | tf_op jit(solution)/shard_map/reduce_scatter | solution.py:71
  98.4 49.7 %all-to-all-start.1 = ((bf16[16,10,2048]{2,1,0:T(8,128)(2,1)}), bf16[16,10,2048]{2,1,0:T(8,128)(2,1)S(1)}, u32[]{:S(2)}, u32[]{:S(2)}) async-start(bf16[16,10,2048]{2,1,0:T(8,128)(2,1)} %reshape.42), calls=%async_computation.1 | async-start | bytes 2097152 | tf_op jit(solution)/shard_map/all_to_all | solution.py:33
  115.3 85.7 %copy-start.1 = (bf16[128,2048]{1,0:T(8,128)(2,1)S(1)}, bf16[128,2048]{1,0:T(8,128)(2,1)}, u32[]{:S(2)}) copy-start(bf16[128,2048]{1,0:T(8,128)(2,1)} %param.9) | copy-start | bytes 1572868
  115.3 85.7 %copy-start.2 = (f32[128,1]{0,1:T(1,128)S(1)}, f32[128,1]{0,1:T(1,128)}, u32[]{:S(2)}) copy-start(f32[128,1]{0,1:T(1,128)} %param.7) | copy-start | bytes 1540
  148.1 51.8 %all-to-all-start.3 = ((bf16[16,10,1024]{2,1,0:T(8,128)(2,1)}), bf16[16,10,1024]{2,1,0:T(8,128)(2,1)S(1)}, u32[]{:S(2)}, u32[]{:S(2)}) async-start(bf16[16,10,1024]{2,1,0:T(8,128)(2,1)} %reshape.46), calls=%async_computation.3 | async-start | bytes 1048576 | tf_op jit(solution)/shard_map/all_to_all | solution.py:61
Sparse Core Ops, SparseCore 0:
  94.1 547.7 reduce-scatter.1
where the time goes:
time: 649 us
  waiting for transfers between devices  523 us (81%)
  starting transfers between devices  54.2 us (8%)
  blocking collectives  34.7 us (5%)
  matrix products  15.7 us (2%)
  between operations  14.1 us (2%)
    reduce_scatter x1, waiting for transfers between devices, shards(): lax.psum_scatter(partial_grad, 'dp', scatter_dimension=0, tiled=True)  439 us
    all_to_all x1, waiting for transfers between devices, shards(): lax.all_to_all(back_rows.reshape(expert_count, capacity, hid_width), 'exp...  38.3 us
    all_to_all x1, blocking collectives, shards(): lax.all_to_all(grad_slots.reshape(expert_count, capacity, out_width), 'ex...  34.7 us
    all_to_all x1, waiting for transfers between devices, shards(): lax.all_to_all(proj_rows.reshape(expert_count, capacity, out_width), 'exp...  28.1 us
    all_to_all x1, starting transfers between devices, shards(): lax.all_to_all(outgoing.reshape(expert_count, capacity, hid_width), 'expe...  24.2 us
    all_to_all x1, waiting for transfers between devices, shards(): lax.all_to_all(outgoing.reshape(expert_count, capacity, hid_width), 'expe...  18 us
    all_to_all x1, starting transfers between devices, shards(): lax.all_to_all(proj_rows.reshape(expert_count, capacity, out_width), 'exp...  16.7 us
    all_to_all x1, starting transfers between devices, shards(): lax.all_to_all(back_rows.reshape(expert_count, capacity, hid_width), 'exp...  13.2 us
  transfers between devices with their start and end apart: 4, of which 4 were waited for; matrix products, arithmetic and copies ran while one was open for 2% of the time, Pallas kernels for 0%

commit v1 on v0

v1 whole, which is shorter than its diff:
```python
import jax
import jax.numpy as jnp
from jax import lax
from jax.sharding import Mesh, PartitionSpec as P

F32, BF16 = jnp.float32, jnp.bfloat16
DP = ("zl", "x", "c")
NEAR = ("x", "c")
EXP = ("y", "zh")


def exchange(rows, count, axes):
    tall, wide = rows.shape
    moved = lax.all_to_all(
        rows.reshape(count, tall // count, wide), axes, split_axis=0, concat_axis=0, tiled=True
    )
    return moved.reshape(tall, wide)


def dot(a, b, dims, out=BF16):
    return lax.dot_general(a, b, (dims, ((), ())), preferred_element_type=F32).astype(out)


def shards(hidden, expert_ids, gate_weights, down_weight, out_grad):
    tok_rows, hid_width = hidden.shape
    experts = lax.axis_size(EXP)
    near, lines = lax.axis_size(NEAR), lax.axis_size("zl")
    strip = hid_width // (near * lines)
    capacity = 5 * tok_rows // (4 * experts)
    weight = down_weight[0]

    expert_list = expert_ids[:, 0]
    onehot = (expert_list[:, None] == jnp.arange(experts, dtype=jnp.int32)[None, :]).astype(
        jnp.int32
    )
    row_rank = jnp.sum(onehot * (jnp.cumsum(onehot, axis=0) - 1), axis=1)
    slot_index = expert_list * capacity + row_rank
    placer = (
        jnp.arange(experts * capacity, dtype=jnp.int32)[:, None] == slot_index[None, :]
    ).astype(BF16)

    grad_rows = (gate_weights * out_grad.astype(F32)).astype(BF16)
    grad_flat = exchange(dot(placer, grad_rows, ((1,), (0,))), experts, EXP)
    hid_rows = exchange(dot(placer, hidden, ((1,), (0,))), experts, EXP)

    grad_near = lax.all_gather(grad_flat, NEAR, axis=0, tiled=True)
    place = jnp.arange(hid_width, dtype=jnp.int32)
    owner = place // strip
    target = ((owner % near) * lines + owner // near) * strip + place % strip
    sorter = (target[:, None] == place[None, :]).astype(BF16)
    sorted_rows = dot(hid_rows, sorter, ((1,), (0,)))
    hid_near = exchange(
        sorted_rows.reshape(-1, near, lines * strip).swapaxes(0, 1).reshape(-1, lines * strip),
        near,
        NEAR,
    )
    partial_grad = dot(hid_near, grad_near, ((0,), (0,)), F32)
    weight_grad = lax.psum_scatter(partial_grad, "zl", scatter_dimension=0, tiled=True)

    proj_slots = exchange(dot(hid_rows, weight, ((1,), (0,))), experts, EXP)
    back_slots = exchange(dot(grad_flat, weight, ((1,), (1,))), experts, EXP)
    projected = dot(placer, proj_slots, ((0,), (0,)), F32)
    layer_out = (gate_weights * projected).astype(BF16)
    gate_grad = jnp.sum(out_grad.astype(F32) * projected, axis=1, keepdims=True)
    hidden_grad = dot(placer, back_slots, ((0,), (0,)))
    return (layer_out, hidden_grad, gate_grad, weight_grad[None])


def solution(mesh):
    fine = Mesh(mesh.devices.reshape(8, 4, 2, 8, 2), DP + EXP)
    tokens = P(DP + EXP, None)
    return jax.shard_map(
        shards,
        mesh=fine,
        in_specs=(tokens, tokens, tokens, P(EXP, None, None), tokens),
        out_specs=(tokens, tokens, tokens, P(EXP, DP, None)),
        check_vma=False,
    )
```

time: 649 us -> 282 us (0.43)
  waiting for transfers between devices: 523 us -> 133 us
  blocking collectives: 34.7 us -> 50.5 us
    reduce_scatter x1, waiting for transfers between devices: 439 us -> 49.2 us  [shards(): lax.psum_scatter(partial_grad, 'zl', scatter_dimension=0, tiled=True)]
    all_to_all x1, blocking collectives: 34.7 us -> 50.5 us  [exchange(): lax.all_to_all(rows.reshape(count, tall // count, wide), axes, split_axis...]
    all_to_all x3 -> x4, starting transfers between devices: 54.2 us -> 58.6 us  [exchange(): lax.all_to_all(rows.reshape(count, tall // count, wide), axes, split_axis...]
    dot_general x7 -> x8, matrix products: 15.7 us -> 16.7 us  [dot(): lax.dot_general(a, b, (dims, ((), ())), preferred_element_type=F32)]
    all_to_all x3 -> x4, waiting for transfers between devices: 84.4 us -> 84.1 us  [exchange(): lax.all_to_all(rows.reshape(count, tall // count, wide), axes, split_axis...]
  transfers between devices with their start and end apart: 4 -> 6, of which waited for: 4 -> 5; matrix products, arithmetic and copies ran while one was open for 2% -> 7% of each run, Pallas kernels for 0% -> 0%
where the time goes in v1:
time: 282 us; the launch traced here: 281 us
  waiting for transfers between devices  133 us (47%)
  starting transfers between devices  58.6 us (21%)
  blocking collectives  50.5 us (18%)
  matrix products  16.7 us (6%)
  between operations  14.2 us (5%)
  local copies, waits for them, and re-layouts  5.57 us (2%)
    all_to_all x4, waiting for transfers between devices, exchange(): lax.all_to_all(rows.reshape(count, tall // count, wide), axes, split_axis...  84.1 us
    all_to_all x4, starting transfers between devices, exchange(): lax.all_to_all(rows.reshape(count, tall // count, wide), axes, split_axis...  58.6 us
    all_to_all x1, blocking collectives, exchange(): lax.all_to_all(rows.reshape(count, tall // count, wide), axes, split_axis...  50.5 us
    reduce_scatter x1, waiting for transfers between devices, shards(): lax.psum_scatter(partial_grad, 'zl', scatter_dimension=0, tiled=True)  49.2 us
    dot_general x8, matrix products, dot(): lax.dot_general(a, b, (dims, ((), ())), preferred_element_type=F32)  16.7 us
  transfers between devices with their start and end apart: 6, of which 5 were waited for; matrix products, arithmetic and copies ran while one was open for 7% of the time, Pallas kernels for 0%

profile of v1, /device:TPU:24, one launch (start us, length us, event | category | flops | bytes accessed | tf_op | source)
XLA Modules:
  0.0 281.3 jit_solution(11033333141901364530)
XLA Ops:
  7.2 0.0 copy-start
  7.2 0.0 all-gather.2.cloned.1.call-start
  7.2 0.8 fusion.19
  8.0 0.2 reduce_window_sum.11
  8.2 0.8 select_reduce_fusion
  9.0 0.7 multiply_add_fusion
  9.7 1.4 convolution_convert_fusion
  11.1 0.2 reshape.100
  11.3 50.5 %all_to_all.25 = bf16[16,10,2048]{2,1,0:T(8,128)(2,1)S(1)} all-to-all(bf16[16,10,2048]{2,1,0:T(8,128)(2,1)S(1)} %reshape.100), channel_id=1, replica_groups=mesh['zl'=8,'x'=4,'c'=2,'y'=8,'zh'=2] {'y','zh'}, dimensions={0} | all-to-all | bytes 1310720 | tf_op jit(solution)/shard_map/all_to_all | solution.py:14
  61.8 1.1 reshape.101
  62.9 0.0 all-gather.2.cloned.1.call-update
  62.9 0.0 copy-done
  62.9 0.2 convolution_convert_fusion.1
  63.2 0.9 reshape.96
  64.1 13.7 %all-to-all-start = ((bf16[16,10,1024]{2,1,0:T(8,128)(2,1)}), bf16[16,10,1024]{2,1,0:T(8,128)(2,1)S(1)}, u32[]{:S(2)}, u32[]{:S(2)}) async-start(bf16[16,10,1024]{2,1,0:T(8,128)(2,1)} %reshape.96), calls=%async_computation | async-start | bytes 1048576 | tf_op jit(solution)/shard_map/all_to_all | solution.py:14
  77.8 26.1 %all-to-all-done = bf16[16,10,1024]{2,1,0:T(8,128)(2,1)S(1)} async-done(((bf16[16,10,1024]{2,1,0:T(8,128)(2,1)}), bf16[16,10,1024]{2,1,0:T(8,128)(2,1)S(1)}, u32[]{:S(2)}, u32[]{:S(2)}) %all-to-all-start) | async-done | bytes 327712 | tf_op jit(solution)/shard_map/all_to_all | solution.py:14
  103.9 0.1 reshape.97
  104.1 1.0 fusion.13
  105.1 0.8 copy.12
  105.9 4.3 %all-to-all-start.4 = ((bf16[8,160,128]{2,1,0:T(8,128)(2,1)}), bf16[8,160,128]{2,1,0:T(8,128)(2,1)S(1)}, u32[]{:S(2)}, u32[]{:S(2)}) async-start(bf16[8,160,128]{2,1,0:T(8,128)(2,1)} %bitcast.30), calls=%async_computation.4 | async-start | bytes 655360 | tf_op jit(solution)/shard_map/all_to_all | solution.py:14
  110.2 3.0 %fusion.5 = bf16[160,2048]{1,0:T(8,128)(2,1)S(1)} fusion(bf16[160,1024]{1,0:T(8,128)(2,1)S(1)} %reshape.97, bf16[1,1024,2048]{2,1,0:T(8,128)(2,1)} %param.8), kind=kOutput, calls=%fused_computation.6 | convolution fusion | flops 671416320 | bytes 5177344 | tf_op jit(solution)/shard_map/dot_general | solution.py:21
  113.2 1.2 reshape.98
  114.5 4.0 %all-to-all-done.4 = bf16[8,160,128]{2,1,0:T(8,128)(2,1)S(1)} async-done(((bf16[8,160,128]{2,1,0:T(8,128)(2,1)}), bf16[8,160,128]{2,1,0:T(8,128)(2,1)S(1)}, u32[]{:S(2)}, u32[]{:S(2)}) %all-to-all-start.4) | async-done | bytes 327712 | tf_op jit(solution)/shard_map/all_to_all | solution.py:14
  118.4 28.9 %all-to-all-start.1 = ((bf16[16,10,2048]{2,1,0:T(8,128)(2,1)}), bf16[16,10,2048]{2,1,0:T(8,128)(2,1)S(1)}, u32[]{:S(2)}, u32[]{:S(2)}) async-start(bf16[16,10,2048]{2,1,0:T(8,128)(2,1)} %reshape.98), calls=%async_computation.1 | async-start | bytes 2097152 | tf_op jit(solution)/shard_map/all_to_all | solution.py:14
  147.4 0.0 copy-start.1
  147.4 0.0 reduce-scatter.2.cloned.1.call-start
  147.4 0.0 all-gather.2.cloned.1.call-done
  147.4 4.4 %fusion.42 = f32[128,2048]{1,0:T(8,128)} fusion(bf16[1280,128]{1,0:T(8,128)(2,1)S(1)} %bitcast.31, bf16[1280,2048]{1,0:T(8,128)(2,1)} %all-gather.2.cloned.1.call-done), kind=kOutput, calls=%fused_computation.58 | convolution fusion | flops 671088640 | bytes 6619136 | tf_op jit(solution)/shard_map/dot_general | solution.py:21
  151.9 0.0 reduce-scatter.2.cloned.1.call-update
  151.9 0.0 copy-done.1
  151.9 0.0 copy-start.2
  151.9 0.0 copy-start.3
  151.9 3.8 %fusion.10 = bf16[160,1024]{1,0:T(8,128)(2,1)S(1)} fusion(bf16[160,2048]{1,0:T(8,128)(2,1)S(1)} %copy-done.1, bf16[1,1024,2048]{2,1,0:T(8,128)(2,1)} %param.8), kind=kOutput, calls=%fused_computation.12 | convolution fusion | flops 671252480 | bytes 5177344 | tf_op jit(solution)/shard_map/dot_general | solution.py:21
  155.7 0.9 reshape.102
  156.6 19.5 %all-to-all-done.1 = bf16[16,10,2048]{2,1,0:T(8,128)(2,1)S(1)} async-done(((bf16[16,10,2048]{2,1,0:T(8,128)(2,1)}), bf16[16,10,2048]{2,1,0:T(8,128)(2,1)S(1)}, u32[]{:S(2)}, u32[]{:S(2)}) %all-to-all-start.1) | async-done | bytes 655392 | tf_op jit(solution)/shard_map/all_to_all | solution.py:14
  176.1 11.6 %all-to-all-start.3 = ((bf16[16,10,1024]{2,1,0:T(8,128)(2,1)}), bf16[16,10,1024]{2,1,0:T(8,128)(2,1)S(1)}, u32[]{:S(2)}, u32[]{:S(2)}) async-start(bf16[16,10,1024]{2,1,0:T(8,128)(2,1)} %reshape.102), calls=%async_computation.3 | async-start | bytes 1048576 | tf_op jit(solution)/shard_map/all_to_all | solution.py:14
  187.6 0.2 reshape.99
  187.9 34.6 %all-to-all-done.3 = bf16[16,10,1024]{2,1,0:T(8,128)(2,1)S(1)} async-done(((bf16[16,10,1024]{2,1,0:T(8,128)(2,1)}), bf16[16,10,1024]{2,1,0:T(8,128)(2,1)S(1)}, u32[]{:S(2)}, u32[]{:S(2)}) %all-to-all-start.3) | async-done | bytes 327712 | tf_op jit(solution)/shard_map/all_to_all | solution.py:14
  222.4 0.1 reshape.103
  222.5 1.0 convolution_convert_fusion.2
  223.5 0.0 copy-done.2
  223.5 0.0 copy-done.3
  223.5 1.8 fusion.15
  225.3 49.2 %reduce-scatter.2.cloned.1.call-done = f32[16,2048]{1,0:T(8,128)} async-done(((f32[128,2048]{1,0:T(8,128)}), f32[16,2048]{1,0:T(8,128)}) %reduce-scatter.2.cloned.1.call-update) | async-done | bytes 131088 | tf_op jit(solution)/shard_map/reduce_scatter | solution.py:58
  (1 shorter events, 0.0 us)
Async XLA Ops:
  7.2 55.7 %copy-start = (bf16[128,1024]{1,0:T(8,128)(2,1)S(1)}, bf16[128,1024]{1,0:T(8,128)(2,1)}, u32[]{:S(2)}) copy-start(bf16[128,1024]{1,0:T(8,128)(2,1)} %param.5) | copy-start | bytes 786436
  7.2 140.3 %all-gather.2.cloned.1.call-start = ((), (), s32[]{:S(2)}) async-start(), calls=%async_computation.6 | async-start | bytes 5898240 | tf_op jit(solution)/shard_map/all_gather | solution.py:46
  64.1 39.9 %all-to-all-start = ((bf16[16,10,1024]{2,1,0:T(8,128)(2,1)}), bf16[16,10,1024]{2,1,0:T(8,128)(2,1)S(1)}, u32[]{:S(2)}, u32[]{:S(2)}) async-start(bf16[16,10,1024]{2,1,0:T(8,128)(2,1)} %reshape.96), calls=%async_computation | async-start | bytes 1048576 | tf_op jit(solution)/shard_map/all_to_all | solution.py:14
  105.9 12.6 %all-to-all-start.4 = ((bf16[8,160,128]{2,1,0:T(8,128)(2,1)}), bf16[8,160,128]{2,1,0:T(8,128)(2,1)S(1)}, u32[]{:S(2)}, u32[]{:S(2)}) async-start(bf16[8,160,128]{2,1,0:T(8,128)(2,1)} %bitcast.30), calls=%async_computation.4 | async-start | bytes 655360 | tf_op jit(solution)/shard_map/all_to_all | solution.py:14
  118.4 57.6 %all-to-all-start.1 = ((bf16[16,10,2048]{2,1,0:T(8,128)(2,1)}), bf16[16,10,2048]{2,1,0:T(8,128)(2,1)S(1)}, u32[]{:S(2)}, u32[]{:S(2)}) async-start(bf16[16,10,2048]{2,1,0:T(8,128)(2,1)} %reshape.98), calls=%async_computation.1 | async-start | bytes 2097152 | tf_op jit(solution)/shard_map/all_to_all | solution.py:14
  147.4 4.5 %copy-start.1 = (bf16[160,2048]{1,0:T(8,128)(2,1)S(1)}, bf16[160,2048]{1,0:T(8,128)(2,1)}, u32[]{:S(2)}) copy-start(bf16[160,2048]{1,0:T(8,128)(2,1)} %reshape.101) | copy-start | bytes 1966084
  147.4 127.1 %reduce-scatter.2.cloned.1.call-start = ((), (), s32[]{:S(2)}) async-start(), calls=%async_computation.7 | async-start | bytes 1179648 | tf_op jit(solution)/shard_map/reduce_scatter | solution.py:58
  151.9 71.6 %copy-start.2 = (bf16[128,2048]{1,0:T(8,128)(2,1)S(1)}, bf16[128,2048]{1,0:T(8,128)(2,1)}, u32[]{:S(2)}) copy-start(bf16[128,2048]{1,0:T(8,128)(2,1)} %param.9) | copy-start | bytes 1572868
  151.9 71.6 %copy-start.3 = (f32[128,1]{0,1:T(1,128)S(1)}, f32[128,1]{0,1:T(1,128)}, u32[]{:S(2)}) copy-start(f32[128,1]{0,1:T(1,128)} %param.7) | copy-start | bytes 1540
  176.1 46.4 %all-to-all-start.3 = ((bf16[16,10,1024]{2,1,0:T(8,128)(2,1)}), bf16[16,10,1024]{2,1,0:T(8,128)(2,1)S(1)}, u32[]{:S(2)}, u32[]{:S(2)}) async-start(bf16[16,10,1024]{2,1,0:T(8,128)(2,1)} %reshape.102), calls=%async_computation.3 | async-start | bytes 1048576 | tf_op jit(solution)/shard_map/all_to_all | solution.py:14
Sparse Core Ops, SparseCore 0:
  63.0 79.4 all-gather.1
  152.2 122.2 reduce-scatter.1

commit v2 on v1

v2 whole, which is shorter than its diff:
```python
import jax
import jax.numpy as jnp
from jax import lax
from jax.sharding import Mesh, PartitionSpec as P

F32, BF16, I32 = jnp.float32, jnp.bfloat16, jnp.int32
LINE = ("zq", "zp")
DP = LINE + ("x", "c")
EXP = ("y", "zh")
NEAR = ("x", "c")
SHARE = ("zp", "x", "c")
RING = ("zh",) + LINE


def exchange(blocks, axes):
    return lax.all_to_all(blocks, axes, split_axis=0, concat_axis=0, tiled=True)


def dot(a, b, dims, out=BF16):
    return lax.dot_general(a, b, (dims, ((), ())), preferred_element_type=F32).astype(out)


def chooser(wanted, count):
    return (wanted[:, None] == jnp.arange(count, dtype=I32)[None, :]).astype(BF16)


def shards(hidden, expert_ids, gate_weights, down_weight, out_grad):
    tok_rows, hid_width = hidden.shape
    out_width = out_grad.shape[1]
    columns, halves = lax.axis_size("y"), lax.axis_size("zh")
    experts = columns * halves
    xs, cs, near, lines = (lax.axis_size(axes) for axes in ("x", "c", NEAR, LINE))
    capacity = 5 * tok_rows // (4 * experts)
    slots = capacity + -capacity % 4
    block = halves * slots
    tall = columns * block
    strip = hid_width // lax.axis_size(DP)
    half = lax.axis_index("zh")
    weight = down_weight[0]

    part = hid_width // lax.axis_size(SHARE)
    share = lax.dynamic_slice_in_dim(weight, lax.axis_index(SHARE) * part, part, axis=0)
    share = lax.ppermute(share, "zh", [(0, 1), (1, 0)])

    expert_list = expert_ids[:, 0]
    onehot = (expert_list[:, None] == jnp.arange(experts, dtype=I32)[None, :]).astype(I32)
    row_rank = jnp.sum(onehot * (jnp.cumsum(onehot, axis=0) - 1), axis=1)
    slot_index = expert_list * slots + row_rank
    placer = (jnp.arange(tall, dtype=I32)[:, None] == slot_index[None, :]).astype(BF16)
    grad_rows = (gate_weights * out_grad.astype(F32)).astype(BF16)
    outgoing = jnp.concatenate(
        [dot(placer, grad_rows, ((1,), (0,))), dot(placer, hidden, ((1,), (0,)))], axis=1
    )
    arrived = exchange(outgoing.reshape(columns, block, -1), "y").reshape(tall, -1)
    arrived, share = lax.optimization_barrier((arrived, share))
    other_weight = lax.all_gather(share, SHARE, axis=0, tiled=True)
    grad_flat, hid_flat = arrived[:, :out_width], arrived[:, out_width:]

    full = jnp.arange(columns * halves * capacity, dtype=I32)
    compact = chooser(full // capacity * slots + full % capacity, tall)
    place = jnp.arange(hid_width, dtype=I32)
    in_quarter = place % (hid_width // xs)
    source = (
        in_quarter // (cs * strip) * (near * strip)
        + place // (hid_width // xs) * (cs * strip)
        + in_quarter % (cs * strip)
    )
    sorter = chooser(source, hid_width)
    hid_sorted = dot(dot(compact, hid_flat, ((1,), (0,))), sorter, ((1,), (1,)))
    grad_sorted = dot(compact, grad_flat, ((1,), (0,)))
    rows = full.shape[0]
    blocks = [
        jnp.concatenate(
            [
                hid_sorted[:, x * (hid_width // xs) : (x + 1) * (hid_width // xs)],
                grad_sorted[:, c * (out_width // cs) : (c + 1) * (out_width // cs)],
            ],
            axis=1,
        )
        for x in range(xs)
        for c in range(cs)
    ]
    near_rows = exchange(jnp.stack(blocks), NEAR).reshape(near * rows, -1)
    hid_near, grad_near = near_rows[:, : hid_width // xs], near_rows[:, hid_width // xs :]
    of_half = (jnp.arange(near * rows, dtype=I32) // capacity % halves)[:, None]
    zero = jnp.zeros((), BF16)
    by_half = jnp.concatenate(
        [jnp.where(of_half == h, hid_near, zero) for h in range(halves)], axis=1
    )
    partial_grad = dot(by_half, grad_near, ((0,), (0,)), F32)
    ring_sum = lax.psum_scatter(partial_grad, RING, scatter_dimension=0, tiled=True)

    own = (jnp.arange(tall, dtype=I32) // slots % halves)[:, None] == half
    proj = jnp.where(
        own, dot(hid_flat, weight, ((1,), (0,))), dot(hid_flat, other_weight, ((1,), (0,)))
    )
    back = jnp.where(
        own, dot(grad_flat, weight, ((1,), (1,))), dot(grad_flat, other_weight, ((1,), (1,)))
    )
    returned = exchange(
        jnp.concatenate([proj, back], axis=1).reshape(columns, block, -1), "y"
    ).reshape(tall, -1)
    returned, ring_sum = lax.optimization_barrier((returned, ring_sum))
    projected = dot(placer, returned[:, :out_width], ((0,), (0,)), F32)
    layer_out = (gate_weights * projected).astype(BF16)
    gate_grad = jnp.sum(out_grad.astype(F32) * projected, axis=1, keepdims=True)
    hidden_grad = dot(placer, returned[:, out_width:], ((0,), (0,)))

    core = lax.axis_index("c")
    kept = lax.dynamic_slice_in_dim(ring_sum, core * strip, strip, axis=0)
    given = lax.dynamic_slice_in_dim(ring_sum, (1 - core) * strip, strip, axis=0)
    taken = lax.ppermute(given, "c", [(0, 1), (1, 0)])
    first = core == 0
    weight_grad = jnp.concatenate(
        [jnp.where(first, kept, taken), jnp.where(first, taken, kept)], axis=1
    )
    return (layer_out, hidden_grad, gate_grad, weight_grad[None])


def solution(mesh):
    fine = Mesh(mesh.devices.reshape(4, 2, 4, 2, 8, 2), DP + EXP)
    tokens = P(DP + EXP, None)
    return jax.shard_map(
        shards,
        mesh=fine,
        in_specs=(tokens, tokens, tokens, P(EXP, None, None), tokens),
        out_specs=(tokens, tokens, tokens, P(EXP, DP, None)),
        check_vma=False,
    )
```

time: 282 us -> 232 us (0.82)
  the two profiles are of different devices: /device:TPU:24 before, /device:TPU:6 now
where the time goes in v2:
time: 232 us; the launch traced here: 230 us
  waiting for transfers between devices  142 us (61%)
  starting transfers between devices  40 us (17%)
  matrix products  16.5 us (7%)
  between operations  15.7 us (7%)
  other arithmetic  12.6 us (5%)
  local copies, waits for them, and re-layouts  2.67 us (1%)
    reduce_scatter x1, waiting for transfers between devices, shards(): lax.psum_scatter(partial_grad, RING, scatter_dimension=0, tiled=True)  73.3 us
    all_to_all x3, waiting for transfers between devices, exchange(): return lax.all_to_all(blocks, axes, split_axis=0, concat_axis=0, tiled=True)  58.1 us
    ppermute x1, starting transfers between devices, shards(): share = lax.ppermute(share, 'zh', [(0, 1), (1, 0)])  19.4 us
    all_to_all x3, starting transfers between devices, exchange(): return lax.all_to_all(blocks, axes, split_axis=0, concat_axis=0, tiled=True)  18.7 us
    dot_general x11, matrix products, dot(): lax.dot_general(a, b, (dims, ((), ())), preferred_element_type=F32)  16.5 us
    ppermute x1, waiting for transfers between devices, shards(): share = lax.ppermute(share, 'zh', [(0, 1), (1, 0)])  6.31 us
    unnamed x7, other arithmetic  5.55 us
  transfers between devices with their start and end apart: 7, of which 6 were waited for; matrix products, arithmetic and copies ran while one was open for 10% of the time, Pallas kernels for 0%

profile of v2, /device:TPU:6, one launch (start us, length us, event | category | flops | bytes accessed | tf_op | source)
XLA Modules:
  0.0 229.9 jit_solution(14832191597820160406)
XLA Ops:
  8.0 0.0 copy-start
  8.0 0.8 fusion.57
  8.8 0.2 reduce_window_sum.11
  9.0 0.8 select_reduce_fusion
  9.8 0.7 multiply_add_fusion
  10.5 0.0 copy-done
  10.5 0.3 convolution_convert_fusion.4
  10.7 1.5 convolution_convert_fusion.1
  12.2 1.1 pad_maximum_fusion
  13.4 7.1 %all-to-all-start = ((bf16[8,24,3072]{2,1,0:T(8,128)(2,1)}), bf16[8,24,3072]{2,1,0:T(8,128)(2,1)S(1)}, u32[]{:S(2)}, u32[]{:S(2)}) async-start(bf16[8,24,3072]{2,1,0:T(8,128)(2,1)} %bitcast.2), calls=%async_computation | async-start | bytes 2359296 | tf_op jit(solution)/shard_map/all_to_all | solution.py:16
  20.5 0.0 all-gather.2.cloned.1.call-start
  20.5 1.0 dynamic-slice_bitcast_fusion
  21.5 19.4 %collective-permute-start = (bf16[64,2048]{1,0:T(8,128)(2,1)S(1)}, bf16[64,2048]{1,0:T(8,128)(2,1)S(1)}, u32[]{:S(2)}, u32[]{:S(2)}) collective-permute-start(bf16[64,2048]{1,0:T(8,128)(2,1)S(1)} %dynamic-slice_bitcast_fusion), channel_id=1, source_target_pairs={{0,1},{1,0},{2,3},{3,2},{4,5},{5,4},{6,7},{7,6},{8,9},{9,8},{10,11... | collective-permute-start | bytes 786440 | tf_op jit(solution)/shard_map/ppermute | solution.py:43
  40.9 6.3 %collective-permute-done = bf16[64,2048]{1,0:T(8,128)(2,1)S(1)} collective-permute-done((bf16[64,2048]{1,0:T(8,128)(2,1)S(1)}, bf16[64,2048]{1,0:T(8,128)(2,1)S(1)}, u32[]{:S(2)}, u32[]{:S(2)}) %collective-permute-start) | collective-permute-done | bytes 262176 | tf_op jit(solution)/shard_map/ppermute | solution.py:43
  47.2 0.0 copy-start.5
  47.2 4.9 %all-to-all-done = bf16[8,24,3072]{2,1,0:T(8,128)(2,1)S(1)} async-done(((bf16[8,24,3072]{2,1,0:T(8,128)(2,1)}), bf16[8,24,3072]{2,1,0:T(8,128)(2,1)S(1)}, u32[]{:S(2)}, u32[]{:S(2)}) %all-to-all-start) | async-done | bytes 1179680 | tf_op jit(solution)/shard_map/all_to_all | solution.py:16
  52.0 0.0 copy-start.1
  52.1 0.0 copy-done.5
  52.1 0.0 all-gather.2.cloned.1.call-update
  52.1 1.2 fusion.20
  53.3 0.4 convolution_convert_fusion.2
  53.8 0.0 copy-done.1
  53.8 0.8 fusion.46
  54.6 0.8 fusion.48
  55.4 0.8 fusion.42
  56.2 0.8 fusion.44
  56.9 0.8 fusion.38
  57.7 0.8 fusion.40
  58.5 0.8 fusion.34
  59.3 0.8 fusion.36
  60.1 4.8 %all-to-all-start.2 = ((bf16[8,160,1280]{2,1,0:T(8,128)(2,1)}), bf16[8,160,1280]{2,1,0:T(8,128)(2,1)S(1)}, u32[]{:S(2)}, u32[]{:S(2)}) async-start(bf16[8,160,1280]{2,1,0:T(8,128)(2,1)} %fusion.36), calls=%async_computation.2 | async-start | bytes 6553600 | tf_op jit(solution)/shard_map/all_to_all | solution.py:16
  64.9 0.0 reduce-scatter.2.cloned.1.call-start
  64.9 53.3 %all-to-all-done.2 = bf16[8,160,1280]{2,1,0:T(8,128)(2,1)S(1)} async-done(((bf16[8,160,1280]{2,1,0:T(8,128)(2,1)}), bf16[8,160,1280]{2,1,0:T(8,128)(2,1)S(1)}, u32[]{:S(2)}, u32[]{:S(2)}) %all-to-all-start.2) | async-done | bytes 3276832 | tf_op jit(solution)/shard_map/all_to_all | solution.py:16
  118.2 0.8 broadcast_select_fusion.1
  119.0 2.9 %fusion.5 = f32[512,1024]{1,0:T(8,128)} fusion(bf16[1280,1280]{1,0:T(8,128)(2,1)S(1)} %bitcast.62, bf16[1280,256]{1,0:T(8,128)(2,1)S(1)} %get-tuple-element.13, bf16[1280,256]{1,0:T(8,128)(2,1)S(1)} %get-tuple-element.12), kind=kOutput, calls=%fused_computation.6 | convolution fusion | flops 1344798720 | bytes 6029312 | tf_op jit(solution)/shard_map/dot_general | solution.py:20
  121.9 0.0 reduce-scatter.2.cloned.1.call-update
  122.0 0.0 copy-start.2
  122.0 4.4 %all-gather.2.cloned.1.call-done = bf16[1024,2048]{1,0:T(8,128)(2,1)} async-done(((bf16[64,2048]{1,0:T(8,128)(2,1)}), bf16[1024,2048]{1,0:T(8,128)(2,1)}) %all-gather.2.cloned.1.call-update) | async-done | bytes 4194320 | tf_op jit(solution)/shard_map/all_gather | solution.py:56
  126.4 0.0 copy-start.3
  126.4 3.4 %convolution_convert_fusion = bf16[192,2048]{1,0:T(8,128)(2,1)S(1)} fusion(bf16[1024,2048]{1,0:T(8,128)(2,1)} %all-gather.2.cloned.1.call-done, bf16[192,3072]{1,0:T(8,128)(2,1)} %bitcast.65), kind=kOutput, calls=%fused_computation.9 | convolution fusion | flops 805699584 | bytes 5373952 | tf_op jit(solution)/shard_map/dot_general | solution.py:20
  129.8 0.0 copy-done.2
  129.9 0.1 copy-done.3
  130.0 0.0 copy-start.7
  130.0 1.5 convolution_convert_fusion.3
  131.5 0.6 copy-done.7
  132.2 1.5 fusion.21
  133.7 1.0 fusion.10
  134.7 0.0 copy-start.4
  134.7 0.0 copy-start.8
  134.8 1.1 pad_maximum_fusion.1
  135.9 6.8 %all-to-all-start.1 = ((bf16[8,24,3072]{2,1,0:T(8,128)(2,1)}), bf16[8,24,3072]{2,1,0:T(8,128)(2,1)S(1)}, u32[]{:S(2)}, u32[]{:S(2)}) async-start(bf16[8,24,3072]{2,1,0:T(8,128)(2,1)} %bitcast.6), calls=%async_computation.1 | async-start | bytes 2359296 | tf_op jit(solution)/shard_map/all_to_all | solution.py:16
  142.7 73.3 %reduce-scatter.2.cloned.1.call-done = f32[32,1024]{1,0:T(8,128)} async-done(((f32[512,1024]{1,0:T(8,128)}), f32[32,1024]{1,0:T(8,128)}) %reduce-scatter.2.cloned.1.call-update) | async-done | bytes 131088 | tf_op jit(solution)/shard_map/reduce_scatter | solution.py:91
  216.0 0.0 copy-start.6
  216.0 0.0 all-to-all-done.1
  216.0 0.0 copy-done.4
  216.0 0.0 copy-done.8
  216.0 1.8 fusion.25
  217.8 0.8 constant_dynamic-slice_fusion
  218.6 1.9 collective-permute-start.1
  220.5 1.0 convolution_convert_fusion.6
  221.5 0.2 collective-permute-done.1
  221.8 0.0 copy-done.6
  221.8 0.7 maximum_bitcast_fusion
  (7 shorter events, 0.1 us)
Async XLA Ops:
  8.0 2.5 %copy-start = (bf16[128,1024]{1,0:T(8,128)(2,1)S(1)}, bf16[128,1024]{1,0:T(8,128)(2,1)}, u32[]{:S(2)}) copy-start(bf16[128,1024]{1,0:T(8,128)(2,1)} %param.5) | copy-start | bytes 786436
  13.4 38.7 %all-to-all-start = ((bf16[8,24,3072]{2,1,0:T(8,128)(2,1)}), bf16[8,24,3072]{2,1,0:T(8,128)(2,1)S(1)}, u32[]{:S(2)}, u32[]{:S(2)}) async-start(bf16[8,24,3072]{2,1,0:T(8,128)(2,1)} %bitcast.2), calls=%async_computation | async-start | bytes 2359296 | tf_op jit(solution)/shard_map/all_to_all | solution.py:16
  20.5 105.9 %all-gather.2.cloned.1.call-start = ((), (), s32[]{:S(2)}) async-start(), calls=%async_computation.4 | async-start | bytes 4456448 | tf_op jit(solution)/shard_map/all_gather | solution.py:56
  21.5 25.7 %collective-permute-start = (bf16[64,2048]{1,0:T(8,128)(2,1)S(1)}, bf16[64,2048]{1,0:T(8,128)(2,1)S(1)}, u32[]{:S(2)}, u32[]{:S(2)}) collective-permute-start(bf16[64,2048]{1,0:T(8,128)(2,1)S(1)} %dynamic-slice_bitcast_fusion), channel_id=1, source_target_pairs={{0,1},{1,0},{2,3},{3,2},{4,5},{5,4},{6,7},{7,6},{8,9},{9,8},{10,11... | collective-permute-start | bytes 786440 | tf_op jit(solution)/shard_map/ppermute | solution.py:43
  47.2 4.9 %copy-start.5 = (bf16[64,2048]{1,0:T(8,128)(2,1)}, bf16[64,2048]{1,0:T(8,128)(2,1)S(1)}, u32[]{:S(2)}) copy-start(bf16[64,2048]{1,0:T(8,128)(2,1)S(1)} %collective-permute-done) | copy-start | bytes 786436
  52.0 1.7 copy-start.1
  60.1 58.1 %all-to-all-start.2 = ((bf16[8,160,1280]{2,1,0:T(8,128)(2,1)}), bf16[8,160,1280]{2,1,0:T(8,128)(2,1)S(1)}, u32[]{:S(2)}, u32[]{:S(2)}) async-start(bf16[8,160,1280]{2,1,0:T(8,128)(2,1)} %fusion.36), calls=%async_computation.2 | async-start | bytes 6553600 | tf_op jit(solution)/shard_map/all_to_all | solution.py:16
  64.9 151.1 %reduce-scatter.2.cloned.1.call-start = ((), (), s32[]{:S(2)}) async-start(), calls=%async_computation.5 | async-start | bytes 2228224 | tf_op jit(solution)/shard_map/reduce_scatter | solution.py:91
  122.0 7.9 %copy-start.2 = (bf16[8,24,3072]{2,1,0:T(8,128)(2,1)S(1)}, bf16[8,24,3072]{2,1,0:T(8,128)(2,1)}, u32[]{:S(2)}) copy-start(bf16[8,24,3072]{2,1,0:T(8,128)(2,1)} %copy-done.1) | copy-start | bytes 3538948
  126.4 3.6 %copy-start.3 = (bf16[1024,2048]{1,0:T(8,128)(2,1)S(1)}, bf16[1024,2048]{1,0:T(8,128)(2,1)}, u32[]{:S(2)}) copy-start(bf16[1024,2048]{1,0:T(8,128)(2,1)} %all-gather.2.cloned.1.call-done) | copy-start | bytes 12582916
  130.0 2.2 copy-start.7
  134.7 81.3 %copy-start.4 = (bf16[128,2048]{1,0:T(8,128)(2,1)S(1)}, bf16[128,2048]{1,0:T(8,128)(2,1)}, u32[]{:S(2)}) copy-start(bf16[128,2048]{1,0:T(8,128)(2,1)} %param.9) | copy-start | bytes 1572868
  134.7 81.3 %copy-start.8 = (f32[128,1]{0,1:T(1,128)S(1)}, f32[128,1]{0,1:T(1,128)}, u32[]{:S(2)}) copy-start(f32[128,1]{0,1:T(1,128)} %param.7) | copy-start | bytes 1540
  135.9 80.1 %all-to-all-start.1 = ((bf16[8,24,3072]{2,1,0:T(8,128)(2,1)}), bf16[8,24,3072]{2,1,0:T(8,128)(2,1)S(1)}, u32[]{:S(2)}, u32[]{:S(2)}) async-start(bf16[8,24,3072]{2,1,0:T(8,128)(2,1)} %bitcast.6), calls=%async_computation.1 | async-start | bytes 2359296 | tf_op jit(solution)/shard_map/all_to_all | solution.py:16
  216.0 5.8 %copy-start.6 = (f32[32,1024]{1,0:T(8,128)S(1)}, f32[32,1024]{1,0:T(8,128)}, u32[]{:S(2)}) copy-start(f32[32,1024]{1,0:T(8,128)} %reduce-scatter.2.cloned.1.call-done) | copy-start | bytes 393220
  218.6 3.1 %collective-permute-start.1 = (f32[16,1024]{1,0:T(8,128)S(1)}, f32[16,1024]{1,0:T(8,128)S(1)}, u32[]{:S(2)}, u32[]{:S(2)}) collective-permute-start(f32[16,1024]{1,0:T(8,128)S(1)} %constant_dynamic-slice_fusion), channel_id=1, source_target_pairs={{0,16},{16,0},{1,17},{17,1},{2,18},{18,2},{3,19},{19,3},{4,20},{20... | collective-permute-start | bytes 196616 | tf_op jit(solution)/shard_map/ppermute | solution.py:112
Sparse Core Ops, SparseCore 0:
  52.2 74.1 all-gather.1
Sparse Core Ops, SparseCore 1:
  122.0 93.9 reduce-scatter.1

commit v3 on v2

--- a/solution.py
+++ b/solution.py
@@ -53,7 +53,7 @@
     )
     arrived = exchange(outgoing.reshape(columns, block, -1), "y").reshape(tall, -1)
     arrived, share = lax.optimization_barrier((arrived, share))
-    other_weight = lax.all_gather(share, SHARE, axis=0, tiled=True)
+    beside = lax.ppermute(share, "zp", [(0, 1), (1, 0)])
     grad_flat, hid_flat = arrived[:, :out_width], arrived[:, out_width:]
 
     full = jnp.arange(columns * halves * capacity, dtype=I32)
@@ -81,6 +81,10 @@
         for c in range(cs)
     ]
     near_rows = exchange(jnp.stack(blocks), NEAR).reshape(near * rows, -1)
+    near_rows, share, beside = lax.optimization_barrier((near_rows, share, beside))
+    even = lax.axis_index("zp") == 0
+    pair = jnp.stack([jnp.where(even, share, beside), jnp.where(even, beside, share)])
+    other_weight = lax.all_gather(pair, NEAR, axis=1, tiled=True).reshape(hid_width, -1)
     hid_near, grad_near = near_rows[:, : hid_width // xs], near_rows[:, hid_width // xs :]
     of_half = (jnp.arange(near * rows, dtype=I32) // capacity % halves)[:, None]
     zero = jnp.zeros((), BF16)

time: 232 us -> 224 us (0.966)
  waiting for transfers between devices: 142 us -> 115 us
  starting transfers between devices: 40 us -> 55.2 us
    reduce_scatter x1, waiting for transfers between devices: 73.3 us -> 23.5 us  [shards(): lax.psum_scatter(partial_grad, RING, scatter_dimension=0, tiled=True)]
    all_gather x1, waiting for transfers between devices: 4.41 us -> 49.1 us  [shards(): lax.all_gather(pair, NEAR, axis=1, tiled=True).reshape(hid_width, -1)]
    all_to_all x3, waiting for transfers between devices: 58.1 us -> 29 us  [exchange(): return lax.all_to_all(blocks, axes, split_axis=0, concat_axis=0, tiled=True)]
    ppermute x0 -> x1, starting transfers between devices: none -> 15.2 us  [shards(): beside = lax.ppermute(share, 'zp', [(0, 1), (1, 0)])]
    ppermute x0 -> x1, waiting for transfers between devices: none -> 6.91 us  [shards(): beside = lax.ppermute(share, 'zp', [(0, 1), (1, 0)])]
  transfers between devices with their start and end apart: 7 -> 8, of which waited for: 6 -> 7; matrix products, arithmetic and copies ran while one was open for 10% -> 7% of each run, Pallas kernels for 0% -> 0%
where the time goes in v3:
time: 224 us; the launch traced here: 220 us
  waiting for transfers between devices  115 us (51%)
  starting transfers between devices  55.2 us (25%)
  matrix products  16.5 us (7%)
  between operations  15.7 us (7%)
  other arithmetic  14.5 us (6%)
  local copies, waits for them, and re-layouts  3.06 us (1%)
    all_gather x1, waiting for transfers between devices, shards(): lax.all_gather(pair, NEAR, axis=1, tiled=True).reshape(hid_width, -1)  49.1 us
    all_to_all x3, waiting for transfers between devices, exchange(): return lax.all_to_all(blocks, axes, split_axis=0, concat_axis=0, tiled=True)  29 us
    reduce_scatter x1, waiting for transfers between devices, shards(): lax.psum_scatter(partial_grad, RING, scatter_dimension=0, tiled=True)  23.5 us
    ppermute x1, starting transfers between devices, shards(): share = lax.ppermute(share, 'zh', [(0, 1), (1, 0)])  19.4 us
    all_to_all x3, starting transfers between devices, exchange(): return lax.all_to_all(blocks, axes, split_axis=0, concat_axis=0, tiled=True)  18.6 us
    dot_general x11, matrix products, dot(): lax.dot_general(a, b, (dims, ((), ())), preferred_element_type=F32)  16.5 us
    ppermute x1, starting transfers between devices, shards(): beside = lax.ppermute(share, 'zp', [(0, 1), (1, 0)])  15.2 us
    ppermute x1, waiting for transfers between devices, shards(): beside = lax.ppermute(share, 'zp', [(0, 1), (1, 0)])  6.91 us
  transfers between devices with their start and end apart: 8, of which 7 were waited for; matrix products, arithmetic and copies ran while one was open for 7% of the time, Pallas kernels for 0%

profile of v3, /device:TPU:6, one launch (start us, length us, event | category | flops | bytes accessed | tf_op | source)
XLA Modules:
  0.0 219.8 jit_solution(17502256986133601021)
XLA Ops:
  8.0 0.0 copy-start
  8.0 0.8 fusion.57
  8.8 0.2 reduce_window_sum.11
  9.0 0.8 select_reduce_fusion
  9.8 0.7 multiply_add_fusion
  10.5 0.0 copy-done
  10.5 0.3 convolution_convert_fusion.4
  10.7 1.5 convolution_convert_fusion.1
  12.2 1.1 pad_maximum_fusion
  13.4 7.1 %all-to-all-start = ((bf16[8,24,3072]{2,1,0:T(8,128)(2,1)}), bf16[8,24,3072]{2,1,0:T(8,128)(2,1)S(1)}, u32[]{:S(2)}, u32[]{:S(2)}) async-start(bf16[8,24,3072]{2,1,0:T(8,128)(2,1)} %bitcast.2), calls=%async_computation | async-start | bytes 2359296 | tf_op jit(solution)/shard_map/all_to_all | solution.py:16
  20.5 1.0 dynamic-slice_bitcast_fusion
  21.4 19.4 %collective-permute-start = (bf16[64,2048]{1,0:T(8,128)(2,1)S(1)}, bf16[64,2048]{1,0:T(8,128)(2,1)}, u32[]{:S(2)}, u32[]{:S(2)}) collective-permute-start(bf16[64,2048]{1,0:T(8,128)(2,1)S(1)} %dynamic-slice_bitcast_fusion), channel_id=1, source_target_pairs={{0,1},{1,0},{2,3},{3,2},{4,5},{5,4},{6,7},{7,6},{8,9},{9,8},{10,11... | collective-permute-start | bytes 786440 | tf_op jit(solution)/shard_map/ppermute | solution.py:43
  40.9 6.4 %collective-permute-done = bf16[64,2048]{1,0:T(8,128)(2,1)} collective-permute-done((bf16[64,2048]{1,0:T(8,128)(2,1)S(1)}, bf16[64,2048]{1,0:T(8,128)(2,1)}, u32[]{:S(2)}, u32[]{:S(2)}) %collective-permute-start) | collective-permute-done | bytes 262176 | tf_op jit(solution)/shard_map/ppermute | solution.py:43
  47.2 4.8 %all-to-all-done = bf16[8,24,3072]{2,1,0:T(8,128)(2,1)S(1)} async-done(((bf16[8,24,3072]{2,1,0:T(8,128)(2,1)}), bf16[8,24,3072]{2,1,0:T(8,128)(2,1)S(1)}, u32[]{:S(2)}, u32[]{:S(2)}) %all-to-all-start) | async-done | bytes 1179680 | tf_op jit(solution)/shard_map/all_to_all | solution.py:16
  52.1 0.0 copy-start.1
  52.1 0.4 convolution_convert_fusion.2
  52.5 1.2 fusion.20
  53.7 0.0 copy-done.1
  53.7 0.8 fusion.46
  54.5 0.8 fusion.48
  55.3 0.8 fusion.42
  56.1 0.8 fusion.44
  56.9 0.8 fusion.38
  57.7 0.8 fusion.40
  58.4 0.8 fusion.34
  59.2 0.8 fusion.36
  60.0 4.8 %all-to-all-start.1 = ((bf16[8,160,1280]{2,1,0:T(8,128)(2,1)}), bf16[8,160,1280]{2,1,0:T(8,128)(2,1)S(1)}, u32[]{:S(2)}, u32[]{:S(2)}) async-start(bf16[8,160,1280]{2,1,0:T(8,128)(2,1)} %fusion.36), calls=%async_computation.1 | async-start | bytes 6553600 | tf_op jit(solution)/shard_map/all_to_all | solution.py:16
  64.8 0.0 all-gather.2.cloned.1.call-start
  64.8 15.2 %collective-permute-start.1 = (bf16[64,2048]{1,0:T(8,128)(2,1)}, bf16[64,2048]{1,0:T(8,128)(2,1)}, u32[]{:S(2)}, u32[]{:S(2)}) collective-permute-start(bf16[64,2048]{1,0:T(8,128)(2,1)} %collective-permute-done), channel_id=1, source_target_pairs={{0,128},{128,0},{1,129},{129,1},{2,130},{130,2},{3,131},{131,3},{4... | collective-permute-start | bytes 786440 | tf_op jit(solution)/shard_map/ppermute | solution.py:56
  80.1 6.9 %collective-permute-done.1 = bf16[64,2048]{1,0:T(8,128)(2,1)} collective-permute-done((bf16[64,2048]{1,0:T(8,128)(2,1)}, bf16[64,2048]{1,0:T(8,128)(2,1)}, u32[]{:S(2)}, u32[]{:S(2)}) %collective-permute-start.1) | collective-permute-done | bytes 262176 | tf_op jit(solution)/shard_map/ppermute | solution.py:56
  87.0 15.6 %all-to-all-done.1 = bf16[8,160,1280]{2,1,0:T(8,128)(2,1)S(1)} async-done(((bf16[8,160,1280]{2,1,0:T(8,128)(2,1)}), bf16[8,160,1280]{2,1,0:T(8,128)(2,1)S(1)}, u32[]{:S(2)}, u32[]{:S(2)}) %all-to-all-start.1) | async-done | bytes 3276832 | tf_op jit(solution)/shard_map/all_to_all | solution.py:16
  102.6 1.1 select_bitcast_fusion.1
  103.6 0.8 pad_maximum_fusion.10
  104.5 0.0 all-gather.2.cloned.1.call-update
  104.5 0.0 reduce-scatter.2.cloned.1.call-start
  104.6 0.9 broadcast_select_fusion.1
  105.5 2.9 %fusion.5 = f32[512,1024]{1,0:T(8,128)} fusion(bf16[1280,1280]{1,0:T(8,128)(2,1)S(1)} %bitcast.67, bf16[1280,256]{1,0:T(8,128)(2,1)S(1)} %get-tuple-element.19, bf16[1280,256]{1,0:T(8,128)(2,1)S(1)} %get-tuple-element.18), kind=kOutput, calls=%fused_computation.6 | convolution fusion | flops 1344798720 | bytes 6029312 | tf_op jit(solution)/shard_map/dot_general | solution.py:20
  108.4 0.0 reduce-scatter.2.cloned.1.call-update
  108.4 49.1 %all-gather.2.cloned.1.call-done = bf16[2,512,2048]{2,1,0:T(8,128)(2,1)} async-done(((bf16[2,64,2048]{2,1,0:T(8,128)(2,1)}), bf16[2,512,2048]{2,1,0:T(8,128)(2,1)}) %all-gather.2.cloned.1.call-update) | async-done | bytes 4194320 | tf_op jit(solution)/shard_map/all_gather | solution.py:87
  157.5 0.0 copy-start.2
  157.5 0.0 copy-start.3
  157.5 3.5 %convolution_convert_fusion = bf16[192,2048]{1,0:T(8,128)(2,1)S(1)} fusion(bf16[1024,2048]{1,0:T(8,128)(2,1)} %bitcast.74, bf16[192,3072]{1,0:T(8,128)(2,1)} %bitcast.70), kind=kOutput, calls=%fused_computation.9 | convolution fusion | flops 805699584 | bytes 5373952 | tf_op jit(solution)/shard_map/dot_general | solution.py:20
  161.0 0.0 copy-done.2
  161.0 0.5 copy-done.3
  161.4 0.0 copy-start.6
  161.4 1.5 convolution_convert_fusion.3
  163.0 0.7 copy-done.6
  163.7 1.0 fusion.10
  164.7 1.5 fusion.21
  166.2 0.0 copy-start.4
  166.2 0.0 copy-start.7
  166.2 1.1 pad_maximum_fusion.1
  167.4 6.7 %all-to-all-start.2 = ((bf16[8,24,3072]{2,1,0:T(8,128)(2,1)}), bf16[8,24,3072]{2,1,0:T(8,128)(2,1)S(1)}, u32[]{:S(2)}, u32[]{:S(2)}) async-start(bf16[8,24,3072]{2,1,0:T(8,128)(2,1)} %bitcast.18), calls=%async_computation.2 | async-start | bytes 2359296 | tf_op jit(solution)/shard_map/all_to_all | solution.py:16
  174.1 23.5 %reduce-scatter.2.cloned.1.call-done = f32[32,1024]{1,0:T(8,128)} async-done(((f32[512,1024]{1,0:T(8,128)}), f32[32,1024]{1,0:T(8,128)}) %reduce-scatter.2.cloned.1.call-update) | async-done | bytes 131088 | tf_op jit(solution)/shard_map/reduce_scatter | solution.py:95
  197.6 8.5 %all-to-all-done.2 = bf16[8,24,3072]{2,1,0:T(8,128)(2,1)S(1)} async-done(((bf16[8,24,3072]{2,1,0:T(8,128)(2,1)}), bf16[8,24,3072]{2,1,0:T(8,128)(2,1)S(1)}, u32[]{:S(2)}, u32[]{:S(2)}) %all-to-all-start.2) | async-done | bytes 1179680 | tf_op jit(solution)/shard_map/all_to_all | solution.py:16
  206.2 0.8 constant_dynamic-slice_fusion
  207.0 1.9 collective-permute-start.2
  208.9 0.0 copy-done.4
  208.9 0.0 copy-done.7
  208.9 1.8 fusion.25
  210.7 1.0 convolution_convert_fusion.6
  211.7 0.0 collective-permute-done.2
  211.7 0.0 copy-done.5
  211.7 0.7 maximum_bitcast_fusion
  (8 shorter events, 0.1 us)
Async XLA Ops:
  8.0 2.5 %copy-start = (bf16[128,1024]{1,0:T(8,128)(2,1)S(1)}, bf16[128,1024]{1,0:T(8,128)(2,1)}, u32[]{:S(2)}) copy-start(bf16[128,1024]{1,0:T(8,128)(2,1)} %param.5) | copy-start | bytes 786436
  13.4 38.7 %all-to-all-start = ((bf16[8,24,3072]{2,1,0:T(8,128)(2,1)}), bf16[8,24,3072]{2,1,0:T(8,128)(2,1)S(1)}, u32[]{:S(2)}, u32[]{:S(2)}) async-start(bf16[8,24,3072]{2,1,0:T(8,128)(2,1)} %bitcast.2), calls=%async_computation | async-start | bytes 2359296 | tf_op jit(solution)/shard_map/all_to_all | solution.py:16
  21.4 25.8 %collective-permute-start = (bf16[64,2048]{1,0:T(8,128)(2,1)S(1)}, bf16[64,2048]{1,0:T(8,128)(2,1)}, u32[]{:S(2)}, u32[]{:S(2)}) collective-permute-start(bf16[64,2048]{1,0:T(8,128)(2,1)S(1)} %dynamic-slice_bitcast_fusion), channel_id=1, source_target_pairs={{0,1},{1,0},{2,3},{3,2},{4,5},{5,4},{6,7},{7,6},{8,9},{9,8},{10,11... | collective-permute-start | bytes 786440 | tf_op jit(solution)/shard_map/ppermute | solution.py:43
  52.1 1.6 copy-start.1
  60.0 42.6 %all-to-all-start.1 = ((bf16[8,160,1280]{2,1,0:T(8,128)(2,1)}), bf16[8,160,1280]{2,1,0:T(8,128)(2,1)S(1)}, u32[]{:S(2)}, u32[]{:S(2)}) async-start(bf16[8,160,1280]{2,1,0:T(8,128)(2,1)} %fusion.36), calls=%async_computation.1 | async-start | bytes 6553600 | tf_op jit(solution)/shard_map/all_to_all | solution.py:16
  64.8 92.7 %all-gather.2.cloned.1.call-start = ((), (), s32[]{:S(2)}) async-start(), calls=%async_computation.4 | async-start | bytes 4718592 | tf_op jit(solution)/shard_map/all_gather | solution.py:87
  64.8 22.2 %collective-permute-start.1 = (bf16[64,2048]{1,0:T(8,128)(2,1)}, bf16[64,2048]{1,0:T(8,128)(2,1)}, u32[]{:S(2)}, u32[]{:S(2)}) collective-permute-start(bf16[64,2048]{1,0:T(8,128)(2,1)} %collective-permute-done), channel_id=1, source_target_pairs={{0,128},{128,0},{1,129},{129,1},{2,130},{130,2},{3,131},{131,3},{4... | collective-permute-start | bytes 786440 | tf_op jit(solution)/shard_map/ppermute | solution.py:56
  104.5 93.1 %reduce-scatter.2.cloned.1.call-start = ((), (), s32[]{:S(2)}) async-start(), calls=%async_computation.5 | async-start | bytes 2228224 | tf_op jit(solution)/shard_map/reduce_scatter | solution.py:95
  157.5 3.5 %copy-start.2 = (bf16[8,24,3072]{2,1,0:T(8,128)(2,1)S(1)}, bf16[8,24,3072]{2,1,0:T(8,128)(2,1)}, u32[]{:S(2)}) copy-start(bf16[8,24,3072]{2,1,0:T(8,128)(2,1)} %copy-done.1) | copy-start | bytes 3538948
  157.5 4.0 %copy-start.3 = (bf16[2,512,2048]{2,1,0:T(8,128)(2,1)S(1)}, bf16[2,512,2048]{2,1,0:T(8,128)(2,1)}, u32[]{:S(2)}) copy-start(bf16[2,512,2048]{2,1,0:T(8,128)(2,1)} %all-gather.2.cloned.1.call-done) | copy-start | bytes 12582916
  161.4 2.2 %copy-start.6 = (bf16[1,1024,2048]{2,1,0:T(8,128)(2,1)S(1)}, bf16[1,1024,2048]{2,1,0:T(8,128)(2,1)}, u32[]{:S(2)}) copy-start(bf16[1,1024,2048]{2,1,0:T(8,128)(2,1)} %param.8) | copy-start | bytes 12582916
  166.2 42.7 %copy-start.4 = (bf16[128,2048]{1,0:T(8,128)(2,1)S(1)}, bf16[128,2048]{1,0:T(8,128)(2,1)}, u32[]{:S(2)}) copy-start(bf16[128,2048]{1,0:T(8,128)(2,1)} %param.9) | copy-start | bytes 1572868
  166.2 42.7 %copy-start.7 = (f32[128,1]{0,1:T(1,128)S(1)}, f32[128,1]{0,1:T(1,128)}, u32[]{:S(2)}) copy-start(f32[128,1]{0,1:T(1,128)} %param.7) | copy-start | bytes 1540
  167.4 38.8 %all-to-all-start.2 = ((bf16[8,24,3072]{2,1,0:T(8,128)(2,1)}), bf16[8,24,3072]{2,1,0:T(8,128)(2,1)S(1)}, u32[]{:S(2)}, u32[]{:S(2)}) async-start(bf16[8,24,3072]{2,1,0:T(8,128)(2,1)} %bitcast.18), calls=%async_computation.2 | async-start | bytes 2359296 | tf_op jit(solution)/shard_map/all_to_all | solution.py:16
  197.6 14.1 %copy-start.5 = (f32[32,1024]{1,0:T(8,128)S(1)}, f32[32,1024]{1,0:T(8,128)}, u32[]{:S(2)}) copy-start(f32[32,1024]{1,0:T(8,128)} %reduce-scatter.2.cloned.1.call-done) | copy-start | bytes 393220
  207.0 4.7 %collective-permute-start.2 = (f32[16,1024]{1,0:T(8,128)S(1)}, f32[16,1024]{1,0:T(8,128)S(1)}, u32[]{:S(2)}, u32[]{:S(2)}) collective-permute-start(f32[16,1024]{1,0:T(8,128)S(1)} %constant_dynamic-slice_fusion), channel_id=1, source_target_pairs={{0,16},{16,0},{1,17},{17,1},{2,18},{18,2},{3,19},{19,3},{4,20},{20... | collective-permute-start | bytes 196616 | tf_op jit(solution)/shard_map/ppermute | solution.py:116
Sparse Core Ops, SparseCore 0:
  104.6 52.8 all-gather.1
Sparse Core Ops, SparseCore 1:
  108.5 89.1 reduce-scatter.1

commit v4 on v2

--- a/solution.py
+++ b/solution.py
@@ -8,8 +8,8 @@
 DP = LINE + ("x", "c")
 EXP = ("y", "zh")
 NEAR = ("x", "c")
-SHARE = ("zp", "x", "c")
-RING = ("zh",) + LINE
+SHARE = LINE + ("c",)
+RING = ("zh",) + LINE + ("c",)
 
 
 def exchange(blocks, axes):
@@ -81,39 +81,52 @@
         for c in range(cs)
     ]
     near_rows = exchange(jnp.stack(blocks), NEAR).reshape(near * rows, -1)
+    near_rows, other_weight = lax.optimization_barrier((near_rows, other_weight))
     hid_near, grad_near = near_rows[:, : hid_width // xs], near_rows[:, hid_width // xs :]
     of_half = (jnp.arange(near * rows, dtype=I32) // capacity % halves)[:, None]
     zero = jnp.zeros((), BF16)
     by_half = jnp.concatenate(
         [jnp.where(of_half == h, hid_near, zero) for h in range(halves)], axis=1
     )
-    partial_grad = dot(by_half, grad_near, ((0,), (0,)), F32)
-    ring_sum = lax.psum_scatter(partial_grad, RING, scatter_dimension=0, tiled=True)
+    partial_grad = dot(by_half, grad_near, ((0,), (0,)))
+    arrived, partial_grad = lax.optimization_barrier((arrived, partial_grad))
+    parts = exchange(partial_grad.reshape(-1, strip, out_width // cs), RING)
 
+    here = lax.axis_index("y")
+    turned = lax.dynamic_slice_in_dim(
+        jnp.concatenate([arrived, arrived], axis=0), here * block, tall, axis=0
+    )
+    grad_turned, hid_turned = turned[:, :out_width], turned[:, out_width:]
     own = (jnp.arange(tall, dtype=I32) // slots % halves)[:, None] == half
     proj = jnp.where(
-        own, dot(hid_flat, weight, ((1,), (0,))), dot(hid_flat, other_weight, ((1,), (0,)))
+        own, dot(hid_turned, weight, ((1,), (0,))), dot(hid_turned, other_weight, ((1,), (0,)))
     )
     back = jnp.where(
-        own, dot(grad_flat, weight, ((1,), (1,))), dot(grad_flat, other_weight, ((1,), (1,)))
+        own, dot(grad_turned, weight, ((1,), (1,))), dot(grad_turned, other_weight, ((1,), (1,)))
     )
-    returned = exchange(
-        jnp.concatenate([proj, back], axis=1).reshape(columns, block, -1), "y"
-    ).reshape(tall, -1)
-    returned, ring_sum = lax.optimization_barrier((returned, ring_sum))
-    projected = dot(placer, returned[:, :out_width], ((0,), (0,)), F32)
+    leaving = jnp.concatenate([proj, back], axis=1)
+    returned = jnp.concatenate(
+        [leaving[:block]]
+        + [
+            lax.ppermute(
+                leaving[k * block : (k + 1) * block],
+                "y",
+                [(y, (y + k) % columns) for y in range(columns)],
+            )
+            for k in range(1, columns)
+        ],
+        axis=0,
+    )
+    turns = jnp.mod(here - expert_list // halves, columns)
+    fetch_index = turns * block + expert_list % halves * slots + row_rank
+    fetcher = (jnp.arange(tall, dtype=I32)[:, None] == fetch_index[None, :]).astype(BF16)
+    projected = dot(fetcher, returned[:, :out_width], ((0,), (0,)), F32)
     layer_out = (gate_weights * projected).astype(BF16)
     gate_grad = jnp.sum(out_grad.astype(F32) * projected, axis=1, keepdims=True)
-    hidden_grad = dot(placer, returned[:, out_width:], ((0,), (0,)))
+    hidden_grad = dot(fetcher, returned[:, out_width:], ((0,), (0,)))
 
-    core = lax.axis_index("c")
-    kept = lax.dynamic_slice_in_dim(ring_sum, core * strip, strip, axis=0)
-    given = lax.dynamic_slice_in_dim(ring_sum, (1 - core) * strip, strip, axis=0)
-    taken = lax.ppermute(given, "c", [(0, 1), (1, 0)])
-    first = core == 0
-    weight_grad = jnp.concatenate(
-        [jnp.where(first, kept, taken), jnp.where(first, taken, kept)], axis=1
-    )
+    summed = jnp.sum(parts.reshape(-1, cs, strip, out_width // cs).astype(F32), axis=0)
+    weight_grad = summed.swapaxes(0, 1).reshape(strip, out_width)
     return (layer_out, hidden_grad, gate_grad, weight_grad[None])
 
 

time: 232 us -> 258 us (1.11)
  starting transfers between devices: 40 us -> 70.6 us
  waiting for transfers between devices: 142 us -> 138 us
    reduce_scatter x1 -> x0, waiting for transfers between devices: 73.3 us -> none  [shards(): lax.psum_scatter(partial_grad, RING, scatter_dimension=0, tiled=True)]
    all_gather x1, waiting for transfers between devices: 4.41 us -> 72.8 us  [shards(): other_weight = lax.all_gather(share, SHARE, axis=0, tiled=True)]
    ppermute x1 -> x7, starting transfers between devices: 1.91 us -> 30.1 us  [shards(): lax.ppermute(leaving[k * block:(k + 1) * block], 'y', [(y, (y + k) % colu...]
    ppermute x1 -> x7, waiting for transfers between devices: 0.24 us -> 13.3 us  [shards(): lax.ppermute(leaving[k * block:(k + 1) * block], 'y', [(y, (y + k) % colu...]
    all_to_all x3, waiting for transfers between devices: 58.1 us -> 45.1 us  [exchange(): return lax.all_to_all(blocks, axes, split_axis=0, concat_axis=0, tiled=True)]
  transfers between devices with their start and end apart: 7 -> 12, of which waited for: 6 -> 9; matrix products, arithmetic and copies ran while one was open for 10% -> 7% of each run, Pallas kernels for 0% -> 0%
where the time goes in v4:
time: 258 us; the launch traced here: 256 us
  waiting for transfers between devices  138 us (53%)
  starting transfers between devices  70.6 us (27%)
  matrix products  18 us (7%)
  between operations  14.4 us (6%)
  other arithmetic  13 us (5%)
  local copies, waits for them, and re-layouts  2.76 us (1%)
    all_gather x1, waiting for transfers between devices, shards(): other_weight = lax.all_gather(share, SHARE, axis=0, tiled=True)  72.8 us
    all_to_all x3, waiting for transfers between devices, exchange(): return lax.all_to_all(blocks, axes, split_axis=0, concat_axis=0, tiled=True)  45.1 us
    ppermute x7, starting transfers between devices, shards(): lax.ppermute(leaving[k * block:(k + 1) * block], 'y', [(y, (y + k) % colu...  30.1 us
    all_to_all x3, starting transfers between devices, exchange(): return lax.all_to_all(blocks, axes, split_axis=0, concat_axis=0, tiled=True)  21.1 us
    ppermute x1, starting transfers between devices, shards(): share = lax.ppermute(share, 'zh', [(0, 1), (1, 0)])  19.4 us
    dot_general x11, matrix products, dot(): lax.dot_general(a, b, (dims, ((), ())), preferred_element_type=F32)  18 us
    ppermute x7, waiting for transfers between devices, shards(): lax.ppermute(leaving[k * block:(k + 1) * block], 'y', [(y, (y + k) % colu...  13.3 us
    ppermute x1, waiting for transfers between devices, shards(): share = lax.ppermute(share, 'zh', [(0, 1), (1, 0)])  6.3 us
  transfers between devices with their start and end apart: 12, of which 9 were waited for; matrix products, arithmetic and copies ran while one was open for 7% of the time, Pallas kernels for 0%

profile of v4, /device:TPU:6, one launch (start us, length us, event | category | flops | bytes accessed | tf_op | source)
XLA Modules:
  0.0 256.3 jit_solution(17097515025482605845)
XLA Ops:
  7.2 0.0 copy-start
  7.2 0.8 fusion.65
  8.0 0.2 reduce_window_sum.11
  8.1 0.8 select_reduce_fusion
  9.0 0.7 fusion.100
  9.7 0.0 copy-done
  9.7 0.3 convolution_convert_fusion.4
  9.9 1.5 convolution_convert_fusion.1
  11.4 1.1 pad_maximum_fusion
  12.6 7.1 %all-to-all-start = ((bf16[8,24,3072]{2,1,0:T(8,128)(2,1)}), bf16[8,24,3072]{2,1,0:T(8,128)(2,1)S(1)}, u32[]{:S(2)}, u32[]{:S(2)}) async-start(bf16[8,24,3072]{2,1,0:T(8,128)(2,1)} %bitcast.2), calls=%async_computation | async-start | bytes 2359296 | tf_op jit(solution)/shard_map/all_to_all | solution.py:16
  19.7 0.0 all-gather.2.cloned.1.call-start
  19.7 1.0 dynamic-slice_bitcast_fusion
  20.7 19.4 %collective-permute-start = (bf16[64,2048]{1,0:T(8,128)(2,1)S(1)}, bf16[64,2048]{1,0:T(8,128)(2,1)S(1)}, u32[]{:S(2)}, u32[]{:S(2)}) collective-permute-start(bf16[64,2048]{1,0:T(8,128)(2,1)S(1)} %dynamic-slice_bitcast_fusion), channel_id=1, source_target_pairs={{0,1},{1,0},{2,3},{3,2},{4,5},{5,4},{6,7},{7,6},{8,9},{9,8},{10,11... | collective-permute-start | bytes 786440 | tf_op jit(solution)/shard_map/ppermute | solution.py:43
  40.1 6.3 %collective-permute-done = bf16[64,2048]{1,0:T(8,128)(2,1)S(1)} collective-permute-done((bf16[64,2048]{1,0:T(8,128)(2,1)S(1)}, bf16[64,2048]{1,0:T(8,128)(2,1)S(1)}, u32[]{:S(2)}, u32[]{:S(2)}) %collective-permute-start) | collective-permute-done | bytes 262176 | tf_op jit(solution)/shard_map/ppermute | solution.py:43
  46.4 4.9 %all-to-all-done = bf16[8,24,3072]{2,1,0:T(8,128)(2,1)S(1)} async-done(((bf16[8,24,3072]{2,1,0:T(8,128)(2,1)}), bf16[8,24,3072]{2,1,0:T(8,128)(2,1)S(1)}, u32[]{:S(2)}, u32[]{:S(2)}) %all-to-all-start) | async-done | bytes 1179680 | tf_op jit(solution)/shard_map/all_to_all | solution.py:16
  51.3 0.0 all-gather.2.cloned.1.call-update
  51.3 1.2 fusion.21
  52.5 0.4 convolution_convert_fusion.2
  53.0 0.8 fusion.46
  53.8 0.8 fusion.48
  54.6 0.8 fusion.42
  55.4 0.8 fusion.44
  56.2 0.8 fusion.38
  57.0 0.8 fusion.40
  57.8 0.8 fusion.34
  58.6 0.8 fusion.36
  59.4 4.9 %all-to-all-start.1 = ((bf16[8,160,1280]{2,1,0:T(8,128)(2,1)}), bf16[8,160,1280]{2,1,0:T(8,128)(2,1)}, u32[]{:S(2)}, u32[]{:S(2)}) async-start(bf16[8,160,1280]{2,1,0:T(8,128)(2,1)} %fusion.36), calls=%async_computation.1 | async-start | bytes 6553600 | tf_op jit(solution)/shard_map/all_to_all | solution.py:16
  64.3 37.8 %all-to-all-done.1 = bf16[8,160,1280]{2,1,0:T(8,128)(2,1)} async-done(((bf16[8,160,1280]{2,1,0:T(8,128)(2,1)}), bf16[8,160,1280]{2,1,0:T(8,128)(2,1)}, u32[]{:S(2)}, u32[]{:S(2)}) %all-to-all-start.1) | async-done | bytes 3276832 | tf_op jit(solution)/shard_map/all_to_all | solution.py:16
  102.1 72.8 %all-gather.2.cloned.1.call-done = bf16[1024,2048]{1,0:T(8,128)(2,1)} async-done(((bf16[64,2048]{1,0:T(8,128)(2,1)}), bf16[1024,2048]{1,0:T(8,128)(2,1)}) %all-gather.2.cloned.1.call-update) | async-done | bytes 4194320 | tf_op jit(solution)/shard_map/all_gather | solution.py:56
  174.9 1.8 broadcast_select_fusion.1
  176.8 0.0 copy-start.1
  176.8 4.5 %fusion.12 = bf16[512,1024]{1,0:T(8,128)(2,1)} fusion(bf16[1280,1280]{1,0:T(8,128)(2,1)} %bitcast.13, bf16[1280,256]{1,0:T(8,128)(2,1)S(1)} %get-tuple-element.17, bf16[1280,256]{1,0:T(8,128)(2,1)S(1)} %get-tuple-element.16), kind=kOutput, calls=%fused_computation.31 | convolution fusion | flops 1345323008 | bytes 4980736 | tf_op jit(solution)/shard_map/dot_general | solution.py:20
  181.3 0.8 fusion.22
  182.2 1.0 fusion.7
  183.2 9.2 %all-to-all-start.2 = ((bf16[32,16,1024]{2,1,0:T(8,128)(2,1)}), bf16[32,16,1024]{2,1,0:T(8,128)(2,1)S(1)}, u32[]{:S(2)}, u32[]{:S(2)}) async-start(bf16[32,16,1024]{2,1,0:T(8,128)(2,1)} %bitcast.62), calls=%async_computation.2 | async-start | bytes 2097152 | tf_op jit(solution)/shard_map/all_to_all | solution.py:16
  192.4 0.0 copy-start.2
  192.4 3.4 %fusion.10 = bf16[192,2048]{1,0:T(8,128)(2,1)S(1)} fusion(bf16[192,2048]{1,0:T(8,128)(2,1)S(1)} %fusion.7, bf16[1024,2048]{1,0:T(8,128)(2,1)} %all-gather.2.cloned.1.call-done, pred[192]{0:T(512)(128)(4,1)S(1)} %fusion.97, bf16[192,3072]{1,0:T(8,128)(2,1)S(1)} %fusion.22), kind=kOutput, calls=%fused_computation.21 | convolution fusion | flops 806092800 | bytes 6160896 | tf_op jit(solution)/shard_map/dot_general | solution.py:20
  195.7 0.1 copy-done.2
  195.8 1.5 fusion.18
  197.3 0.6 copy-done.6
  198.0 1.5 fusion.23
  199.5 0.1 pad_maximum_fusion.9
  199.6 3.5 %collective-permute-start.1 = (bf16[24,3072]{1,0:T(8,128)(2,1)S(1)}, bf16[24,3072]{1,0:T(8,128)(2,1)S(1)}, u32[]{:S(2)}, u32[]{:S(2)}) collective-permute-start(bf16[24,3072]{1,0:T(8,128)(2,1)S(1)} %get-tuple-element.20), channel_id=1, source_target_pairs={{0,2},{2,4},{4,6},{6,8},{8,10},{10,12},{12,14},{14,0},{1,3},{3,5},... | collective-permute-start | bytes 442376 | tf_op jit(solution)/shard_map/ppermute | solution.py:111
  203.1 4.4 %collective-permute-start.2 = (bf16[24,3072]{1,0:T(8,128)(2,1)S(1)}, bf16[24,3072]{1,0:T(8,128)(2,1)S(1)}, u32[]{:S(2)}, u32[]{:S(2)}) collective-permute-start(bf16[24,3072]{1,0:T(8,128)(2,1)S(1)} %get-tuple-element.21), channel_id=1, source_target_pairs={{0,4},{2,6},{4,8},{6,10},{8,12},{10,14},{12,0},{14,2},{1,5},{3,7},... | collective-permute-start | bytes 442376 | tf_op jit(solution)/shard_map/ppermute | solution.py:111
  207.5 4.5 %collective-permute-start.3 = (bf16[24,3072]{1,0:T(8,128)(2,1)S(1)}, bf16[24,3072]{1,0:T(8,128)(2,1)S(1)}, u32[]{:S(2)}, u32[]{:S(2)}) collective-permute-start(bf16[24,3072]{1,0:T(8,128)(2,1)S(1)} %get-tuple-element.22), channel_id=1, source_target_pairs={{0,6},{2,8},{4,10},{6,12},{8,14},{10,0},{12,2},{14,4},{1,7},{3,9},... | collective-permute-start | bytes 442376 | tf_op jit(solution)/shard_map/ppermute | solution.py:111
  212.1 4.2 %collective-permute-start.4 = (bf16[24,3072]{1,0:T(8,128)(2,1)S(1)}, bf16[24,3072]{1,0:T(8,128)(2,1)S(1)}, u32[]{:S(2)}, u32[]{:S(2)}) collective-permute-start(bf16[24,3072]{1,0:T(8,128)(2,1)S(1)} %get-tuple-element.23), channel_id=1, source_target_pairs={{0,8},{2,10},{4,12},{6,14},{8,0},{10,2},{12,4},{14,6},{1,9},{3,11}... | collective-permute-start | bytes 442376 | tf_op jit(solution)/shard_map/ppermute | solution.py:111
  216.3 4.8 %collective-permute-start.5 = (bf16[24,3072]{1,0:T(8,128)(2,1)S(1)}, bf16[24,3072]{1,0:T(8,128)(2,1)S(1)}, u32[]{:S(2)}, u32[]{:S(2)}) collective-permute-start(bf16[24,3072]{1,0:T(8,128)(2,1)S(1)} %get-tuple-element.24), channel_id=1, source_target_pairs={{0,10},{2,12},{4,14},{6,0},{8,2},{10,4},{12,6},{14,8},{1,11},{3,13... | collective-permute-start | bytes 442376 | tf_op jit(solution)/shard_map/ppermute | solution.py:111
  221.1 0.0 collective-permute-done.1
  221.1 5.4 %collective-permute-start.6 = (bf16[24,3072]{1,0:T(8,128)(2,1)S(1)}, bf16[24,3072]{1,0:T(8,128)(2,1)S(1)}, u32[]{:S(2)}, u32[]{:S(2)}) collective-permute-start(bf16[24,3072]{1,0:T(8,128)(2,1)S(1)} %get-tuple-element.25), channel_id=1, source_target_pairs={{0,12},{2,14},{4,0},{6,2},{8,4},{10,6},{12,8},{14,10},{1,13},{3,15... | collective-permute-start | bytes 442376 | tf_op jit(solution)/shard_map/ppermute | solution.py:111
  226.5 0.0 copy-start.3
  226.5 0.0 copy-start.5
  226.6 0.0 collective-permute-done.2
  226.6 3.2 %collective-permute-start.7 = (bf16[24,3072]{1,0:T(8,128)(2,1)S(1)}, bf16[24,3072]{1,0:T(8,128)(2,1)S(1)}, u32[]{:S(2)}, u32[]{:S(2)}) collective-permute-start(bf16[24,3072]{1,0:T(8,128)(2,1)S(1)} %get-tuple-element.18), channel_id=1, source_target_pairs={{0,14},{2,0},{4,2},{6,4},{8,6},{10,8},{12,10},{14,12},{1,15},{3,1}... | collective-permute-start | bytes 442376 | tf_op jit(solution)/shard_map/ppermute | solution.py:111
  229.8 0.0 collective-permute-done.3
  229.8 0.7 collective-permute-done.4
  230.5 6.5 %collective-permute-done.5 = bf16[24,3072]{1,0:T(8,128)(2,1)S(1)} collective-permute-done((bf16[24,3072]{1,0:T(8,128)(2,1)S(1)}, bf16[24,3072]{1,0:T(8,128)(2,1)S(1)}, u32[]{:S(2)}, u32[]{:S(2)}) %collective-permute-start.5) | collective-permute-done | bytes 147488 | tf_op jit(solution)/shard_map/ppermute | solution.py:111
  237.0 4.9 %collective-permute-done.6 = bf16[24,3072]{1,0:T(8,128)(2,1)S(1)} collective-permute-done((bf16[24,3072]{1,0:T(8,128)(2,1)S(1)}, bf16[24,3072]{1,0:T(8,128)(2,1)S(1)}, u32[]{:S(2)}, u32[]{:S(2)}) %collective-permute-start.6) | collective-permute-done | bytes 147488 | tf_op jit(solution)/shard_map/ppermute | solution.py:111
  241.9 1.3 collective-permute-done.7
  243.2 1.0 convolution_convert_fusion.6
  244.2 1.8 fusion.25
  246.0 2.4 all-to-all-done.2
  248.3 0.2 convert_reduce_fusion
  248.5 0.1 copy.9
  248.6 0.8 broadcast_in_dim_reshape.3
  (19 shorter events, 0.2 us)
Async XLA Ops:
  7.2 2.5 copy-start
  12.6 38.7 %all-to-all-start = ((bf16[8,24,3072]{2,1,0:T(8,128)(2,1)}), bf16[8,24,3072]{2,1,0:T(8,128)(2,1)S(1)}, u32[]{:S(2)}, u32[]{:S(2)}) async-start(bf16[8,24,3072]{2,1,0:T(8,128)(2,1)} %bitcast.2), calls=%async_computation | async-start | bytes 2359296 | tf_op jit(solution)/shard_map/all_to_all | solution.py:16
  19.7 155.3 %all-gather.2.cloned.1.call-start = ((), (), s32[]{:S(2)}) async-start(), calls=%async_computation.3 | async-start | bytes 4456448 | tf_op jit(solution)/shard_map/all_gather | solution.py:56
  20.7 25.7 %collective-permute-start = (bf16[64,2048]{1,0:T(8,128)(2,1)S(1)}, bf16[64,2048]{1,0:T(8,128)(2,1)S(1)}, u32[]{:S(2)}, u32[]{:S(2)}) collective-permute-start(bf16[64,2048]{1,0:T(8,128)(2,1)S(1)} %dynamic-slice_bitcast_fusion), channel_id=1, source_target_pairs={{0,1},{1,0},{2,3},{3,2},{4,5},{5,4},{6,7},{7,6},{8,9},{9,8},{10,11... | collective-permute-start | bytes 786440 | tf_op jit(solution)/shard_map/ppermute | solution.py:43
  46.4 4.9 %copy-start.4 = (bf16[64,2048]{1,0:T(8,128)(2,1)}, bf16[64,2048]{1,0:T(8,128)(2,1)S(1)}, u32[]{:S(2)}) copy-start(bf16[64,2048]{1,0:T(8,128)(2,1)S(1)} %collective-permute-done) | copy-start | bytes 786436
  59.4 42.7 %all-to-all-start.1 = ((bf16[8,160,1280]{2,1,0:T(8,128)(2,1)}), bf16[8,160,1280]{2,1,0:T(8,128)(2,1)}, u32[]{:S(2)}, u32[]{:S(2)}) async-start(bf16[8,160,1280]{2,1,0:T(8,128)(2,1)} %fusion.36), calls=%async_computation.1 | async-start | bytes 6553600 | tf_op jit(solution)/shard_map/all_to_all | solution.py:16
  176.8 5.4 %copy-start.1 = (bf16[1,1024,2048]{2,1,0:T(8,128)(2,1)S(1)}, bf16[1,1024,2048]{2,1,0:T(8,128)(2,1)}, u32[]{:S(2)}) copy-start(bf16[1,1024,2048]{2,1,0:T(8,128)(2,1)} %param.8) | copy-start | bytes 12582916
  183.2 65.2 %all-to-all-start.2 = ((bf16[32,16,1024]{2,1,0:T(8,128)(2,1)}), bf16[32,16,1024]{2,1,0:T(8,128)(2,1)S(1)}, u32[]{:S(2)}, u32[]{:S(2)}) async-start(bf16[32,16,1024]{2,1,0:T(8,128)(2,1)} %bitcast.62), calls=%async_computation.2 | async-start | bytes 2097152 | tf_op jit(solution)/shard_map/all_to_all | solution.py:16
  192.4 3.5 %copy-start.2 = (bf16[1,1024,2048]{2,1,0:T(8,128)(2,1)S(1)}, bf16[1,1024,2048]{2,1,0:T(8,128)(2,1)}, u32[]{:S(2)}) copy-start(bf16[1,1024,2048]{2,1,0:T(8,128)(2,1)} %param.8) | copy-start | bytes 12582916
  195.8 2.2 copy-start.6
  199.6 21.5 %collective-permute-start.1 = (bf16[24,3072]{1,0:T(8,128)(2,1)S(1)}, bf16[24,3072]{1,0:T(8,128)(2,1)S(1)}, u32[]{:S(2)}, u32[]{:S(2)}) collective-permute-start(bf16[24,3072]{1,0:T(8,128)(2,1)S(1)} %get-tuple-element.20), channel_id=1, source_target_pairs={{0,2},{2,4},{4,6},{6,8},{8,10},{10,12},{12,14},{14,0},{1,3},{3,5},... | collective-permute-start | bytes 442376 | tf_op jit(solution)/shard_map/ppermute | solution.py:111
  203.1 23.5 %collective-permute-start.2 = (bf16[24,3072]{1,0:T(8,128)(2,1)S(1)}, bf16[24,3072]{1,0:T(8,128)(2,1)S(1)}, u32[]{:S(2)}, u32[]{:S(2)}) collective-permute-start(bf16[24,3072]{1,0:T(8,128)(2,1)S(1)} %get-tuple-element.21), channel_id=1, source_target_pairs={{0,4},{2,6},{4,8},{6,10},{8,12},{10,14},{12,0},{14,2},{1,5},{3,7},... | collective-permute-start | bytes 442376 | tf_op jit(solution)/shard_map/ppermute | solution.py:111
  207.5 22.3 %collective-permute-start.3 = (bf16[24,3072]{1,0:T(8,128)(2,1)S(1)}, bf16[24,3072]{1,0:T(8,128)(2,1)S(1)}, u32[]{:S(2)}, u32[]{:S(2)}) collective-permute-start(bf16[24,3072]{1,0:T(8,128)(2,1)S(1)} %get-tuple-element.22), channel_id=1, source_target_pairs={{0,6},{2,8},{4,10},{6,12},{8,14},{10,0},{12,2},{14,4},{1,7},{3,9},... | collective-permute-start | bytes 442376 | tf_op jit(solution)/shard_map/ppermute | solution.py:111
  212.1 18.4 %collective-permute-start.4 = (bf16[24,3072]{1,0:T(8,128)(2,1)S(1)}, bf16[24,3072]{1,0:T(8,128)(2,1)S(1)}, u32[]{:S(2)}, u32[]{:S(2)}) collective-permute-start(bf16[24,3072]{1,0:T(8,128)(2,1)S(1)} %get-tuple-element.23), channel_id=1, source_target_pairs={{0,8},{2,10},{4,12},{6,14},{8,0},{10,2},{12,4},{14,6},{1,9},{3,11}... | collective-permute-start | bytes 442376 | tf_op jit(solution)/shard_map/ppermute | solution.py:111
  216.3 20.7 %collective-permute-start.5 = (bf16[24,3072]{1,0:T(8,128)(2,1)S(1)}, bf16[24,3072]{1,0:T(8,128)(2,1)S(1)}, u32[]{:S(2)}, u32[]{:S(2)}) collective-permute-start(bf16[24,3072]{1,0:T(8,128)(2,1)S(1)} %get-tuple-element.24), channel_id=1, source_target_pairs={{0,10},{2,12},{4,14},{6,0},{8,2},{10,4},{12,6},{14,8},{1,11},{3,13... | collective-permute-start | bytes 442376 | tf_op jit(solution)/shard_map/ppermute | solution.py:111
  221.1 20.8 %collective-permute-start.6 = (bf16[24,3072]{1,0:T(8,128)(2,1)S(1)}, bf16[24,3072]{1,0:T(8,128)(2,1)S(1)}, u32[]{:S(2)}, u32[]{:S(2)}) collective-permute-start(bf16[24,3072]{1,0:T(8,128)(2,1)S(1)} %get-tuple-element.25), channel_id=1, source_target_pairs={{0,12},{2,14},{4,0},{6,2},{8,4},{10,6},{12,8},{14,10},{1,13},{3,15... | collective-permute-start | bytes 442376 | tf_op jit(solution)/shard_map/ppermute | solution.py:111
  226.5 17.7 %copy-start.3 = (bf16[128,2048]{1,0:T(8,128)(2,1)S(1)}, bf16[128,2048]{1,0:T(8,128)(2,1)}, u32[]{:S(2)}) copy-start(bf16[128,2048]{1,0:T(8,128)(2,1)} %param.9) | copy-start | bytes 1572868
  226.5 17.7 %copy-start.5 = (f32[128,1]{0,1:T(1,128)S(1)}, f32[128,1]{0,1:T(1,128)}, u32[]{:S(2)}) copy-start(f32[128,1]{0,1:T(1,128)} %param.7) | copy-start | bytes 1540
  226.6 16.6 %collective-permute-start.7 = (bf16[24,3072]{1,0:T(8,128)(2,1)S(1)}, bf16[24,3072]{1,0:T(8,128)(2,1)S(1)}, u32[]{:S(2)}, u32[]{:S(2)}) collective-permute-start(bf16[24,3072]{1,0:T(8,128)(2,1)S(1)} %get-tuple-element.18), channel_id=1, source_target_pairs={{0,14},{2,0},{4,2},{6,4},{8,6},{10,8},{12,10},{14,12},{1,15},{3,1}... | collective-permute-start | bytes 442376 | tf_op jit(solution)/shard_map/ppermute | solution.py:111
Sparse Core Ops, SparseCore 0:
  51.4 123.4 all-gather.1

commit v5 on v4

--- a/solution.py
+++ b/solution.py
@@ -8,7 +8,7 @@
 DP = LINE + ("x", "c")
 EXP = ("y", "zh")
 NEAR = ("x", "c")
-SHARE = LINE + ("c",)
+SHARE = ("zp", "x")
 RING = ("zh",) + LINE + ("c",)
 
 
@@ -38,8 +38,10 @@
     half = lax.axis_index("zh")
     weight = down_weight[0]
 
-    part = hid_width // lax.axis_size(SHARE)
-    share = lax.dynamic_slice_in_dim(weight, lax.axis_index(SHARE) * part, part, axis=0)
+    core = lax.axis_index("c")
+    part = hid_width // cs // lax.axis_size(SHARE)
+    start = core * (hid_width // cs) + lax.axis_index(SHARE) * part
+    share = lax.dynamic_slice_in_dim(weight, start, part, axis=0)
     share = lax.ppermute(share, "zh", [(0, 1), (1, 0)])
 
     expert_list = expert_ids[:, 0]
@@ -53,7 +55,7 @@
     )
     arrived = exchange(outgoing.reshape(columns, block, -1), "y").reshape(tall, -1)
     arrived, share = lax.optimization_barrier((arrived, share))
-    other_weight = lax.all_gather(share, SHARE, axis=0, tiled=True)
+    near_weight = lax.all_gather(share, SHARE, axis=0, tiled=True)
     grad_flat, hid_flat = arrived[:, :out_width], arrived[:, out_width:]
 
     full = jnp.arange(columns * halves * capacity, dtype=I32)
@@ -81,7 +83,8 @@
         for c in range(cs)
     ]
     near_rows = exchange(jnp.stack(blocks), NEAR).reshape(near * rows, -1)
-    near_rows, other_weight = lax.optimization_barrier((near_rows, other_weight))
+    near_rows, near_weight = lax.optimization_barrier((near_rows, near_weight))
+    far_weight = lax.ppermute(near_weight, "c", [(0, 1), (1, 0)])
     hid_near, grad_near = near_rows[:, : hid_width // xs], near_rows[:, hid_width // xs :]
     of_half = (jnp.arange(near * rows, dtype=I32) // capacity % halves)[:, None]
     zero = jnp.zeros((), BF16)
@@ -98,12 +101,18 @@
     )
     grad_turned, hid_turned = turned[:, :out_width], turned[:, out_width:]
     own = (jnp.arange(tall, dtype=I32) // slots % halves)[:, None] == half
-    proj = jnp.where(
-        own, dot(hid_turned, weight, ((1,), (0,))), dot(hid_turned, other_weight, ((1,), (0,)))
+    first = core == 0
+    lower, upper = hid_turned[:, : hid_width // cs], hid_turned[:, hid_width // cs :]
+    proj_other = dot(jnp.where(first, lower, upper), near_weight, ((1,), (0,)), F32) + dot(
+        jnp.where(first, upper, lower), far_weight, ((1,), (0,)), F32
     )
-    back = jnp.where(
-        own, dot(grad_turned, weight, ((1,), (1,))), dot(grad_turned, other_weight, ((1,), (1,)))
+    proj = jnp.where(own, dot(hid_turned, weight, ((1,), (0,))), proj_other.astype(BF16))
+    back_near = dot(grad_turned, near_weight, ((1,), (1,)))
+    back_far = dot(grad_turned, far_weight, ((1,), (1,)))
+    back_other = jnp.concatenate(
+        [jnp.where(first, back_near, back_far), jnp.where(first, back_far, back_near)], axis=1
     )
+    back = jnp.where(own, dot(grad_turned, weight, ((1,), (1,))), back_other)
     leaving = jnp.concatenate([proj, back], axis=1)
     returned = jnp.concatenate(
         [leaving[:block]]

time: 258 us -> 223 us (0.86)
  waiting for transfers between devices: 138 us -> 89.2 us
  starting transfers between devices: 70.6 us -> 80.1 us
    all_gather x1, waiting for transfers between devices: 72.8 us -> 14.5 us  [shards(): near_weight = lax.all_gather(share, SHARE, axis=0, tiled=True)]
    all_to_all x3, waiting for transfers between devices: 45.1 us -> 55.1 us  [exchange(): return lax.all_to_all(blocks, axes, split_axis=0, concat_axis=0, tiled=True)]
    all_to_all x3, starting transfers between devices: 21.1 us -> 28.5 us  [exchange(): return lax.all_to_all(blocks, axes, split_axis=0, concat_axis=0, tiled=True)]
    dot_general x11 -> x13, matrix products: 18 us -> 19 us  [dot(): lax.dot_general(a, b, (dims, ((), ())), preferred_element_type=F32)]
  transfers between devices with their start and end apart: 12 -> 13, of which waited for: 9 -> 8; matrix products, arithmetic and copies ran while one was open for 7% -> 10% of each run, Pallas kernels for 0% -> 0%
where the time goes in v5:
time: 223 us; the launch traced here: 219 us
  waiting for transfers between devices  89.2 us (40%)
  starting transfers between devices  80.1 us (36%)
  matrix products  19 us (9%)
  between operations  14.4 us (6%)
  other arithmetic  12.9 us (6%)
  local copies, waits for them, and re-layouts  3.45 us (2%)
    all_to_all x3, waiting for transfers between devices, exchange(): return lax.all_to_all(blocks, axes, split_axis=0, concat_axis=0, tiled=True)  55.1 us
    ppermute x7, starting transfers between devices, shards(): lax.ppermute(leaving[k * block:(k + 1) * block], 'y', [(y, (y + k) % colu...  30.3 us
    all_to_all x3, starting transfers between devices, exchange(): return lax.all_to_all(blocks, axes, split_axis=0, concat_axis=0, tiled=True)  28.5 us
    ppermute x1, starting transfers between devices, shards(): share = lax.ppermute(share, 'zh', [(0, 1), (1, 0)])  19.4 us
    dot_general x13, matrix products, dot(): lax.dot_general(a, b, (dims, ((), ())), preferred_element_type=F32)  19 us
    all_gather x1, waiting for transfers between devices, shards(): near_weight = lax.all_gather(share, SHARE, axis=0, tiled=True)  14.5 us
    ppermute x7, waiting for transfers between devices, shards(): lax.ppermute(leaving[k * block:(k + 1) * block], 'y', [(y, (y + k) % colu...  13.2 us
    ppermute x1, waiting for transfers between devices, shards(): share = lax.ppermute(share, 'zh', [(0, 1), (1, 0)])  6.28 us
  transfers between devices with their start and end apart: 13, of which 8 were waited for; matrix products, arithmetic and copies ran while one was open for 10% of the time, Pallas kernels for 0%

profile of v5, /device:TPU:6, one launch (start us, length us, event | category | flops | bytes accessed | tf_op | source)
XLA Modules:
  0.0 219.1 jit_solution(14257904033248293195)
XLA Ops:
  7.2 0.0 copy-start
  7.2 0.8 fusion.77
  8.0 0.2 reduce_window_sum.11
  8.1 0.8 select_reduce_fusion
  9.0 0.7 fusion.112
  9.7 0.3 convolution_convert_fusion.2
  9.9 1.5 convolution_convert_fusion
  11.4 1.1 pad_maximum_fusion
  12.6 7.1 %all-to-all-start = ((bf16[8,24,3072]{2,1,0:T(8,128)(2,1)}), bf16[8,24,3072]{2,1,0:T(8,128)(2,1)S(1)}, u32[]{:S(2)}, u32[]{:S(2)}) async-start(bf16[8,24,3072]{2,1,0:T(8,128)(2,1)} %bitcast.2), calls=%async_computation | async-start | bytes 2359296 | tf_op jit(solution)/shard_map/all_to_all | solution.py:16
  19.7 0.0 all-gather.2.cloned.1.call-start
  19.7 1.0 dynamic-slice_bitcast_fusion
  20.7 19.4 %collective-permute-start = (bf16[64,2048]{1,0:T(8,128)(2,1)S(1)}, bf16[64,2048]{1,0:T(8,128)(2,1)S(1)}, u32[]{:S(2)}, u32[]{:S(2)}) collective-permute-start(bf16[64,2048]{1,0:T(8,128)(2,1)S(1)} %dynamic-slice_bitcast_fusion), channel_id=1, source_target_pairs={{0,1},{1,0},{2,3},{3,2},{4,5},{5,4},{6,7},{7,6},{8,9},{9,8},{10,11... | collective-permute-start | bytes 786440 | tf_op jit(solution)/shard_map/ppermute | solution.py:45
  40.1 6.3 %collective-permute-done = bf16[64,2048]{1,0:T(8,128)(2,1)S(1)} collective-permute-done((bf16[64,2048]{1,0:T(8,128)(2,1)S(1)}, bf16[64,2048]{1,0:T(8,128)(2,1)S(1)}, u32[]{:S(2)}, u32[]{:S(2)}) %collective-permute-start) | collective-permute-done | bytes 262176 | tf_op jit(solution)/shard_map/ppermute | solution.py:45
  46.4 4.9 %all-to-all-done = bf16[8,24,3072]{2,1,0:T(8,128)(2,1)S(1)} async-done(((bf16[8,24,3072]{2,1,0:T(8,128)(2,1)}), bf16[8,24,3072]{2,1,0:T(8,128)(2,1)S(1)}, u32[]{:S(2)}, u32[]{:S(2)}) %all-to-all-start) | async-done | bytes 1179680 | tf_op jit(solution)/shard_map/all_to_all | solution.py:16
  51.3 0.4 convolution_convert_fusion.1
  51.7 1.2 fusion.22
  52.9 0.8 fusion.50
  53.7 0.8 fusion.52
  54.5 0.8 fusion.46
  55.3 0.8 fusion.48
  56.1 0.0 all-gather.2.cloned.1.call-update
  56.1 0.8 fusion.42
  56.9 0.8 fusion.44
  57.7 0.8 fusion.38
  58.5 0.8 fusion.40
  59.3 4.9 %all-to-all-start.1 = ((bf16[8,160,1280]{2,1,0:T(8,128)(2,1)}), bf16[8,160,1280]{2,1,0:T(8,128)(2,1)}, u32[]{:S(2)}, u32[]{:S(2)}) async-start(bf16[8,160,1280]{2,1,0:T(8,128)(2,1)} %fusion.40), calls=%async_computation.1 | async-start | bytes 6553600 | tf_op jit(solution)/shard_map/all_to_all | solution.py:16
  64.2 50.2 %all-to-all-done.1 = bf16[8,160,1280]{2,1,0:T(8,128)(2,1)} async-done(((bf16[8,160,1280]{2,1,0:T(8,128)(2,1)}), bf16[8,160,1280]{2,1,0:T(8,128)(2,1)}, u32[]{:S(2)}, u32[]{:S(2)}) %all-to-all-start.1) | async-done | bytes 3276832 | tf_op jit(solution)/shard_map/all_to_all | solution.py:16
  114.4 14.5 %all-gather.2.cloned.1.call-done = bf16[512,2048]{1,0:T(8,128)(2,1)} async-done(((bf16[64,2048]{1,0:T(8,128)(2,1)}), bf16[512,2048]{1,0:T(8,128)(2,1)}) %all-gather.2.cloned.1.call-update) | async-done | bytes 2097168 | tf_op jit(solution)/shard_map/all_gather | solution.py:58
  129.0 1.9 collective-permute-start.1
  130.9 1.8 broadcast_select_fusion.1
  132.7 4.3 %fusion.13 = bf16[512,1024]{1,0:T(8,128)(2,1)} fusion(bf16[1280,1280]{1,0:T(8,128)(2,1)} %bitcast.13, bf16[1280,256]{1,0:T(8,128)(2,1)S(1)} %get-tuple-element.17, bf16[1280,256]{1,0:T(8,128)(2,1)S(1)} %get-tuple-element.16), kind=kOutput, calls=%fused_computation.32 | convolution fusion | flops 1345323008 | bytes 4980736 | tf_op jit(solution)/shard_map/dot_general | solution.py:20
  137.0 16.5 %all-to-all-start.2 = ((bf16[32,16,1024]{2,1,0:T(8,128)(2,1)}), bf16[32,16,1024]{2,1,0:T(8,128)(2,1)S(1)}, u32[]{:S(2)}, u32[]{:S(2)}) async-start(bf16[32,16,1024]{2,1,0:T(8,128)(2,1)} %bitcast.16), calls=%async_computation.2 | async-start | bytes 2097152 | tf_op jit(solution)/shard_map/all_to_all | solution.py:16
  153.6 0.8 fusion.23
  154.4 0.7 copy-done.2
  155.1 0.9 convolution_convert_fusion.6
  156.0 0.6 fusion.58
  156.6 0.7 copy-done.1
  157.3 1.0 fusion.8
  158.3 0.0 collective-permute-done.1
  158.3 2.3 %fusion.11 = bf16[192,2048]{1,0:T(8,128)(2,1)S(1)} fusion(bf16[192,2048]{1,0:T(8,128)(2,1)S(1)} %fusion.8, f32[192,2048]{1,0:T(8,128)S(1)} %fusion.58, bf16[512,2048]{1,0:T(8,128)(2,1)} %collective-permute-done.1, pred[192]{0:T(512)(128)(4,1)S(1)} %fusion.109, pred[]{:T(512)S(6)} %eq.134, bf16[192,3072]{1,0:T(8,128)(2,1)S(1)} %fusion.23), kind=kOutput, calls=%fused_computation.20 | convolution fusion | flops 403931136 | bytes 5636609 | tf_op jit(solution)/shard_map/dot_general | solution.py:20
  160.6 2.4 %broadcast_select_fusion.3 = (bf16[192,512]{1,0:T(8,128)(2,1)S(1)}, bf16[192,512]{1,0:T(8,128)(2,1)S(1)}) fusion(bf16[192,512]{1,0:T(8,128)(2,1)S(1)} %convolution_convert_fusion.6, pred[]{:T(512)S(6)} %eq.134, bf16[512,2048]{1,0:T(8,128)(2,1)} %collective-permute-done.1, bf16[192,3072]{1,0:T(8,128)(2,1)S(1)} %fusion.23), kind=kOutput, calls=%fused_computation.92 | convolution fusion | flops 402948096 | bytes 3473409 | tf_op jit(solution)/shard_map/dot_general | solution.py:20
  163.0 1.5 fusion.24
  164.6 0.1 pad_maximum_fusion.9
  164.7 0.0 copy-start.3
  164.7 0.0 copy-start.5
  164.7 3.7 %collective-permute-start.2 = (bf16[24,3072]{1,0:T(8,128)(2,1)S(1)}, bf16[24,3072]{1,0:T(8,128)(2,1)S(1)}, u32[]{:S(2)}, u32[]{:S(2)}) collective-permute-start(bf16[24,3072]{1,0:T(8,128)(2,1)S(1)} %get-tuple-element.20), channel_id=1, source_target_pairs={{0,2},{2,4},{4,6},{6,8},{8,10},{10,12},{12,14},{14,0},{1,3},{3,5},... | collective-permute-start | bytes 442376 | tf_op jit(solution)/shard_map/ppermute | solution.py:120
  168.4 4.3 %collective-permute-start.3 = (bf16[24,3072]{1,0:T(8,128)(2,1)S(1)}, bf16[24,3072]{1,0:T(8,128)(2,1)S(1)}, u32[]{:S(2)}, u32[]{:S(2)}) collective-permute-start(bf16[24,3072]{1,0:T(8,128)(2,1)S(1)} %get-tuple-element.21), channel_id=1, source_target_pairs={{0,4},{2,6},{4,8},{6,10},{8,12},{10,14},{12,0},{14,2},{1,5},{3,7},... | collective-permute-start | bytes 442376 | tf_op jit(solution)/shard_map/ppermute | solution.py:120
  172.7 4.6 %collective-permute-start.4 = (bf16[24,3072]{1,0:T(8,128)(2,1)S(1)}, bf16[24,3072]{1,0:T(8,128)(2,1)S(1)}, u32[]{:S(2)}, u32[]{:S(2)}) collective-permute-start(bf16[24,3072]{1,0:T(8,128)(2,1)S(1)} %get-tuple-element.22), channel_id=1, source_target_pairs={{0,6},{2,8},{4,10},{6,12},{8,14},{10,0},{12,2},{14,4},{1,7},{3,9},... | collective-permute-start | bytes 442376 | tf_op jit(solution)/shard_map/ppermute | solution.py:120
  177.3 4.3 %collective-permute-start.5 = (bf16[24,3072]{1,0:T(8,128)(2,1)S(1)}, bf16[24,3072]{1,0:T(8,128)(2,1)S(1)}, u32[]{:S(2)}, u32[]{:S(2)}) collective-permute-start(bf16[24,3072]{1,0:T(8,128)(2,1)S(1)} %get-tuple-element.23), channel_id=1, source_target_pairs={{0,8},{2,10},{4,12},{6,14},{8,0},{10,2},{12,4},{14,6},{1,9},{3,11}... | collective-permute-start | bytes 442376 | tf_op jit(solution)/shard_map/ppermute | solution.py:120
  181.6 4.6 %collective-permute-start.6 = (bf16[24,3072]{1,0:T(8,128)(2,1)S(1)}, bf16[24,3072]{1,0:T(8,128)(2,1)S(1)}, u32[]{:S(2)}, u32[]{:S(2)}) collective-permute-start(bf16[24,3072]{1,0:T(8,128)(2,1)S(1)} %get-tuple-element.24), channel_id=1, source_target_pairs={{0,10},{2,12},{4,14},{6,0},{8,2},{10,4},{12,6},{14,8},{1,11},{3,13... | collective-permute-start | bytes 442376 | tf_op jit(solution)/shard_map/ppermute | solution.py:120
  186.2 0.0 collective-permute-done.2
  186.2 5.5 %collective-permute-start.7 = (bf16[24,3072]{1,0:T(8,128)(2,1)S(1)}, bf16[24,3072]{1,0:T(8,128)(2,1)S(1)}, u32[]{:S(2)}, u32[]{:S(2)}) collective-permute-start(bf16[24,3072]{1,0:T(8,128)(2,1)S(1)} %get-tuple-element.25), channel_id=1, source_target_pairs={{0,12},{2,14},{4,0},{6,2},{8,4},{10,6},{12,8},{14,10},{1,13},{3,15... | collective-permute-start | bytes 442376 | tf_op jit(solution)/shard_map/ppermute | solution.py:120
  191.7 0.0 collective-permute-done.3
  191.7 3.4 %collective-permute-start.8 = (bf16[24,3072]{1,0:T(8,128)(2,1)S(1)}, bf16[24,3072]{1,0:T(8,128)(2,1)S(1)}, u32[]{:S(2)}, u32[]{:S(2)}) collective-permute-start(bf16[24,3072]{1,0:T(8,128)(2,1)S(1)} %get-tuple-element.18), channel_id=1, source_target_pairs={{0,14},{2,0},{4,2},{6,4},{8,6},{10,8},{12,10},{14,12},{1,15},{3,1}... | collective-permute-start | bytes 442376 | tf_op jit(solution)/shard_map/ppermute | solution.py:120
  195.1 0.0 collective-permute-done.4
  195.1 0.4 collective-permute-done.5
  195.5 6.8 %collective-permute-done.6 = bf16[24,3072]{1,0:T(8,128)(2,1)S(1)} collective-permute-done((bf16[24,3072]{1,0:T(8,128)(2,1)S(1)}, bf16[24,3072]{1,0:T(8,128)(2,1)S(1)}, u32[]{:S(2)}, u32[]{:S(2)}) %collective-permute-start.6) | collective-permute-done | bytes 147488 | tf_op jit(solution)/shard_map/ppermute | solution.py:120
  202.4 4.9 %collective-permute-done.7 = bf16[24,3072]{1,0:T(8,128)(2,1)S(1)} collective-permute-done((bf16[24,3072]{1,0:T(8,128)(2,1)S(1)}, bf16[24,3072]{1,0:T(8,128)(2,1)S(1)}, u32[]{:S(2)}, u32[]{:S(2)}) %collective-permute-start.7) | collective-permute-done | bytes 147488 | tf_op jit(solution)/shard_map/ppermute | solution.py:120
  207.3 1.1 collective-permute-done.8
  208.4 1.0 convolution_convert_fusion.4
  209.4 1.8 fusion.28
  211.2 0.2 convert_reduce_fusion
  211.3 0.1 copy.9
  211.5 0.8 broadcast_in_dim_reshape.3
  (21 shorter events, 0.2 us)
Async XLA Ops:
  7.2 2.5 %copy-start = (bf16[128,1024]{1,0:T(8,128)(2,1)S(1)}, bf16[128,1024]{1,0:T(8,128)(2,1)}, u32[]{:S(2)}) copy-start(bf16[128,1024]{1,0:T(8,128)(2,1)} %param.5) | copy-start | bytes 786436
  12.6 38.7 %all-to-all-start = ((bf16[8,24,3072]{2,1,0:T(8,128)(2,1)}), bf16[8,24,3072]{2,1,0:T(8,128)(2,1)S(1)}, u32[]{:S(2)}, u32[]{:S(2)}) async-start(bf16[8,24,3072]{2,1,0:T(8,128)(2,1)} %bitcast.2), calls=%async_computation | async-start | bytes 2359296 | tf_op jit(solution)/shard_map/all_to_all | solution.py:16
  19.7 109.3 %all-gather.2.cloned.1.call-start = ((), (), s32[]{:S(2)}) async-start(), calls=%async_computation.3 | async-start | bytes 2359296 | tf_op jit(solution)/shard_map/all_gather | solution.py:58
  20.7 25.7 %collective-permute-start = (bf16[64,2048]{1,0:T(8,128)(2,1)S(1)}, bf16[64,2048]{1,0:T(8,128)(2,1)S(1)}, u32[]{:S(2)}, u32[]{:S(2)}) collective-permute-start(bf16[64,2048]{1,0:T(8,128)(2,1)S(1)} %dynamic-slice_bitcast_fusion), channel_id=1, source_target_pairs={{0,1},{1,0},{2,3},{3,2},{4,5},{5,4},{6,7},{7,6},{8,9},{9,8},{10,11... | collective-permute-start | bytes 786440 | tf_op jit(solution)/shard_map/ppermute | solution.py:45
  46.4 6.5 %copy-start.4 = (bf16[64,2048]{1,0:T(8,128)(2,1)}, bf16[64,2048]{1,0:T(8,128)(2,1)S(1)}, u32[]{:S(2)}) copy-start(bf16[64,2048]{1,0:T(8,128)(2,1)S(1)} %collective-permute-done) | copy-start | bytes 786436
  59.3 55.2 %all-to-all-start.1 = ((bf16[8,160,1280]{2,1,0:T(8,128)(2,1)}), bf16[8,160,1280]{2,1,0:T(8,128)(2,1)}, u32[]{:S(2)}, u32[]{:S(2)}) async-start(bf16[8,160,1280]{2,1,0:T(8,128)(2,1)} %fusion.40), calls=%async_computation.1 | async-start | bytes 6553600 | tf_op jit(solution)/shard_map/all_to_all | solution.py:16
  129.0 29.4 %collective-permute-start.1 = (bf16[512,2048]{1,0:T(8,128)(2,1)}, bf16[512,2048]{1,0:T(8,128)(2,1)}, u32[]{:S(2)}, u32[]{:S(2)}) collective-permute-start(bf16[512,2048]{1,0:T(8,128)(2,1)} %all-gather.2.cloned.1.call-done), channel_id=1, source_target_pairs={{0,16},{16,0},{1,17},{17,1},{2,18},{18,2},{3,19},{19,3},{4,20},{20... | collective-permute-start | bytes 6291464 | tf_op jit(solution)/shard_map/ppermute | solution.py:87
  137.0 74.2 %all-to-all-start.2 = ((bf16[32,16,1024]{2,1,0:T(8,128)(2,1)}), bf16[32,16,1024]{2,1,0:T(8,128)(2,1)S(1)}, u32[]{:S(2)}, u32[]{:S(2)}) async-start(bf16[32,16,1024]{2,1,0:T(8,128)(2,1)} %bitcast.16), calls=%async_computation.2 | async-start | bytes 2097152 | tf_op jit(solution)/shard_map/all_to_all | solution.py:16
  153.5 1.6 copy-start.2
  155.1 2.2 copy-start.1
  164.7 44.7 %copy-start.3 = (bf16[128,2048]{1,0:T(8,128)(2,1)S(1)}, bf16[128,2048]{1,0:T(8,128)(2,1)}, u32[]{:S(2)}) copy-start(bf16[128,2048]{1,0:T(8,128)(2,1)} %param.9) | copy-start | bytes 1572868
  164.7 44.7 %copy-start.5 = (f32[128,1]{0,1:T(1,128)S(1)}, f32[128,1]{0,1:T(1,128)}, u32[]{:S(2)}) copy-start(f32[128,1]{0,1:T(1,128)} %param.7) | copy-start | bytes 1540
  164.7 21.5 %collective-permute-start.2 = (bf16[24,3072]{1,0:T(8,128)(2,1)S(1)}, bf16[24,3072]{1,0:T(8,128)(2,1)S(1)}, u32[]{:S(2)}, u32[]{:S(2)}) collective-permute-start(bf16[24,3072]{1,0:T(8,128)(2,1)S(1)} %get-tuple-element.20), channel_id=1, source_target_pairs={{0,2},{2,4},{4,6},{6,8},{8,10},{10,12},{12,14},{14,0},{1,3},{3,5},... | collective-permute-start | bytes 442376 | tf_op jit(solution)/shard_map/ppermute | solution.py:120
  168.4 23.3 %collective-permute-start.3 = (bf16[24,3072]{1,0:T(8,128)(2,1)S(1)}, bf16[24,3072]{1,0:T(8,128)(2,1)S(1)}, u32[]{:S(2)}, u32[]{:S(2)}) collective-permute-start(bf16[24,3072]{1,0:T(8,128)(2,1)S(1)} %get-tuple-element.21), channel_id=1, source_target_pairs={{0,4},{2,6},{4,8},{6,10},{8,12},{10,14},{12,0},{14,2},{1,5},{3,7},... | collective-permute-start | bytes 442376 | tf_op jit(solution)/shard_map/ppermute | solution.py:120
  172.7 22.4 %collective-permute-start.4 = (bf16[24,3072]{1,0:T(8,128)(2,1)S(1)}, bf16[24,3072]{1,0:T(8,128)(2,1)S(1)}, u32[]{:S(2)}, u32[]{:S(2)}) collective-permute-start(bf16[24,3072]{1,0:T(8,128)(2,1)S(1)} %get-tuple-element.22), channel_id=1, source_target_pairs={{0,6},{2,8},{4,10},{6,12},{8,14},{10,0},{12,2},{14,4},{1,7},{3,9},... | collective-permute-start | bytes 442376 | tf_op jit(solution)/shard_map/ppermute | solution.py:120
  177.3 18.2 %collective-permute-start.5 = (bf16[24,3072]{1,0:T(8,128)(2,1)S(1)}, bf16[24,3072]{1,0:T(8,128)(2,1)S(1)}, u32[]{:S(2)}, u32[]{:S(2)}) collective-permute-start(bf16[24,3072]{1,0:T(8,128)(2,1)S(1)} %get-tuple-element.23), channel_id=1, source_target_pairs={{0,8},{2,10},{4,12},{6,14},{8,0},{10,2},{12,4},{14,6},{1,9},{3,11}... | collective-permute-start | bytes 442376 | tf_op jit(solution)/shard_map/ppermute | solution.py:120
  181.6 20.8 %collective-permute-start.6 = (bf16[24,3072]{1,0:T(8,128)(2,1)S(1)}, bf16[24,3072]{1,0:T(8,128)(2,1)S(1)}, u32[]{:S(2)}, u32[]{:S(2)}) collective-permute-start(bf16[24,3072]{1,0:T(8,128)(2,1)S(1)} %get-tuple-element.24), channel_id=1, source_target_pairs={{0,10},{2,12},{4,14},{6,0},{8,2},{10,4},{12,6},{14,8},{1,11},{3,13... | collective-permute-start | bytes 442376 | tf_op jit(solution)/shard_map/ppermute | solution.py:120
  186.2 21.1 %collective-permute-start.7 = (bf16[24,3072]{1,0:T(8,128)(2,1)S(1)}, bf16[24,3072]{1,0:T(8,128)(2,1)S(1)}, u32[]{:S(2)}, u32[]{:S(2)}) collective-permute-start(bf16[24,3072]{1,0:T(8,128)(2,1)S(1)} %get-tuple-element.25), channel_id=1, source_target_pairs={{0,12},{2,14},{4,0},{6,2},{8,4},{10,6},{12,8},{14,10},{1,13},{3,15... | collective-permute-start | bytes 442376 | tf_op jit(solution)/shard_map/ppermute | solution.py:120
  191.7 16.7 %collective-permute-start.8 = (bf16[24,3072]{1,0:T(8,128)(2,1)S(1)}, bf16[24,3072]{1,0:T(8,128)(2,1)S(1)}, u32[]{:S(2)}, u32[]{:S(2)}) collective-permute-start(bf16[24,3072]{1,0:T(8,128)(2,1)S(1)} %get-tuple-element.18), channel_id=1, source_target_pairs={{0,14},{2,0},{4,2},{6,4},{8,6},{10,8},{12,10},{14,12},{1,15},{3,1}... | collective-permute-start | bytes 442376 | tf_op jit(solution)/shard_map/ppermute | solution.py:120
Sparse Core Ops, SparseCore 0:
  56.2 72.6 all-gather.1

commit v6 on v1

v6 whole, which is shorter than its diff:
```python
import jax
import jax.numpy as jnp
from jax import lax
from jax.sharding import Mesh, PartitionSpec as P

F32, BF16, I32 = jnp.float32, jnp.bfloat16, jnp.int32
DP = ("zl", "x", "c")
EXP = ("y", "zh")
NEAR = ("x", "c")
LINE = ("zl", "c")


def exchange(blocks, axes):
    return lax.all_to_all(blocks, axes, split_axis=0, concat_axis=0, tiled=True)


def dot(a, b, dims, out=BF16):
    return lax.dot_general(a, b, (dims, ((), ())), preferred_element_type=F32).astype(out)


def chooser(wanted, count):
    return (wanted[:, None] == jnp.arange(count, dtype=I32)[None, :]).astype(BF16)


def shards(hidden, expert_ids, gate_weights, down_weight, out_grad):
    tok_rows, hid_width = hidden.shape
    out_width = out_grad.shape[1]
    experts = lax.axis_size(EXP)
    xs, cs, near = (lax.axis_size(axes) for axes in ("x", "c", NEAR))
    capacity = 5 * tok_rows // (4 * experts)
    rows = experts * capacity
    block = 16 * (-(-(capacity + (capacity + 1) // 2) // 16))
    tall = experts * block
    strip = hid_width // lax.axis_size(DP)
    weight = down_weight[0]

    def wide_place(expert, rank):
        return expert * block + rank

    def pair_place(expert, rank):
        return expert * block + capacity + rank // 2

    def paired(narrow, odd):
        zero = jnp.zeros((), narrow.dtype)
        return jnp.concatenate(
            [jnp.where(odd, zero, narrow), jnp.where(odd, narrow, zero)], axis=1
        )

    def unpaired(wide, odd):
        return jnp.where(odd, wide[:, hid_width:], wide[:, :hid_width])

    expert_list = expert_ids[:, 0]
    onehot = (expert_list[:, None] == jnp.arange(experts, dtype=I32)[None, :]).astype(I32)
    row_rank = jnp.sum(onehot * (jnp.cumsum(onehot, axis=0) - 1), axis=1)
    odd = (row_rank % 2 == 1)[:, None]
    places = jnp.concatenate(
        [wide_place(expert_list, row_rank), pair_place(expert_list, row_rank)]
    )
    placer = (jnp.arange(tall, dtype=I32)[:, None] == places[None, :]).astype(BF16)
    grad_rows = (gate_weights * out_grad.astype(F32)).astype(BF16)
    outgoing = dot(
        placer, jnp.concatenate([grad_rows, paired(hidden, odd)], axis=0), ((1,), (0,))
    )
    arrived = exchange(outgoing.reshape(experts, block, -1), EXP).reshape(tall, -1)
    full = jnp.arange(rows, dtype=I32)
    source, rank = full // capacity, full % capacity
    full_odd = (rank % 2 == 1)[:, None]
    picker = chooser(jnp.concatenate([wide_place(source, rank), pair_place(source, rank)]), tall)
    picked = dot(picker, arrived, ((1,), (0,)))
    grad_flat, hid_flat = picked[:rows], unpaired(picked[rows:], full_odd)

    quarter, half = hid_width // xs, out_width // cs
    place = jnp.arange(hid_width, dtype=I32)
    in_quarter = place % quarter
    column = (
        in_quarter // (cs * strip) * (near * strip)
        + place // quarter * (cs * strip)
        + in_quarter % (cs * strip)
    )
    hid_sorted = dot(hid_flat, chooser(column, hid_width), ((1,), (1,)))
    blocks = [
        jnp.concatenate(
            [
                hid_sorted[:, x * quarter : (x + 1) * quarter],
                grad_flat[:, c * half : (c + 1) * half],
            ],
            axis=1,
        )
        for x in range(xs)
        for c in range(cs)
    ]
    near_rows = exchange(jnp.stack(blocks), NEAR).reshape(near * rows, -1)

    proj = dot(hid_flat, weight, ((1,), (0,)))
    back = dot(grad_flat, weight, ((1,), (1,)))
    leaving = dot(
        picker, jnp.concatenate([proj, paired(back, full_odd)], axis=0), ((0,), (0,))
    )
    leaving, near_rows = lax.optimization_barrier((leaving, near_rows))
    returned = exchange(leaving.reshape(experts, block, -1), EXP).reshape(tall, -1)
    partial_grad = dot(near_rows[:, :quarter], near_rows[:, quarter:], ((0,), (0,)))

    returned, partial_grad = lax.optimization_barrier((returned, partial_grad))
    parts = exchange(partial_grad.reshape(-1, strip, half), LINE)
    fetched = dot(placer, returned, ((0,), (0,)), F32)
    projected = fetched[:tok_rows]
    layer_out = (gate_weights * projected).astype(BF16)
    gate_grad = jnp.sum(out_grad.astype(F32) * projected, axis=1, keepdims=True)
    hidden_grad = unpaired(fetched[tok_rows:], odd).astype(BF16)
    summed = jnp.sum(parts.reshape(-1, cs, strip, half).astype(F32), axis=0)
    weight_grad = summed.swapaxes(0, 1).reshape(strip, out_width)
    return (layer_out, hidden_grad, gate_grad, weight_grad[None])


def solution(mesh):
    fine = Mesh(mesh.devices.reshape(8, 4, 2, 8, 2), DP + EXP)
    tokens = P(DP + EXP, None)
    return jax.shard_map(
        shards,
        mesh=fine,
        in_specs=(tokens, tokens, tokens, P(EXP, None, None), tokens),
        out_specs=(tokens, tokens, tokens, P(EXP, DP, None)),
        check_vma=False,
    )
```

time: 282 us -> 247 us (0.88)
  the two profiles are of different devices: /device:TPU:24 before, /device:TPU:6 now
where the time goes in v6:
time: 247 us; the launch traced here: 243 us
  waiting for transfers between devices  110 us (45%)
  starting transfers between devices  99.8 us (40%)
  matrix products  16.2 us (7%)
  other arithmetic  13.5 us (5%)
  local copies, waits for them, and re-layouts  2.65 us (1%)
    all_to_all x4, waiting for transfers between devices, exchange(): return lax.all_to_all(blocks, axes, split_axis=0, concat_axis=0, tiled=True)  110 us
    all_to_all x4, starting transfers between devices, exchange(): return lax.all_to_all(blocks, axes, split_axis=0, concat_axis=0, tiled=True)  99.8 us
    dot_general x8, matrix products, dot(): lax.dot_general(a, b, (dims, ((), ())), preferred_element_type=F32)  16.2 us
    unnamed x7, other arithmetic  5.45 us
  transfers between devices with their start and end apart: 4, of which 4 were waited for; matrix products, arithmetic and copies ran while one was open for 6% of the time, Pallas kernels for 0%

profile of v6, /device:TPU:6, one launch (start us, length us, event | category | flops | bytes accessed | tf_op | source)
XLA Modules:
  0.0 243.1 jit_solution(9469718345960931496)
XLA Ops:
  0.6 0.7 fusion.54
  1.4 0.2 reduce_window_sum.11
  1.5 0.8 select_reduce_fusion
  2.4 0.7 multiply_add_fusion
  3.1 1.2 fusion.23
  4.3 1.1 broadcast_select_fusion.3
  5.3 1.4 convolution_convert_fusion.1
  6.8 24.1 %all-to-all-start = ((bf16[16,16,2048]{2,1,0:T(8,128)(2,1)}), bf16[16,16,2048]{2,1,0:T(8,128)(2,1)S(1)}, u32[]{:S(2)}, u32[]{:S(2)}) async-start(bf16[16,16,2048]{2,1,0:T(8,128)(2,1)} %bitcast.2), calls=%async_computation | async-start | bytes 2097152 | tf_op jit(solution)/shard_map/all_to_all | solution.py:14
  30.9 0.1 pad_add_fusion
  31.0 31.9 %all-to-all-done = bf16[16,16,2048]{2,1,0:T(8,128)(2,1)S(1)} async-done(((bf16[16,16,2048]{2,1,0:T(8,128)(2,1)}), bf16[16,16,2048]{2,1,0:T(8,128)(2,1)S(1)}, u32[]{:S(2)}, u32[]{:S(2)}) %all-to-all-start) | async-done | bytes 1048608 | tf_op jit(solution)/shard_map/all_to_all | solution.py:14
  62.9 0.6 convolution_convert_fusion
  63.5 0.0 copy-start.1
  63.5 1.1 fusion.19
  64.7 0.8 fusion.46
  65.5 0.8 fusion.48
  66.2 0.0 copy-done.1
  66.2 0.8 fusion.42
  67.0 0.8 fusion.44
  67.8 0.8 fusion.38
  68.6 0.8 fusion.40
  69.4 0.8 fusion.34
  70.2 0.8 fusion.36
  71.0 4.7 %all-to-all-start.1 = ((bf16[8,160,1280]{2,1,0:T(8,128)(2,1)}), bf16[8,160,1280]{2,1,0:T(8,128)(2,1)S(1)}, u32[]{:S(2)}, u32[]{:S(2)}) async-start(bf16[8,160,1280]{2,1,0:T(8,128)(2,1)} %fusion.36), calls=%async_computation.1 | async-start | bytes 6553600 | tf_op jit(solution)/shard_map/all_to_all | solution.py:14
  75.7 0.0 copy-start.2
  75.7 3.4 %fusion.7 = bf16[160,2048]{1,0:T(8,128)(2,1)S(1)} fusion(bf16[1,1024,2048]{2,1,0:T(8,128)(2,1)} %param.8, bf16[320,2048]{1,0:T(8,128)(2,1)} %copy-done.1, pred[160]{0:T(512)(128)(4,1)S(1)} %fusion.77), kind=kOutput, calls=%fused_computation.11 | convolution fusion | flops 671580160 | bytes 5505184 | tf_op jit(solution)/shard_map/dot_general | solution.py:18
  79.1 0.0 copy-done.2
  79.1 3.7 %broadcast_select_fusion.1 = (bf16[160,1024]{1,0:T(8,128)(2,1)S(1)}, bf16[160,1024]{1,0:T(8,128)(2,1)S(1)}) fusion(pred[160]{0:T(512)(128)(4,1)S(1)} %fusion.77, bf16[1,1024,2048]{2,1,0:T(8,128)(2,1)} %param.8, bf16[320,2048]{1,0:T(8,128)(2,1)S(1)} %copy-done.2), kind=kOutput, calls=%fused_computation.63 | convolution fusion | flops 671580160 | bytes 5505536 | tf_op jit(solution)/shard_map/dot_general | solution.py:18
  82.8 1.8 convolution_convert_fusion.2
  84.7 28.8 %all-to-all-done.1 = bf16[8,160,1280]{2,1,0:T(8,128)(2,1)S(1)} async-done(((bf16[8,160,1280]{2,1,0:T(8,128)(2,1)}), bf16[8,160,1280]{2,1,0:T(8,128)(2,1)S(1)}, u32[]{:S(2)}, u32[]{:S(2)}) %all-to-all-start.1) | async-done | bytes 3276832 | tf_op jit(solution)/shard_map/all_to_all | solution.py:14
  113.5 0.0 copy-start
  113.5 1.7 copy-done
  115.2 10.2 %all-to-all-start.2 = ((bf16[16,16,2048]{2,1,0:T(8,128)(2,1)}), bf16[16,16,2048]{2,1,0:T(8,128)(2,1)S(1)}, u32[]{:S(2)}, u32[]{:S(2)}) async-start(bf16[16,16,2048]{2,1,0:T(8,128)(2,1)} %bitcast.63), calls=%async_computation.2 | async-start | bytes 2097152 | tf_op jit(solution)/shard_map/all_to_all | solution.py:14
  125.3 3.6 %fusion.16 = bf16[256,1024]{1,0:T(8,128)(2,1)} fusion(bf16[1280,1280]{1,0:T(8,128)(2,1)} %bitcast.61), kind=kOutput, calls=%fused_computation.20 | convolution fusion | flops 671350784 | bytes 3801088 | tf_op jit(solution)/shard_map/dot_general | solution.py:18
  129.0 0.0 copy-start.3
  129.0 0.0 copy-start.4
  129.0 26.5 %all-to-all-done.2 = bf16[16,16,2048]{2,1,0:T(8,128)(2,1)S(1)} async-done(((bf16[16,16,2048]{2,1,0:T(8,128)(2,1)}), bf16[16,16,2048]{2,1,0:T(8,128)(2,1)S(1)}, u32[]{:S(2)}, u32[]{:S(2)}) %all-to-all-start.2) | async-done | bytes 1048608 | tf_op jit(solution)/shard_map/all_to_all | solution.py:14
  155.5 60.8 %all-to-all-start.3 = ((bf16[16,16,1024]{2,1,0:T(8,128)(2,1)}), bf16[16,16,1024]{2,1,0:T(8,128)(2,1)S(1)}, u32[]{:S(2)}, u32[]{:S(2)}) async-start(bf16[16,16,1024]{2,1,0:T(8,128)(2,1)} %bitcast.17), calls=%async_computation.3 | async-start | bytes 1048576 | tf_op jit(solution)/shard_map/all_to_all | solution.py:14
  216.3 0.5 fusion.49
  216.8 0.9 fusion.32
  217.7 0.0 copy-done.3
  217.7 0.0 copy-done.4
  217.7 1.5 fusion.24
  219.2 23.0 %all-to-all-done.3 = bf16[16,16,1024]{2,1,0:T(8,128)(2,1)S(1)} async-done(((bf16[16,16,1024]{2,1,0:T(8,128)(2,1)}), bf16[16,16,1024]{2,1,0:T(8,128)(2,1)S(1)}, u32[]{:S(2)}, u32[]{:S(2)}) %all-to-all-start.3) | async-done | bytes 524320 | tf_op jit(solution)/shard_map/all_to_all | solution.py:14
  242.1 0.1 convert_reduce_fusion
  242.2 0.1 copy.9
  242.3 0.8 broadcast_in_dim_reshape.3
  (7 shorter events, 0.1 us)
Async XLA Ops:
  6.8 56.2 %all-to-all-start = ((bf16[16,16,2048]{2,1,0:T(8,128)(2,1)}), bf16[16,16,2048]{2,1,0:T(8,128)(2,1)S(1)}, u32[]{:S(2)}, u32[]{:S(2)}) async-start(bf16[16,16,2048]{2,1,0:T(8,128)(2,1)} %bitcast.2), calls=%async_computation | async-start | bytes 2097152 | tf_op jit(solution)/shard_map/all_to_all | solution.py:14
  63.5 2.8 %copy-start.1 = (bf16[320,2048]{1,0:T(8,128)(2,1)}, bf16[320,2048]{1,0:T(8,128)(2,1)S(1)}, u32[]{:S(2)}) copy-start(bf16[320,2048]{1,0:T(8,128)(2,1)S(1)} %convolution_convert_fusion) | copy-start | bytes 3932164
  71.0 42.5 %all-to-all-start.1 = ((bf16[8,160,1280]{2,1,0:T(8,128)(2,1)}), bf16[8,160,1280]{2,1,0:T(8,128)(2,1)S(1)}, u32[]{:S(2)}, u32[]{:S(2)}) async-start(bf16[8,160,1280]{2,1,0:T(8,128)(2,1)} %fusion.36), calls=%async_computation.1 | async-start | bytes 6553600 | tf_op jit(solution)/shard_map/all_to_all | solution.py:14
  75.7 3.4 %copy-start.2 = (bf16[320,2048]{1,0:T(8,128)(2,1)S(1)}, bf16[320,2048]{1,0:T(8,128)(2,1)}, u32[]{:S(2)}) copy-start(bf16[320,2048]{1,0:T(8,128)(2,1)} %copy-done.1) | copy-start | bytes 3932164
  113.5 1.7 copy-start
  115.2 40.3 %all-to-all-start.2 = ((bf16[16,16,2048]{2,1,0:T(8,128)(2,1)}), bf16[16,16,2048]{2,1,0:T(8,128)(2,1)S(1)}, u32[]{:S(2)}, u32[]{:S(2)}) async-start(bf16[16,16,2048]{2,1,0:T(8,128)(2,1)} %bitcast.63), calls=%async_computation.2 | async-start | bytes 2097152 | tf_op jit(solution)/shard_map/all_to_all | solution.py:14
  129.0 88.7 %copy-start.3 = (bf16[128,2048]{1,0:T(8,128)(2,1)S(1)}, bf16[128,2048]{1,0:T(8,128)(2,1)}, u32[]{:S(2)}) copy-start(bf16[128,2048]{1,0:T(8,128)(2,1)} %param.9) | copy-start | bytes 1572868
  129.0 88.7 %copy-start.4 = (f32[128,1]{0,1:T(1,128)S(1)}, f32[128,1]{0,1:T(1,128)}, u32[]{:S(2)}) copy-start(f32[128,1]{0,1:T(1,128)} %param.7) | copy-start | bytes 1540
  155.5 86.6 %all-to-all-start.3 = ((bf16[16,16,1024]{2,1,0:T(8,128)(2,1)}), bf16[16,16,1024]{2,1,0:T(8,128)(2,1)S(1)}, u32[]{:S(2)}, u32[]{:S(2)}) async-start(bf16[16,16,1024]{2,1,0:T(8,128)(2,1)} %bitcast.17), calls=%async_computation.3 | async-start | bytes 1048576 | tf_op jit(solution)/shard_map/all_to_all | solution.py:14

commit v7 on v3

v7 whole, which is shorter than its diff:
```python
import functools

import jax
import jax.numpy as jnp
from jax import lax
from jax.experimental import pallas as pl
from jax.experimental.pallas import tpu as pltpu
from jax.sharding import Mesh, PartitionSpec as P

F32, BF16, I32 = jnp.float32, jnp.bfloat16, jnp.int32
LINE = ("zq", "zp")
DP = LINE + ("x", "c")
EXP = ("y", "zh")
NEAR = ("x", "c")
SHARE = ("zp", "x", "c")
RING = ("zh",) + LINE + ("c",)


def exchange(blocks, axes):
    return lax.all_to_all(blocks, axes, split_axis=0, concat_axis=0, tiled=True)


def dot(a, b, dims, out=BF16):
    return lax.dot_general(a, b, (dims, ((), ())), preferred_element_type=F32).astype(out)


def pack_kernel(capacity, slots, strip, xs, cs, hid_width, arrived, blocks):
    tall, width = arrived.shape
    rows = blocks.shape[1]
    quarter = hid_width // xs
    half = (width - hid_width) // cs
    full = lax.broadcasted_iota(I32, (rows, tall), 0)
    wanted = full // capacity * slots + full % capacity
    compact = (wanted == lax.broadcasted_iota(I32, (rows, tall), 1)).astype(BF16)
    kept = dot(compact, arrived[...], ((1,), (0,)))
    group = cs * strip
    place = lax.broadcasted_iota(I32, (hid_width, hid_width), 0)
    target = place // group % xs * quarter + place // (group * xs) * group + place % group
    sorter = (target == lax.broadcasted_iota(I32, (hid_width, hid_width), 1)).astype(BF16)
    hid = dot(kept[:, width - hid_width :], sorter, ((1,), (0,)))
    for x in range(xs):
        for c in range(cs):
            blocks[x * cs + c, :, :quarter] = hid[:, x * quarter : (x + 1) * quarter]
            blocks[x * cs + c, :, quarter:] = kept[:, c * half : (c + 1) * half]


def shards(hidden, expert_ids, gate_weights, down_weight, out_grad):
    tok_rows, hid_width = hidden.shape
    out_width = out_grad.shape[1]
    columns, halves = lax.axis_size("y"), lax.axis_size("zh")
    experts = columns * halves
    xs, cs, near = (lax.axis_size(axes) for axes in ("x", "c", NEAR))
    capacity = 5 * tok_rows // (4 * experts)
    slots = capacity + -capacity % 4
    block = halves * slots
    tall = columns * block
    strip = hid_width // lax.axis_size(DP)
    half = lax.axis_index("zh")
    weight = down_weight[0]

    part = hid_width // lax.axis_size(SHARE)
    start = lax.axis_index(SHARE) * part
    share = lax.dynamic_slice_in_dim(weight, start, part, axis=0)
    share = lax.ppermute(share, "zh", [(0, 1), (1, 0)])

    expert_list = expert_ids[:, 0]
    onehot = (expert_list[:, None] == jnp.arange(experts, dtype=I32)[None, :]).astype(I32)
    row_rank = jnp.sum(onehot * (jnp.cumsum(onehot, axis=0) - 1), axis=1)
    slot_index = expert_list * slots + row_rank
    placer = (jnp.arange(tall, dtype=I32)[:, None] == slot_index[None, :]).astype(BF16)
    grad_rows = (gate_weights * out_grad.astype(F32)).astype(BF16)
    outgoing = jnp.concatenate(
        [dot(placer, grad_rows, ((1,), (0,))), dot(placer, hidden, ((1,), (0,)))], axis=1
    )
    arrived = exchange(outgoing.reshape(columns, block, -1), "y").reshape(tall, -1)
    arrived, share = lax.optimization_barrier((arrived, share))
    beside = lax.ppermute(share, "zp", [(0, 1), (1, 0)])

    rows = experts * capacity
    near_rows = exchange(
        pl.pallas_call(
            functools.partial(pack_kernel, capacity, slots, strip, xs, cs, hid_width),
            out_shape=jax.ShapeDtypeStruct(
                (near, rows, hid_width // xs + out_width // cs), BF16
            ),
            compiler_params=pltpu.CompilerParams(vmem_limit_bytes=40 * 2**20),
            cost_estimate=pl.CostEstimate(
                flops=2 * rows * (tall * (hid_width + out_width) + hid_width**2),
                bytes_accessed=8 * 2**20,
                transcendentals=0,
            ),
        )(arrived),
        NEAR,
    ).reshape(near * rows, -1)
    near_rows, share, beside = lax.optimization_barrier((near_rows, share, beside))
    even = lax.axis_index("zp") == 0
    pair = jnp.stack([jnp.where(even, share, beside), jnp.where(even, beside, share)])
    other_weight = lax.all_gather(pair, NEAR, axis=1, tiled=True).reshape(hid_width, -1)
    hid_near, grad_near = near_rows[:, : hid_width // xs], near_rows[:, hid_width // xs :]
    of_half = (jnp.arange(near * rows, dtype=I32) // capacity % halves)[:, None]
    zero = jnp.zeros((), BF16)
    by_half = jnp.concatenate(
        [jnp.where(of_half == h, hid_near, zero) for h in range(halves)], axis=1
    )
    partial_grad = dot(by_half, grad_near, ((0,), (0,)))
    parts = exchange(partial_grad.reshape(-1, strip, out_width // cs), RING)

    grad_flat, hid_flat = arrived[:, :out_width], arrived[:, out_width:]
    own = (jnp.arange(tall, dtype=I32) // slots % halves)[:, None] == half
    proj = jnp.where(
        own, dot(hid_flat, weight, ((1,), (0,))), dot(hid_flat, other_weight, ((1,), (0,)))
    )
    back = jnp.where(
        own, dot(grad_flat, weight, ((1,), (1,))), dot(grad_flat, other_weight, ((1,), (1,)))
    )
    leaving = jnp.concatenate([proj, back], axis=1)
    leaving, parts = lax.optimization_barrier((leaving, parts))
    returned = exchange(leaving.reshape(columns, block, -1), "y").reshape(tall, -1)
    projected = dot(placer, returned[:, :out_width], ((0,), (0,)), F32)
    layer_out = (gate_weights * projected).astype(BF16)
    gate_grad = jnp.sum(out_grad.astype(F32) * projected, axis=1, keepdims=True)
    hidden_grad = dot(placer, returned[:, out_width:], ((0,), (0,)))

    summed = jnp.sum(parts.reshape(-1, cs, strip, out_width // cs).astype(F32), axis=0)
    weight_grad = summed.swapaxes(0, 1).reshape(strip, out_width)
    return (layer_out, hidden_grad, gate_grad, weight_grad[None])


def solution(mesh):
    fine = Mesh(mesh.devices.reshape(4, 2, 4, 2, 8, 2), DP + EXP)
    tokens = P(DP + EXP, None)
    return jax.shard_map(
        shards,
        mesh=fine,
        in_specs=(tokens, tokens, tokens, P(EXP, None, None), tokens),
        out_specs=(tokens, tokens, tokens, P(EXP, DP, None)),
        check_vma=False,
    )
```

time: 224 us -> 235 us (1.049)
  starting transfers between devices: 55.2 us -> 77.1 us
  other arithmetic: 14.5 us -> 7.61 us
  waiting for transfers between devices: 115 us -> 111 us
  Pallas kernels: 0 us -> 2.68 us
    all_to_all x3 -> x4, waiting for transfers between devices: 29 us -> 75.4 us  [exchange(): return lax.all_to_all(blocks, axes, split_axis=0, concat_axis=0, tiled=True)]
    all_gather x1, waiting for transfers between devices: 49.1 us -> 23 us  [shards(): lax.all_gather(pair, NEAR, axis=1, tiled=True).reshape(hid_width, -1)]
    all_to_all x3 -> x4, starting transfers between devices: 18.6 us -> 42.6 us  [exchange(): return lax.all_to_all(blocks, axes, split_axis=0, concat_axis=0, tiled=True)]
    reduce_scatter x1 -> x0, waiting for transfers between devices: 23.5 us -> none  [shards(): lax.psum_scatter(partial_grad, RING, scatter_dimension=0, tiled=True)]
    unnamed x7 -> x0, other arithmetic: 5.5 us -> none
    pallas_call x0 -> x1, Pallas kernels: none -> 2.68 us  [shards(): pl.pallas_call(functools.partial(pack_kernel, capacity, slots, strip, xs,...]
    dot_general x11 -> x9, matrix products: 16.5 us -> 16.2 us  [dot(): lax.dot_general(a, b, (dims, ((), ())), preferred_element_type=F32)]
  transfers between devices with their start and end apart: 8 -> 7, of which waited for: 7 -> 7; matrix products, arithmetic and copies ran while one was open for 7% -> 7% of each run, Pallas kernels for 0% -> 0%
where the time goes in v7:
time: 235 us; the launch traced here: 232 us
  waiting for transfers between devices  111 us (47%)
  starting transfers between devices  77.1 us (33%)
  matrix products  16.2 us (7%)
  between operations  14.2 us (6%)
  other arithmetic  7.61 us (3%)
  Pallas kernels  2.68 us (1%)
  local copies, waits for them, and re-layouts  2.62 us (1%)
    all_to_all x4, waiting for transfers between devices, exchange(): return lax.all_to_all(blocks, axes, split_axis=0, concat_axis=0, tiled=True)  75.4 us
    all_to_all x4, starting transfers between devices, exchange(): return lax.all_to_all(blocks, axes, split_axis=0, concat_axis=0, tiled=True)  42.6 us
    all_gather x1, waiting for transfers between devices, shards(): lax.all_gather(pair, NEAR, axis=1, tiled=True).reshape(hid_width, -1)  23 us
    ppermute x1, starting transfers between devices, shards(): share = lax.ppermute(share, 'zh', [(0, 1), (1, 0)])  19.4 us
    dot_general x9, matrix products, dot(): lax.dot_general(a, b, (dims, ((), ())), preferred_element_type=F32)  16.2 us
    ppermute x1, starting transfers between devices, shards(): beside = lax.ppermute(share, 'zp', [(0, 1), (1, 0)])  15.1 us
    ppermute x1, waiting for transfers between devices, shards(): beside = lax.ppermute(share, 'zp', [(0, 1), (1, 0)])  6.6 us
    ppermute x1, waiting for transfers between devices, shards(): share = lax.ppermute(share, 'zh', [(0, 1), (1, 0)])  6.31 us
  transfers between devices with their start and end apart: 7, of which 7 were waited for; matrix products, arithmetic and copies ran while one was open for 7% of the time, Pallas kernels for 0%

profile of v7, /device:TPU:6, one launch (start us, length us, event | category | flops | bytes accessed | tf_op | source)
XLA Modules:
  0.0 231.7 jit_solution(8018213455070180093)
XLA Ops:
  7.2 0.0 copy-start
  7.2 0.8 fusion.35
  8.0 0.2 reduce_window_sum.11
  8.1 0.8 select_reduce_fusion
  9.0 0.7 multiply_add_fusion
  9.6 0.0 copy-done
  9.6 0.3 convolution_convert_fusion.3
  9.9 1.5 convolution_convert_fusion.1
  11.4 1.1 pad_maximum_fusion
  12.5 7.1 %all-to-all-start = ((bf16[8,24,3072]{2,1,0:T(8,128)(2,1)}), bf16[8,24,3072]{2,1,0:T(8,128)(2,1)S(1)}, u32[]{:S(2)}, u32[]{:S(2)}) async-start(bf16[8,24,3072]{2,1,0:T(8,128)(2,1)} %bitcast.2), calls=%async_computation | async-start | bytes 2359296 | tf_op jit(solution)/shard_map/all_to_all | solution.py:20
  19.6 1.0 dynamic-slice_bitcast_fusion
  20.6 19.4 %collective-permute-start = (bf16[64,2048]{1,0:T(8,128)(2,1)S(1)}, bf16[64,2048]{1,0:T(8,128)(2,1)S(1)}, u32[]{:S(2)}, u32[]{:S(2)}) collective-permute-start(bf16[64,2048]{1,0:T(8,128)(2,1)S(1)} %dynamic-slice_bitcast_fusion), channel_id=1, source_target_pairs={{0,1},{1,0},{2,3},{3,2},{4,5},{5,4},{6,7},{7,6},{8,9},{9,8},{10,11... | collective-permute-start | bytes 786440 | tf_op jit(solution)/shard_map/ppermute | solution.py:64
  40.0 6.3 %collective-permute-done = bf16[64,2048]{1,0:T(8,128)(2,1)S(1)} collective-permute-done((bf16[64,2048]{1,0:T(8,128)(2,1)S(1)}, bf16[64,2048]{1,0:T(8,128)(2,1)S(1)}, u32[]{:S(2)}, u32[]{:S(2)}) %collective-permute-start) | collective-permute-done | bytes 262176 | tf_op jit(solution)/shard_map/ppermute | solution.py:64
  46.3 4.9 %all-to-all-done = bf16[8,24,3072]{2,1,0:T(8,128)(2,1)S(1)} async-done(((bf16[8,24,3072]{2,1,0:T(8,128)(2,1)}), bf16[8,24,3072]{2,1,0:T(8,128)(2,1)S(1)}, u32[]{:S(2)}, u32[]{:S(2)}) %all-to-all-start) | async-done | bytes 1179680 | tf_op jit(solution)/shard_map/all_to_all | solution.py:20
  51.2 2.7 %shard_map.84 = bf16[8,160,1280]{2,1,0:T(8,128)(2,1)} custom-call(bf16[192,3072]{1,0:T(8,128)(2,1)S(1)} %bitcast.36), custom_call_target="tpu_custom_call" | custom-call | flops 524288000 | bytes 8388608 | tf_op jit(solution)/shard_map/pallas_call | solution.py:81
  53.9 4.9 %all-to-all-start.1 = ((bf16[8,160,1280]{2,1,0:T(8,128)(2,1)}), bf16[8,160,1280]{2,1,0:T(8,128)(2,1)}, u32[]{:S(2)}, u32[]{:S(2)}) async-start(bf16[8,160,1280]{2,1,0:T(8,128)(2,1)} %shard_map.84), calls=%async_computation.1 | async-start | bytes 6553600 | tf_op jit(solution)/shard_map/all_to_all | solution.py:20
  58.8 0.0 all-gather.2.cloned.1.call-start
  58.8 15.1 %collective-permute-start.1 = (bf16[64,2048]{1,0:T(8,128)(2,1)S(1)}, bf16[64,2048]{1,0:T(8,128)(2,1)S(1)}, u32[]{:S(2)}, u32[]{:S(2)}) collective-permute-start(bf16[64,2048]{1,0:T(8,128)(2,1)S(1)} %collective-permute-done), channel_id=1, source_target_pairs={{0,128},{128,0},{1,129},{129,1},{2,130},{130,2},{3,131},{131,3},{4... | collective-permute-start | bytes 786440 | tf_op jit(solution)/shard_map/ppermute | solution.py:77
  73.9 6.6 %collective-permute-done.1 = bf16[64,2048]{1,0:T(8,128)(2,1)S(1)} collective-permute-done((bf16[64,2048]{1,0:T(8,128)(2,1)S(1)}, bf16[64,2048]{1,0:T(8,128)(2,1)S(1)}, u32[]{:S(2)}, u32[]{:S(2)}) %collective-permute-start.1) | collective-permute-done | bytes 262176 | tf_op jit(solution)/shard_map/ppermute | solution.py:77
  80.5 16.1 %all-to-all-done.1 = bf16[8,160,1280]{2,1,0:T(8,128)(2,1)} async-done(((bf16[8,160,1280]{2,1,0:T(8,128)(2,1)}), bf16[8,160,1280]{2,1,0:T(8,128)(2,1)}, u32[]{:S(2)}, u32[]{:S(2)}) %all-to-all-start.1) | async-done | bytes 3276832 | tf_op jit(solution)/shard_map/all_to_all | solution.py:20
  96.7 0.8 pad_maximum_fusion.2
  97.5 0.0 all-gather.2.cloned.1.call-update
  97.6 1.8 broadcast_select_fusion.1
  99.4 4.3 %fusion.12 = bf16[512,1024]{1,0:T(8,128)(2,1)} fusion(bf16[1280,1280]{1,0:T(8,128)(2,1)} %bitcast.6, bf16[1280,256]{1,0:T(8,128)(2,1)S(1)} %get-tuple-element.19, bf16[1280,256]{1,0:T(8,128)(2,1)S(1)} %get-tuple-element.18), kind=kOutput, calls=%fused_computation.11 | convolution fusion | flops 1345323008 | bytes 4980736 | tf_op jit(solution)/shard_map/dot_general | solution.py:24
  103.7 23.7 %all-to-all-start.2 = ((bf16[32,16,1024]{2,1,0:T(8,128)(2,1)}), bf16[32,16,1024]{2,1,0:T(8,128)(2,1)S(1)}, u32[]{:S(2)}, u32[]{:S(2)}) async-start(bf16[32,16,1024]{2,1,0:T(8,128)(2,1)} %bitcast.10), calls=%async_computation.2 | async-start | bytes 2097152 | tf_op jit(solution)/shard_map/all_to_all | solution.py:20
  127.4 23.0 %all-gather.2.cloned.1.call-done = bf16[2,512,2048]{2,1,0:T(8,128)(2,1)} async-done(((bf16[2,64,2048]{2,1,0:T(8,128)(2,1)}), bf16[2,512,2048]{2,1,0:T(8,128)(2,1)}) %all-gather.2.cloned.1.call-update) | async-done | bytes 4194320 | tf_op jit(solution)/shard_map/all_gather | solution.py:98
  150.4 0.0 copy-start.1
  150.4 3.3 %convolution_convert_fusion = bf16[192,2048]{1,0:T(8,128)(2,1)S(1)} fusion(bf16[1024,2048]{1,0:T(8,128)(2,1)} %bitcast.41, bf16[192,3072]{1,0:T(8,128)(2,1)S(1)} %bitcast.37), kind=kOutput, calls=%fused_computation.7 | convolution fusion | flops 805699584 | bytes 5373952 | tf_op jit(solution)/shard_map/dot_general | solution.py:24
  153.8 0.1 copy-done.1
  153.9 0.0 copy-start.3
  153.9 1.5 convolution_convert_fusion.2
  155.4 0.6 copy-done.3
  156.1 1.0 fusion.9
  157.1 1.5 fusion.21
  158.6 1.1 pad_maximum_fusion.1
  159.8 0.0 copy-start.2
  159.8 0.0 copy-start.4
  159.8 23.7 %all-to-all-done.2 = bf16[32,16,1024]{2,1,0:T(8,128)(2,1)S(1)} async-done(((bf16[32,16,1024]{2,1,0:T(8,128)(2,1)}), bf16[32,16,1024]{2,1,0:T(8,128)(2,1)S(1)}, u32[]{:S(2)}, u32[]{:S(2)}) %all-to-all-start.2) | async-done | bytes 1048608 | tf_op jit(solution)/shard_map/all_to_all | solution.py:20
  183.4 6.9 %all-to-all-start.3 = ((bf16[8,24,3072]{2,1,0:T(8,128)(2,1)}), bf16[8,24,3072]{2,1,0:T(8,128)(2,1)S(1)}, u32[]{:S(2)}, u32[]{:S(2)}) async-start(bf16[8,24,3072]{2,1,0:T(8,128)(2,1)} %bitcast.11), calls=%async_computation.3 | async-start | bytes 2359296 | tf_op jit(solution)/shard_map/all_to_all | solution.py:20
  190.3 0.2 convert_reduce_fusion
  190.5 0.1 copy.9
  190.7 0.8 broadcast_in_dim_reshape.3
  191.4 30.7 %all-to-all-done.3 = bf16[8,24,3072]{2,1,0:T(8,128)(2,1)S(1)} async-done(((bf16[8,24,3072]{2,1,0:T(8,128)(2,1)}), bf16[8,24,3072]{2,1,0:T(8,128)(2,1)S(1)}, u32[]{:S(2)}, u32[]{:S(2)}) %all-to-all-start.3) | async-done | bytes 1179680 | tf_op jit(solution)/shard_map/all_to_all | solution.py:20
  222.1 0.0 copy-done.2
  222.1 0.0 copy-done.4
  222.1 1.8 fusion.25
  223.9 1.0 convolution_convert_fusion.4
  (3 shorter events, 0.1 us)
Async XLA Ops:
  7.2 2.5 %copy-start = (bf16[128,1024]{1,0:T(8,128)(2,1)S(1)}, bf16[128,1024]{1,0:T(8,128)(2,1)}, u32[]{:S(2)}) copy-start(bf16[128,1024]{1,0:T(8,128)(2,1)} %param.5) | copy-start | bytes 786436
  12.5 38.7 %all-to-all-start = ((bf16[8,24,3072]{2,1,0:T(8,128)(2,1)}), bf16[8,24,3072]{2,1,0:T(8,128)(2,1)S(1)}, u32[]{:S(2)}, u32[]{:S(2)}) async-start(bf16[8,24,3072]{2,1,0:T(8,128)(2,1)} %bitcast.2), calls=%async_computation | async-start | bytes 2359296 | tf_op jit(solution)/shard_map/all_to_all | solution.py:20
  20.6 25.7 %collective-permute-start = (bf16[64,2048]{1,0:T(8,128)(2,1)S(1)}, bf16[64,2048]{1,0:T(8,128)(2,1)S(1)}, u32[]{:S(2)}, u32[]{:S(2)}) collective-permute-start(bf16[64,2048]{1,0:T(8,128)(2,1)S(1)} %dynamic-slice_bitcast_fusion), channel_id=1, source_target_pairs={{0,1},{1,0},{2,3},{3,2},{4,5},{5,4},{6,7},{7,6},{8,9},{9,8},{10,11... | collective-permute-start | bytes 786440 | tf_op jit(solution)/shard_map/ppermute | solution.py:64
  53.9 42.7 %all-to-all-start.1 = ((bf16[8,160,1280]{2,1,0:T(8,128)(2,1)}), bf16[8,160,1280]{2,1,0:T(8,128)(2,1)}, u32[]{:S(2)}, u32[]{:S(2)}) async-start(bf16[8,160,1280]{2,1,0:T(8,128)(2,1)} %shard_map.84), calls=%async_computation.1 | async-start | bytes 6553600 | tf_op jit(solution)/shard_map/all_to_all | solution.py:20
  58.8 91.6 %all-gather.2.cloned.1.call-start = ((), (), s32[]{:S(2)}) async-start(), calls=%async_computation.4 | async-start | bytes 4718592 | tf_op jit(solution)/shard_map/all_gather | solution.py:98
  58.8 21.7 %collective-permute-start.1 = (bf16[64,2048]{1,0:T(8,128)(2,1)S(1)}, bf16[64,2048]{1,0:T(8,128)(2,1)S(1)}, u32[]{:S(2)}, u32[]{:S(2)}) collective-permute-start(bf16[64,2048]{1,0:T(8,128)(2,1)S(1)} %collective-permute-done), channel_id=1, source_target_pairs={{0,128},{128,0},{1,129},{129,1},{2,130},{130,2},{3,131},{131,3},{4... | collective-permute-start | bytes 786440 | tf_op jit(solution)/shard_map/ppermute | solution.py:77
  103.7 79.7 %all-to-all-start.2 = ((bf16[32,16,1024]{2,1,0:T(8,128)(2,1)}), bf16[32,16,1024]{2,1,0:T(8,128)(2,1)S(1)}, u32[]{:S(2)}, u32[]{:S(2)}) async-start(bf16[32,16,1024]{2,1,0:T(8,128)(2,1)} %bitcast.10), calls=%async_computation.2 | async-start | bytes 2097152 | tf_op jit(solution)/shard_map/all_to_all | solution.py:20
  150.4 3.4 %copy-start.1 = (bf16[2,512,2048]{2,1,0:T(8,128)(2,1)S(1)}, bf16[2,512,2048]{2,1,0:T(8,128)(2,1)}, u32[]{:S(2)}) copy-start(bf16[2,512,2048]{2,1,0:T(8,128)(2,1)} %all-gather.2.cloned.1.call-done) | copy-start | bytes 12582916
  153.9 2.2 copy-start.3
  159.8 62.4 %copy-start.2 = (bf16[128,2048]{1,0:T(8,128)(2,1)S(1)}, bf16[128,2048]{1,0:T(8,128)(2,1)}, u32[]{:S(2)}) copy-start(bf16[128,2048]{1,0:T(8,128)(2,1)} %param.9) | copy-start | bytes 1572868
  159.8 62.4 %copy-start.4 = (f32[128,1]{0,1:T(1,128)S(1)}, f32[128,1]{0,1:T(1,128)}, u32[]{:S(2)}) copy-start(f32[128,1]{0,1:T(1,128)} %param.7) | copy-start | bytes 1540
  183.4 38.7 %all-to-all-start.3 = ((bf16[8,24,3072]{2,1,0:T(8,128)(2,1)}), bf16[8,24,3072]{2,1,0:T(8,128)(2,1)S(1)}, u32[]{:S(2)}, u32[]{:S(2)}) async-start(bf16[8,24,3072]{2,1,0:T(8,128)(2,1)} %bitcast.11), calls=%async_computation.3 | async-start | bytes 2359296 | tf_op jit(solution)/shard_map/all_to_all | solution.py:20
Sparse Core Ops, SparseCore 0:
  97.7 52.7 all-gather.1

commit v8 on v7

--- a/solution.py
+++ b/solution.py
@@ -13,7 +13,7 @@
 EXP = ("y", "zh")
 NEAR = ("x", "c")
 SHARE = ("zp", "x", "c")
-RING = ("zh",) + LINE + ("c",)
+RING = ("zh",) + LINE
 
 
 def exchange(blocks, axes):
@@ -102,27 +102,58 @@
     by_half = jnp.concatenate(
         [jnp.where(of_half == h, hid_near, zero) for h in range(halves)], axis=1
     )
-    partial_grad = dot(by_half, grad_near, ((0,), (0,)))
-    parts = exchange(partial_grad.reshape(-1, strip, out_width // cs), RING)
+    partial_grad = dot(by_half, grad_near, ((0,), (0,)), F32)
+    ring_sum = lax.psum_scatter(partial_grad, RING, scatter_dimension=0, tiled=True)
 
-    grad_flat, hid_flat = arrived[:, :out_width], arrived[:, out_width:]
-    own = (jnp.arange(tall, dtype=I32) // slots % halves)[:, None] == half
-    proj = jnp.where(
-        own, dot(hid_flat, weight, ((1,), (0,))), dot(hid_flat, other_weight, ((1,), (0,)))
-    )
-    back = jnp.where(
-        own, dot(grad_flat, weight, ((1,), (1,))), dot(grad_flat, other_weight, ((1,), (1,)))
-    )
-    leaving = jnp.concatenate([proj, back], axis=1)
-    leaving, parts = lax.optimization_barrier((leaving, parts))
-    returned = exchange(leaving.reshape(columns, block, -1), "y").reshape(tall, -1)
-    projected = dot(placer, returned[:, :out_width], ((0,), (0,)), F32)
+    full = jnp.arange(columns * capacity, dtype=I32)
+    origin, rank = full // capacity, full % capacity
+    odd = (rank % 2 == 1)[:, None]
+    back_block = 16 * (-(-(capacity + (capacity + 1) // 2) // 16))
+    short = columns * back_block
+
+    def products(which, matrix, arrived):
+        wanted = origin * block + which * slots + rank
+        chosen = (wanted[:, None] == jnp.arange(tall, dtype=I32)[None, :]).astype(BF16)
+        picked = dot(chosen, arrived, ((1,), (0,)))
+        proj = dot(picked[:, out_width:], matrix, ((1,), (0,)))
+        back = dot(picked[:, :out_width], matrix, ((1,), (1,)))
+        zero = jnp.zeros((), BF16)
+        pairs = jnp.concatenate(
+            [jnp.where(odd, zero, back), jnp.where(odd, back, zero)], axis=1
+        )
+        spots = origin * back_block
+        spots = jnp.concatenate([spots + rank, spots + capacity + rank // 2])
+        spread = (jnp.arange(short, dtype=I32)[:, None] == spots[None, :]).astype(BF16)
+        return dot(spread, jnp.concatenate([proj, pairs], axis=0), ((1,), (0,)))
+
+    own_leaving, _ = lax.optimization_barrier((products(half, weight, arrived), partial_grad))
+    own_back = exchange(own_leaving.reshape(columns, back_block, -1), "y").reshape(short, -1)
+    arrived, own_back = lax.optimization_barrier((arrived, own_back))
+    other_leaving = products(1 - half, other_weight, arrived)
+    other_back = exchange(other_leaving.reshape(columns, back_block, -1), "y")
+    other_back, ring_sum = lax.optimization_barrier((other_back.reshape(short, -1), ring_sum))
+    returned = jnp.concatenate([own_back, other_back], axis=0)
+    seat = jnp.where(expert_list % halves == half, 0, short) + expert_list // halves * back_block
+    seats = jnp.concatenate([seat + row_rank, seat + capacity + row_rank // 2])
+    fetcher = (jnp.arange(2 * short, dtype=I32)[:, None] == seats[None, :]).astype(BF16)
+    fetched = dot(fetcher, returned, ((0,), (0,)), F32)
+    projected = fetched[:tok_rows]
+    hidden_grad = jnp.where(
+        (row_rank % 2 == 1)[:, None],
+        fetched[tok_rows:, hid_width:],
+        fetched[tok_rows:, :hid_width],
+    ).astype(BF16)
     layer_out = (gate_weights * projected).astype(BF16)
     gate_grad = jnp.sum(out_grad.astype(F32) * projected, axis=1, keepdims=True)
-    hidden_grad = dot(placer, returned[:, out_width:], ((0,), (0,)))
 
-    summed = jnp.sum(parts.reshape(-1, cs, strip, out_width // cs).astype(F32), axis=0)
-    weight_grad = summed.swapaxes(0, 1).reshape(strip, out_width)
+    core = lax.axis_index("c")
+    first = core == 0
+    kept = lax.dynamic_slice_in_dim(ring_sum, core * strip, strip, axis=0)
+    given = lax.dynamic_slice_in_dim(ring_sum, (1 - core) * strip, strip, axis=0)
+    taken = lax.ppermute(given, "c", [(0, 1), (1, 0)])
+    weight_grad = jnp.concatenate(
+        [jnp.where(first, kept, taken), jnp.where(first, taken, kept)], axis=1
+    )
     return (layer_out, hidden_grad, gate_grad, weight_grad[None])
 
 

time: 235 us -> 210 us (0.89)
  waiting for transfers between devices: 111 us -> 84 us
  starting transfers between devices: 77.1 us -> 55.3 us
  blocking collectives: 0 us -> 20 us
    all_to_all x4 -> x3, waiting for transfers between devices: 75.4 us -> 21 us  [exchange(): return lax.all_to_all(blocks, axes, split_axis=0, concat_axis=0, tiled=True)]
    reduce_scatter x0 -> x1, waiting for transfers between devices: none -> 29.9 us  [shards(): lax.psum_scatter(partial_grad, RING, scatter_dimension=0, tiled=True)]
    all_to_all x4 -> x3, starting transfers between devices: 42.6 us -> 18.8 us  [exchange(): return lax.all_to_all(blocks, axes, split_axis=0, concat_axis=0, tiled=True)]
    all_to_all x0 -> x1, blocking collectives: none -> 20 us  [exchange(): return lax.all_to_all(blocks, axes, split_axis=0, concat_axis=0, tiled=True)]
    all_gather x1, waiting for transfers between devices: 23 us -> 20.2 us  [shards(): lax.all_gather(pair, NEAR, axis=1, tiled=True).reshape(hid_width, -1)]
    dot_general x9 -> x12, matrix products: 16.2 us -> 18.3 us  [dot(): lax.dot_general(a, b, (dims, ((), ())), preferred_element_type=F32)]
  transfers between devices with their start and end apart: 7 -> 8, of which waited for: 7 -> 6; matrix products, arithmetic and copies ran while one was open for 7% -> 11% of each run, Pallas kernels for 0% -> 0%
where the time goes in v8:
time: 210 us; the launch traced here: 208 us
  waiting for transfers between devices  84 us (40%)
  starting transfers between devices  55.3 us (26%)
  blocking collectives  20 us (10%)
  matrix products  18.3 us (9%)
  between operations  15.7 us (7%)
  other arithmetic  9.5 us (5%)
  local copies, waits for them, and re-layouts  4.03 us (2%)
    reduce_scatter x1, waiting for transfers between devices, shards(): lax.psum_scatter(partial_grad, RING, scatter_dimension=0, tiled=True)  29.9 us
    all_to_all x3, waiting for transfers between devices, exchange(): return lax.all_to_all(blocks, axes, split_axis=0, concat_axis=0, tiled=True)  21 us
    all_gather x1, waiting for transfers between devices, shards(): lax.all_gather(pair, NEAR, axis=1, tiled=True).reshape(hid_width, -1)  20.2 us
    all_to_all x1, blocking collectives, exchange(): return lax.all_to_all(blocks, axes, split_axis=0, concat_axis=0, tiled=True)  20 us
    ppermute x1, starting transfers between devices, shards(): share = lax.ppermute(share, 'zh', [(0, 1), (1, 0)])  19.4 us
    all_to_all x3, starting transfers between devices, exchange(): return lax.all_to_all(blocks, axes, split_axis=0, concat_axis=0, tiled=True)  18.8 us
    dot_general x12, matrix products, dot(): lax.dot_general(a, b, (dims, ((), ())), preferred_element_type=F32)  18.3 us
    ppermute x1, starting transfers between devices, shards(): beside = lax.ppermute(share, 'zp', [(0, 1), (1, 0)])  15.1 us
  transfers between devices with their start and end apart: 8, of which 6 were waited for; matrix products, arithmetic and copies ran while one was open for 11% of the time, Pallas kernels for 0%

profile of v8, /device:TPU:6, one launch (start us, length us, event | category | flops | bytes accessed | tf_op | source)
XLA Modules:
  0.0 207.8 jit_solution(10761717829948162176)
XLA Ops:
  8.0 0.0 copy-start
  8.0 0.8 fusion.41
  8.8 0.2 reduce_window_sum.11
  9.0 0.8 select_reduce_fusion
  9.8 0.7 fusion.57
  10.5 0.0 copy-done
  10.5 0.3 convolution_convert_fusion.6
  10.8 1.5 convolution_convert_fusion.2
  12.3 1.1 pad_maximum_fusion
  13.4 7.1 %all-to-all-start = ((bf16[8,24,3072]{2,1,0:T(8,128)(2,1)}), bf16[8,24,3072]{2,1,0:T(8,128)(2,1)S(1)}, u32[]{:S(2)}, u32[]{:S(2)}) async-start(bf16[8,24,3072]{2,1,0:T(8,128)(2,1)} %bitcast.2), calls=%async_computation | async-start | bytes 2359296 | tf_op jit(solution)/shard_map/all_to_all | solution.py:20
  20.5 1.0 dynamic-slice_bitcast_fusion
  21.5 19.4 %collective-permute-start = (bf16[64,2048]{1,0:T(8,128)(2,1)S(1)}, bf16[64,2048]{1,0:T(8,128)(2,1)S(1)}, u32[]{:S(2)}, u32[]{:S(2)}) collective-permute-start(bf16[64,2048]{1,0:T(8,128)(2,1)S(1)} %dynamic-slice_bitcast_fusion), channel_id=1, source_target_pairs={{0,1},{1,0},{2,3},{3,2},{4,5},{5,4},{6,7},{7,6},{8,9},{9,8},{10,11... | collective-permute-start | bytes 786440 | tf_op jit(solution)/shard_map/ppermute | solution.py:64
  40.8 6.3 %collective-permute-done = bf16[64,2048]{1,0:T(8,128)(2,1)S(1)} collective-permute-done((bf16[64,2048]{1,0:T(8,128)(2,1)S(1)}, bf16[64,2048]{1,0:T(8,128)(2,1)S(1)}, u32[]{:S(2)}, u32[]{:S(2)}) %collective-permute-start) | collective-permute-done | bytes 262176 | tf_op jit(solution)/shard_map/ppermute | solution.py:64
  47.1 4.9 %all-to-all-done = bf16[8,24,3072]{2,1,0:T(8,128)(2,1)S(1)} async-done(((bf16[8,24,3072]{2,1,0:T(8,128)(2,1)}), bf16[8,24,3072]{2,1,0:T(8,128)(2,1)S(1)}, u32[]{:S(2)}, u32[]{:S(2)}) %all-to-all-start) | async-done | bytes 1179680 | tf_op jit(solution)/shard_map/all_to_all | solution.py:20
  52.1 1.0 shard_map.84
  53.1 0.0 copy-start.1
  53.1 1.7 copy-done.1
  54.8 4.9 %all-to-all-start.1 = ((bf16[8,160,1280]{2,1,0:T(8,128)(2,1)}), bf16[8,160,1280]{2,1,0:T(8,128)(2,1)}, u32[]{:S(2)}, u32[]{:S(2)}) async-start(bf16[8,160,1280]{2,1,0:T(8,128)(2,1)} %copy-done.1), calls=%async_computation.1 | async-start | bytes 6553600 | tf_op jit(solution)/shard_map/all_to_all | solution.py:20
  59.7 0.0 all-gather.2.cloned.1.call-start
  59.7 15.1 %collective-permute-start.1 = (bf16[64,2048]{1,0:T(8,128)(2,1)S(1)}, bf16[64,2048]{1,0:T(8,128)(2,1)S(1)}, u32[]{:S(2)}, u32[]{:S(2)}) collective-permute-start(bf16[64,2048]{1,0:T(8,128)(2,1)S(1)} %collective-permute-done), channel_id=1, source_target_pairs={{0,128},{128,0},{1,129},{129,1},{2,130},{130,2},{3,131},{131,3},{4... | collective-permute-start | bytes 786440 | tf_op jit(solution)/shard_map/ppermute | solution.py:77
  74.8 6.6 %collective-permute-done.1 = bf16[64,2048]{1,0:T(8,128)(2,1)S(1)} collective-permute-done((bf16[64,2048]{1,0:T(8,128)(2,1)S(1)}, bf16[64,2048]{1,0:T(8,128)(2,1)S(1)}, u32[]{:S(2)}, u32[]{:S(2)}) %collective-permute-start.1) | collective-permute-done | bytes 262176 | tf_op jit(solution)/shard_map/ppermute | solution.py:77
  81.4 16.1 %all-to-all-done.1 = bf16[8,160,1280]{2,1,0:T(8,128)(2,1)} async-done(((bf16[8,160,1280]{2,1,0:T(8,128)(2,1)}), bf16[8,160,1280]{2,1,0:T(8,128)(2,1)}, u32[]{:S(2)}, u32[]{:S(2)}) %all-to-all-start.1) | async-done | bytes 3276832 | tf_op jit(solution)/shard_map/all_to_all | solution.py:20
  97.6 0.8 pad_maximum_fusion.1
  98.4 0.0 all-gather.2.cloned.1.call-update
  98.4 0.0 reduce-scatter.2.cloned.1.call-start
  98.6 0.1 pad_add_fusion.1
  98.7 1.8 broadcast_select_fusion.1
  100.5 4.7 %fusion.4 = f32[512,1024]{1,0:T(8,128)} fusion(bf16[1280,1280]{1,0:T(8,128)(2,1)} %bitcast.6, bf16[1280,256]{1,0:T(8,128)(2,1)S(1)} %get-tuple-element.27, bf16[1280,256]{1,0:T(8,128)(2,1)S(1)} %get-tuple-element.26), kind=kOutput, calls=%fused_computation.6 | convolution fusion | flops 1344798720 | bytes 6029312 | tf_op jit(solution)/shard_map/dot_general | solution.py:24
  105.2 0.0 reduce-scatter.2.cloned.1.call-update
  105.3 0.4 convolution_convert_fusion.1
  105.6 0.0 copy-start.2
  105.6 3.2 %fusion.6 = bf16[80,2048]{1,0:T(8,128)(2,1)S(1)} fusion(bf16[1,1024,2048]{2,1,0:T(8,128)(2,1)} %param.8, bf16[80,3072]{1,0:T(8,128)(2,1)S(1)} %convolution_convert_fusion.1), kind=kOutput, calls=%fused_computation.11 | convolution fusion | flops 335708160 | bytes 4685824 | tf_op jit(solution)/shard_map/dot_general | solution.py:24
  108.8 0.2 copy-done.2
  109.1 1.4 broadcast_select_fusion.5
  110.5 0.3 convolution_convert_fusion.4
  110.8 20.0 %all_to_all.20 = bf16[8,16,2048]{2,1,0:T(8,128)(2,1)S(1)} all-to-all(bf16[8,16,2048]{2,1,0:T(8,128)(2,1)S(1)} %bitcast.45), channel_id=1, replica_groups=mesh['zq'=4,'zp'=2,'x'=4,'c'=2,'y'=8,'zh'=2] {'y'}, dimensions={0} | all-to-all | bytes 1048576 | tf_op jit(solution)/shard_map/all_to_all | solution.py:20
  130.8 0.4 convolution_convert_fusion
  131.1 20.2 %all-gather.2.cloned.1.call-done = bf16[2,512,2048]{2,1,0:T(8,128)(2,1)} async-done(((bf16[2,64,2048]{2,1,0:T(8,128)(2,1)}), bf16[2,512,2048]{2,1,0:T(8,128)(2,1)}) %all-gather.2.cloned.1.call-update) | async-done | bytes 4194320 | tf_op jit(solution)/shard_map/all_gather | solution.py:98
  151.3 0.0 copy-start.3
  151.3 3.2 %convolution_convert_fusion.5 = bf16[80,2048]{1,0:T(8,128)(2,1)S(1)} fusion(bf16[1024,2048]{1,0:T(8,128)(2,1)} %bitcast.41, bf16[80,3072]{1,0:T(8,128)(2,1)S(1)} %convolution_convert_fusion), kind=kOutput, calls=%fused_computation.12 | convolution fusion | flops 335708160 | bytes 4685824 | tf_op jit(solution)/shard_map/dot_general | solution.py:24
  154.5 0.3 copy-done.3
  154.8 1.4 broadcast_select_fusion.3
  156.2 1.1 convolution_convert_fusion.3
  157.3 0.0 copy-start.4
  157.3 0.0 copy-start.6
  157.3 6.9 %all-to-all-start.3 = ((bf16[8,16,2048]{2,1,0:T(8,128)(2,1)}), bf16[8,16,2048]{2,1,0:T(8,128)(2,1)S(1)}, u32[]{:S(2)}, u32[]{:S(2)}) async-start(bf16[8,16,2048]{2,1,0:T(8,128)(2,1)} %bitcast.12), calls=%async_computation.3 | async-start | bytes 1048576 | tf_op jit(solution)/shard_map/all_to_all | solution.py:20
  164.2 29.9 %reduce-scatter.2.cloned.1.call-done = f32[32,1024]{1,0:T(8,128)} async-done(((f32[512,1024]{1,0:T(8,128)}), f32[32,1024]{1,0:T(8,128)}) %reduce-scatter.2.cloned.1.call-update) | async-done | bytes 131088 | tf_op jit(solution)/shard_map/reduce_scatter | solution.py:106
  194.1 0.0 all-to-all-done.3
  194.1 0.8 constant_dynamic-slice_fusion
  194.9 1.9 collective-permute-start.2
  196.9 0.5 fusion.17
  197.4 0.0 copy-done.4
  197.4 0.0 copy-done.6
  197.4 0.0 copy-start.5
  197.4 1.5 fusion.16
  198.8 0.9 fusion.32
  199.7 0.0 collective-permute-done.2
  199.7 0.0 copy-done.5
  199.7 0.7 maximum_bitcast_fusion
  (10 shorter events, 0.2 us)
Async XLA Ops:
  8.0 2.5 %copy-start = (bf16[128,1024]{1,0:T(8,128)(2,1)S(1)}, bf16[128,1024]{1,0:T(8,128)(2,1)}, u32[]{:S(2)}) copy-start(bf16[128,1024]{1,0:T(8,128)(2,1)} %param.5) | copy-start | bytes 786436
  13.4 38.7 %all-to-all-start = ((bf16[8,24,3072]{2,1,0:T(8,128)(2,1)}), bf16[8,24,3072]{2,1,0:T(8,128)(2,1)S(1)}, u32[]{:S(2)}, u32[]{:S(2)}) async-start(bf16[8,24,3072]{2,1,0:T(8,128)(2,1)} %bitcast.2), calls=%async_computation | async-start | bytes 2359296 | tf_op jit(solution)/shard_map/all_to_all | solution.py:20
  21.5 25.7 %collective-permute-start = (bf16[64,2048]{1,0:T(8,128)(2,1)S(1)}, bf16[64,2048]{1,0:T(8,128)(2,1)S(1)}, u32[]{:S(2)}, u32[]{:S(2)}) collective-permute-start(bf16[64,2048]{1,0:T(8,128)(2,1)S(1)} %dynamic-slice_bitcast_fusion), channel_id=1, source_target_pairs={{0,1},{1,0},{2,3},{3,2},{4,5},{5,4},{6,7},{7,6},{8,9},{9,8},{10,11... | collective-permute-start | bytes 786440 | tf_op jit(solution)/shard_map/ppermute | solution.py:64
  53.1 1.7 copy-start.1
  54.8 42.7 %all-to-all-start.1 = ((bf16[8,160,1280]{2,1,0:T(8,128)(2,1)}), bf16[8,160,1280]{2,1,0:T(8,128)(2,1)}, u32[]{:S(2)}, u32[]{:S(2)}) async-start(bf16[8,160,1280]{2,1,0:T(8,128)(2,1)} %copy-done.1), calls=%async_computation.1 | async-start | bytes 6553600 | tf_op jit(solution)/shard_map/all_to_all | solution.py:20
  59.7 91.6 %all-gather.2.cloned.1.call-start = ((), (), s32[]{:S(2)}) async-start(), calls=%async_computation.5 | async-start | bytes 4718592 | tf_op jit(solution)/shard_map/all_gather | solution.py:98
  59.7 21.7 %collective-permute-start.1 = (bf16[64,2048]{1,0:T(8,128)(2,1)S(1)}, bf16[64,2048]{1,0:T(8,128)(2,1)S(1)}, u32[]{:S(2)}, u32[]{:S(2)}) collective-permute-start(bf16[64,2048]{1,0:T(8,128)(2,1)S(1)} %collective-permute-done), channel_id=1, source_target_pairs={{0,128},{128,0},{1,129},{129,1},{2,130},{130,2},{3,131},{131,3},{4... | collective-permute-start | bytes 786440 | tf_op jit(solution)/shard_map/ppermute | solution.py:77
  98.4 95.7 %reduce-scatter.2.cloned.1.call-start = ((), (), s32[]{:S(2)}) async-start(), calls=%async_computation.6 | async-start | bytes 2228224 | tf_op jit(solution)/shard_map/reduce_scatter | solution.py:106
  105.6 3.5 %copy-start.2 = (bf16[1,1024,2048]{2,1,0:T(8,128)(2,1)S(1)}, bf16[1,1024,2048]{2,1,0:T(8,128)(2,1)}, u32[]{:S(2)}) copy-start(bf16[1,1024,2048]{2,1,0:T(8,128)(2,1)} %param.8) | copy-start | bytes 12582916
  151.3 3.5 %copy-start.3 = (bf16[2,512,2048]{2,1,0:T(8,128)(2,1)S(1)}, bf16[2,512,2048]{2,1,0:T(8,128)(2,1)}, u32[]{:S(2)}) copy-start(bf16[2,512,2048]{2,1,0:T(8,128)(2,1)} %all-gather.2.cloned.1.call-done) | copy-start | bytes 12582916
  157.3 40.1 %copy-start.4 = (bf16[128,2048]{1,0:T(8,128)(2,1)S(1)}, bf16[128,2048]{1,0:T(8,128)(2,1)}, u32[]{:S(2)}) copy-start(bf16[128,2048]{1,0:T(8,128)(2,1)} %param.9) | copy-start | bytes 1572868
  157.3 40.1 %copy-start.6 = (f32[128,1]{0,1:T(1,128)S(1)}, f32[128,1]{0,1:T(1,128)}, u32[]{:S(2)}) copy-start(f32[128,1]{0,1:T(1,128)} %param.7) | copy-start | bytes 1540
  157.3 36.8 %all-to-all-start.3 = ((bf16[8,16,2048]{2,1,0:T(8,128)(2,1)}), bf16[8,16,2048]{2,1,0:T(8,128)(2,1)S(1)}, u32[]{:S(2)}, u32[]{:S(2)}) async-start(bf16[8,16,2048]{2,1,0:T(8,128)(2,1)} %bitcast.12), calls=%async_computation.3 | async-start | bytes 1048576 | tf_op jit(solution)/shard_map/all_to_all | solution.py:20
  194.9 4.8 %collective-permute-start.2 = (f32[16,1024]{1,0:T(8,128)S(1)}, f32[16,1024]{1,0:T(8,128)S(1)}, u32[]{:S(2)}, u32[]{:S(2)}) collective-permute-start(f32[16,1024]{1,0:T(8,128)S(1)} %constant_dynamic-slice_fusion), channel_id=1, source_target_pairs={{0,16},{16,0},{1,17},{17,1},{2,18},{18,2},{3,19},{19,3},{4,20},{20... | collective-permute-start | bytes 196616 | tf_op jit(solution)/shard_map/ppermute | solution.py:153
  197.4 2.3 %copy-start.5 = (f32[32,1024]{1,0:T(8,128)S(1)}, f32[32,1024]{1,0:T(8,128)}, u32[]{:S(2)}) copy-start(f32[32,1024]{1,0:T(8,128)} %reduce-scatter.2.cloned.1.call-done) | copy-start | bytes 393220
Sparse Core Ops, SparseCore 0:
  98.6 52.7 all-gather.1
Sparse Core Ops, SparseCore 1:
  105.3 88.7 reduce-scatter.1

commit v9 on v8

--- a/solution.py
+++ b/solution.py
@@ -12,8 +12,9 @@
 DP = LINE + ("x", "c")
 EXP = ("y", "zh")
 NEAR = ("x", "c")
+GROUP = ("zp",) + NEAR
 SHARE = ("zp", "x", "c")
-RING = ("zh",) + LINE
+RING = ("zh", "zq")
 
 
 def exchange(blocks, axes):
@@ -24,11 +25,11 @@
     return lax.dot_general(a, b, (dims, ((), ())), preferred_element_type=F32).astype(out)
 
 
-def pack_kernel(capacity, slots, strip, xs, cs, hid_width, arrived, blocks):
+def pack_kernel(capacity, slots, strip, zs, xs, cs, hid_width, arrived, blocks):
     tall, width = arrived.shape
     rows = blocks.shape[1]
     quarter = hid_width // xs
-    half = (width - hid_width) // cs
+    part = (width - hid_width) // (zs * cs)
     full = lax.broadcasted_iota(I32, (rows, tall), 0)
     wanted = full // capacity * slots + full % capacity
     compact = (wanted == lax.broadcasted_iota(I32, (rows, tall), 1)).astype(BF16)
@@ -38,10 +39,12 @@
     target = place // group % xs * quarter + place // (group * xs) * group + place % group
     sorter = (target == lax.broadcasted_iota(I32, (hid_width, hid_width), 1)).astype(BF16)
     hid = dot(kept[:, width - hid_width :], sorter, ((1,), (0,)))
-    for x in range(xs):
-        for c in range(cs):
-            blocks[x * cs + c, :, :quarter] = hid[:, x * quarter : (x + 1) * quarter]
-            blocks[x * cs + c, :, quarter:] = kept[:, c * half : (c + 1) * half]
+    for z in range(zs):
+        for x in range(xs):
+            for c in range(cs):
+                block, wide = (z * xs + x) * cs + c, z * cs + c
+                blocks[block, :, :quarter] = hid[:, x * quarter : (x + 1) * quarter]
+                blocks[block, :, quarter:] = kept[:, wide * part : (wide + 1) * part]
 
 
 def shards(hidden, expert_ids, gate_weights, down_weight, out_grad):
@@ -49,7 +52,7 @@
     out_width = out_grad.shape[1]
     columns, halves = lax.axis_size("y"), lax.axis_size("zh")
     experts = columns * halves
-    xs, cs, near = (lax.axis_size(axes) for axes in ("x", "c", NEAR))
+    zs, xs, cs, group = (lax.axis_size(axes) for axes in ("zp", "x", "c", GROUP))
     capacity = 5 * tok_rows // (4 * experts)
     slots = capacity + -capacity % 4
     block = halves * slots
@@ -79,9 +82,9 @@
     rows = experts * capacity
     near_rows = exchange(
         pl.pallas_call(
-            functools.partial(pack_kernel, capacity, slots, strip, xs, cs, hid_width),
+            functools.partial(pack_kernel, capacity, slots, strip, zs, xs, cs, hid_width),
             out_shape=jax.ShapeDtypeStruct(
-                (near, rows, hid_width // xs + out_width // cs), BF16
+                (group, rows, hid_width // xs + out_width // (zs * cs)), BF16
             ),
             compiler_params=pltpu.CompilerParams(vmem_limit_bytes=40 * 2**20),
             cost_estimate=pl.CostEstimate(
@@ -90,14 +93,14 @@
                 transcendentals=0,
             ),
         )(arrived),
-        NEAR,
-    ).reshape(near * rows, -1)
+        GROUP,
+    ).reshape(group * rows, -1)
     near_rows, share, beside = lax.optimization_barrier((near_rows, share, beside))
     even = lax.axis_index("zp") == 0
     pair = jnp.stack([jnp.where(even, share, beside), jnp.where(even, beside, share)])
     other_weight = lax.all_gather(pair, NEAR, axis=1, tiled=True).reshape(hid_width, -1)
     hid_near, grad_near = near_rows[:, : hid_width // xs], near_rows[:, hid_width // xs :]
-    of_half = (jnp.arange(near * rows, dtype=I32) // capacity % halves)[:, None]
+    of_half = (jnp.arange(group * rows, dtype=I32) // capacity % halves)[:, None]
     zero = jnp.zeros((), BF16)
     by_half = jnp.concatenate(
         [jnp.where(of_half == h, hid_near, zero) for h in range(halves)], axis=1
@@ -130,11 +133,32 @@
     own_back = exchange(own_leaving.reshape(columns, back_block, -1), "y").reshape(short, -1)
     arrived, own_back = lax.optimization_barrier((arrived, own_back))
     other_leaving = products(1 - half, other_weight, arrived)
+    other_leaving, ring_sum = lax.optimization_barrier((other_leaving, ring_sum))
     other_back = exchange(other_leaving.reshape(columns, back_block, -1), "y")
-    other_back, ring_sum = lax.optimization_barrier((other_back.reshape(short, -1), ring_sum))
+    other_back = other_back.reshape(short, -1)
+
+    members = zs * cs
+    seat = lax.axis_index(("zp", "c"))
+    held = [
+        lax.dynamic_slice_in_dim(ring_sum, (seat ^ k) * strip, strip, axis=0)
+        for k in range(members)
+    ]
+    held = [held[0]] + [
+        lax.ppermute(held[k], ("zp", "c"), [(i, i ^ k) for i in range(members)])
+        for k in range(1, members)
+    ]
+    quarters = []
+    for p in range(members):
+        chosen = held[0]
+        for k in range(1, members):
+            chosen = jnp.where((seat ^ k) == p, held[k], chosen)
+        quarters.append(chosen)
+    weight_grad = jnp.concatenate(quarters, axis=1)
+    other_back, weight_grad = lax.optimization_barrier((other_back, weight_grad))
+
     returned = jnp.concatenate([own_back, other_back], axis=0)
-    seat = jnp.where(expert_list % halves == half, 0, short) + expert_list // halves * back_block
-    seats = jnp.concatenate([seat + row_rank, seat + capacity + row_rank // 2])
+    base = jnp.where(expert_list % halves == half, 0, short) + expert_list // halves * back_block
+    seats = jnp.concatenate([base + row_rank, base + capacity + row_rank // 2])
     fetcher = (jnp.arange(2 * short, dtype=I32)[:, None] == seats[None, :]).astype(BF16)
     fetched = dot(fetcher, returned, ((0,), (0,)), F32)
     projected = fetched[:tok_rows]
@@ -146,14 +170,6 @@
     layer_out = (gate_weights * projected).astype(BF16)
     gate_grad = jnp.sum(out_grad.astype(F32) * projected, axis=1, keepdims=True)
 
-    core = lax.axis_index("c")
-    first = core == 0
-    kept = lax.dynamic_slice_in_dim(ring_sum, core * strip, strip, axis=0)
-    given = lax.dynamic_slice_in_dim(ring_sum, (1 - core) * strip, strip, axis=0)
-    taken = lax.ppermute(given, "c", [(0, 1), (1, 0)])
-    weight_grad = jnp.concatenate(
-        [jnp.where(first, kept, taken), jnp.where(first, taken, kept)], axis=1
-    )
     return (layer_out, hidden_grad, gate_grad, weight_grad[None])
 
 

time: 210 us -> 249 us (1.19)
  waiting for transfers between devices: 84 us -> 129 us
  blocking collectives: 20 us -> 0 us
  starting transfers between devices: 55.3 us -> 67.6 us
    ppermute x1, waiting for transfers between devices: 6.6 us -> 48 us  [shards(): beside = lax.ppermute(share, 'zp', [(0, 1), (1, 0)])]
    all_to_all x1 -> x0, blocking collectives: 20 us -> none  [exchange(): return lax.all_to_all(blocks, axes, split_axis=0, concat_axis=0, tiled=True)]
    all_to_all x3 -> x4, starting transfers between devices: 18.8 us -> 37.2 us  [exchange(): return lax.all_to_all(blocks, axes, split_axis=0, concat_axis=0, tiled=True)]
    all_gather x1, waiting for transfers between devices: 20.2 us -> 5.21 us  [shards(): lax.all_gather(pair, NEAR, axis=1, tiled=True).reshape(hid_width, -1)]
    all_to_all x3 -> x4, waiting for transfers between devices: 21 us -> 33.6 us  [exchange(): return lax.all_to_all(blocks, axes, split_axis=0, concat_axis=0, tiled=True)]
    ppermute x1, starting transfers between devices: 15.1 us -> 3.38 us  [shards(): beside = lax.ppermute(share, 'zp', [(0, 1), (1, 0)])]
    ppermute x1 -> x3, starting transfers between devices: 1.91 us -> 7.57 us  [shards(): lax.ppermute(held[k], ('zp', 'c'), [(i, i ^ k) for i in range(members)])]
    reduce_scatter x1, waiting for transfers between devices: 29.9 us -> 34.9 us  [shards(): lax.psum_scatter(partial_grad, RING, scatter_dimension=0, tiled=True)]
  transfers between devices with their start and end apart: 8 -> 11, of which waited for: 6 -> 10; matrix products, arithmetic and copies ran while one was open for 11% -> 9% of each run, Pallas kernels for 0% -> 0%
where the time goes in v9:
time: 249 us; the launch traced here: 248 us
  waiting for transfers between devices  129 us (52%)
  starting transfers between devices  67.6 us (27%)
  matrix products  18.7 us (8%)
  between operations  15.8 us (6%)
  other arithmetic  11.7 us (5%)
  local copies, waits for them, and re-layouts  4.21 us (2%)
    ppermute x1, waiting for transfers between devices, shards(): beside = lax.ppermute(share, 'zp', [(0, 1), (1, 0)])  48 us
    all_to_all x4, starting transfers between devices, exchange(): return lax.all_to_all(blocks, axes, split_axis=0, concat_axis=0, tiled=True)  37.2 us
    reduce_scatter x1, waiting for transfers between devices, shards(): lax.psum_scatter(partial_grad, RING, scatter_dimension=0, tiled=True)  34.9 us
    all_to_all x4, waiting for transfers between devices, exchange(): return lax.all_to_all(blocks, axes, split_axis=0, concat_axis=0, tiled=True)  33.6 us
    ppermute x1, starting transfers between devices, shards(): share = lax.ppermute(share, 'zh', [(0, 1), (1, 0)])  19.4 us
    dot_general x12, matrix products, dot(): lax.dot_general(a, b, (dims, ((), ())), preferred_element_type=F32)  18.7 us
    ppermute x3, starting transfers between devices, shards(): lax.ppermute(held[k], ('zp', 'c'), [(i, i ^ k) for i in range(members)])  7.57 us
    ppermute x1, waiting for transfers between devices, shards(): share = lax.ppermute(share, 'zh', [(0, 1), (1, 0)])  6.3 us
  transfers between devices with their start and end apart: 11, of which 10 were waited for; matrix products, arithmetic and copies ran while one was open for 9% of the time, Pallas kernels for 0%

profile of v9, /device:TPU:6, one launch (start us, length us, event | category | flops | bytes accessed | tf_op | source)
XLA Modules:
  0.0 248.3 jit_solution(13603571982464277912)
XLA Ops:
  8.0 0.0 copy-start
  8.0 0.8 fusion.41
  8.8 0.2 reduce_window_sum.11
  9.0 0.8 select_reduce_fusion
  9.8 0.7 fusion.57
  10.5 0.0 copy-done
  10.5 0.3 convolution_convert_fusion.6
  10.8 1.5 convolution_convert_fusion.2
  12.3 1.1 pad_maximum_fusion
  13.4 7.1 %all-to-all-start = ((bf16[8,24,3072]{2,1,0:T(8,128)(2,1)}), bf16[8,24,3072]{2,1,0:T(8,128)(2,1)S(1)}, u32[]{:S(2)}, u32[]{:S(2)}) async-start(bf16[8,24,3072]{2,1,0:T(8,128)(2,1)} %bitcast.2), calls=%async_computation | async-start | bytes 2359296 | tf_op jit(solution)/shard_map/all_to_all | solution.py:21
  20.5 1.0 dynamic-slice_bitcast_fusion
  21.4 19.4 %collective-permute-start = (bf16[64,2048]{1,0:T(8,128)(2,1)S(1)}, bf16[64,2048]{1,0:T(8,128)(2,1)S(1)}, u32[]{:S(2)}, u32[]{:S(2)}) collective-permute-start(bf16[64,2048]{1,0:T(8,128)(2,1)S(1)} %dynamic-slice_bitcast_fusion), channel_id=1, source_target_pairs={{0,1},{1,0},{2,3},{3,2},{4,5},{5,4},{6,7},{7,6},{8,9},{9,8},{10,11... | collective-permute-start | bytes 786440 | tf_op jit(solution)/shard_map/ppermute | solution.py:67
  40.8 6.3 %collective-permute-done = bf16[64,2048]{1,0:T(8,128)(2,1)S(1)} collective-permute-done((bf16[64,2048]{1,0:T(8,128)(2,1)S(1)}, bf16[64,2048]{1,0:T(8,128)(2,1)S(1)}, u32[]{:S(2)}, u32[]{:S(2)}) %collective-permute-start) | collective-permute-done | bytes 262176 | tf_op jit(solution)/shard_map/ppermute | solution.py:67
  47.1 4.9 %all-to-all-done = bf16[8,24,3072]{2,1,0:T(8,128)(2,1)S(1)} async-done(((bf16[8,24,3072]{2,1,0:T(8,128)(2,1)}), bf16[8,24,3072]{2,1,0:T(8,128)(2,1)S(1)}, u32[]{:S(2)}, u32[]{:S(2)}) %all-to-all-start) | async-done | bytes 1179680 | tf_op jit(solution)/shard_map/all_to_all | solution.py:21
  52.1 1.0 shard_map.84
  53.1 0.0 copy-start.1
  53.1 1.9 copy-done.1
  55.0 17.5 %all-to-all-start.1 = ((bf16[16,160,768]{2,1,0:T(8,128)(2,1)}), bf16[16,160,768]{2,1,0:T(8,128)(2,1)}, u32[]{:S(2)}, u32[]{:S(2)}) async-start(bf16[16,160,768]{2,1,0:T(8,128)(2,1)} %copy-done.1), calls=%async_computation.1 | async-start | bytes 7864320 | tf_op jit(solution)/shard_map/all_to_all | solution.py:21
  72.5 0.0 all-gather.2.cloned.1.call-start
  72.5 3.4 %collective-permute-start.1 = (bf16[64,2048]{1,0:T(8,128)(2,1)S(1)}, bf16[64,2048]{1,0:T(8,128)(2,1)S(1)}, u32[]{:S(2)}, u32[]{:S(2)}) collective-permute-start(bf16[64,2048]{1,0:T(8,128)(2,1)S(1)} %collective-permute-done), channel_id=1, source_target_pairs={{0,128},{128,0},{1,129},{129,1},{2,130},{130,2},{3,131},{131,3},{4... | collective-permute-start | bytes 786440 | tf_op jit(solution)/shard_map/ppermute | solution.py:80
  75.9 48.0 %collective-permute-done.1 = bf16[64,2048]{1,0:T(8,128)(2,1)S(1)} collective-permute-done((bf16[64,2048]{1,0:T(8,128)(2,1)S(1)}, bf16[64,2048]{1,0:T(8,128)(2,1)S(1)}, u32[]{:S(2)}, u32[]{:S(2)}) %collective-permute-start.1) | collective-permute-done | bytes 262176 | tf_op jit(solution)/shard_map/ppermute | solution.py:80
  123.9 5.9 %all-to-all-done.1 = bf16[16,160,768]{2,1,0:T(8,128)(2,1)} async-done(((bf16[16,160,768]{2,1,0:T(8,128)(2,1)}), bf16[16,160,768]{2,1,0:T(8,128)(2,1)}, u32[]{:S(2)}, u32[]{:S(2)}) %all-to-all-start.1) | async-done | bytes 3932192 | tf_op jit(solution)/shard_map/all_to_all | solution.py:21
  129.9 0.8 pad_maximum_fusion.1
  130.7 0.0 all-gather.2.cloned.1.call-update
  130.8 0.1 pad_add_fusion.1
  130.9 0.4 convolution_convert_fusion.1
  131.3 0.0 copy-start.2
  131.3 3.2 %fusion.9 = bf16[80,2048]{1,0:T(8,128)(2,1)S(1)} fusion(bf16[1,1024,2048]{2,1,0:T(8,128)(2,1)} %param.8, bf16[80,3072]{1,0:T(8,128)(2,1)S(1)} %convolution_convert_fusion.1), kind=kOutput, calls=%fused_computation.14 | convolution fusion | flops 335708160 | bytes 4685824 | tf_op jit(solution)/shard_map/dot_general | solution.py:25
  134.5 0.2 copy-done.2
  134.8 1.4 broadcast_select_fusion.5
  136.2 1.1 convolution_convert_fusion.4
  137.3 3.2 %broadcast_select_fusion.1 = (bf16[2560,256]{1,0:T(8,128)(2,1)S(1)}, bf16[2560,256]{1,0:T(8,128)(2,1)S(1)}) fusion(pred[2560]{0:T(1024)(128)(4,1)S(1)} %get-tuple-element.50, bf16[2560,768]{1,0:T(8,128)(2,1)} %bitcast.6, pred[2560]{0:T(1024)(128)(4,1)S(1)} %get-tuple-element.51), kind=kLoop, calls=%fused_computation.19 | loop fusion | flops 1310720 | bytes 3937280 | tf_op jit(solution)/shard_map/jit(_where)/select_n | solution.py:106
  140.5 4.3 %fusion.4 = f32[512,512]{1,0:T(8,128)} fusion(bf16[2560,256]{1,0:T(8,128)(2,1)S(1)} %get-tuple-element.31, bf16[2560,256]{1,0:T(8,128)(2,1)S(1)} %get-tuple-element.30, bf16[2560,768]{1,0:T(8,128)(2,1)} %bitcast.6), kind=kOutput, calls=%fused_computation.6 | convolution fusion | flops 1347420160 | bytes 6291456 | tf_op jit(solution)/shard_map/dot_general | solution.py:25
  144.8 6.9 %all-to-all-start.2 = ((bf16[8,16,2048]{2,1,0:T(8,128)(2,1)}), bf16[8,16,2048]{2,1,0:T(8,128)(2,1)S(1)}, u32[]{:S(2)}, u32[]{:S(2)}) async-start(bf16[8,16,2048]{2,1,0:T(8,128)(2,1)} %bitcast.7), calls=%async_computation.2 | async-start | bytes 1048576 | tf_op jit(solution)/shard_map/all_to_all | solution.py:21
  151.8 0.0 reduce-scatter.2.cloned.1.call-start
  151.8 0.5 reduce-scatter.2.cloned.1.call-update
  152.4 17.8 %all-to-all-done.2 = bf16[8,16,2048]{2,1,0:T(8,128)(2,1)S(1)} async-done(((bf16[8,16,2048]{2,1,0:T(8,128)(2,1)}), bf16[8,16,2048]{2,1,0:T(8,128)(2,1)S(1)}, u32[]{:S(2)}, u32[]{:S(2)}) %all-to-all-start.2) | async-done | bytes 524320 | tf_op jit(solution)/shard_map/all_to_all | solution.py:21
  170.1 0.4 convolution_convert_fusion
  170.5 5.2 %all-gather.2.cloned.1.call-done = bf16[2,512,2048]{2,1,0:T(8,128)(2,1)} async-done(((bf16[2,64,2048]{2,1,0:T(8,128)(2,1)}), bf16[2,512,2048]{2,1,0:T(8,128)(2,1)}) %all-gather.2.cloned.1.call-update) | async-done | bytes 4194320 | tf_op jit(solution)/shard_map/all_gather | solution.py:101
  175.7 0.0 copy-start.3
  175.7 3.2 %convolution_convert_fusion.5 = bf16[80,2048]{1,0:T(8,128)(2,1)S(1)} fusion(bf16[1024,2048]{1,0:T(8,128)(2,1)} %bitcast.40, bf16[80,3072]{1,0:T(8,128)(2,1)S(1)} %convolution_convert_fusion), kind=kOutput, calls=%fused_computation.15 | convolution fusion | flops 335708160 | bytes 4685824 | tf_op jit(solution)/shard_map/dot_general | solution.py:25
  178.9 0.3 copy-done.3
  179.2 1.4 broadcast_select_fusion.3
  180.6 1.1 convolution_convert_fusion.3
  181.6 34.9 %reduce-scatter.2.cloned.1.call-done = f32[64,512]{1,0:T(8,128)} async-done(((f32[512,512]{1,0:T(8,128)}), f32[64,512]{1,0:T(8,128)}) %reduce-scatter.2.cloned.1.call-update) | async-done | bytes 131088 | tf_op jit(solution)/shard_map/reduce_scatter | solution.py:109
  216.6 5.7 %all-to-all-start.3 = ((bf16[8,16,2048]{2,1,0:T(8,128)(2,1)}), bf16[8,16,2048]{2,1,0:T(8,128)(2,1)S(1)}, u32[]{:S(2)}, u32[]{:S(2)}) async-start(bf16[8,16,2048]{2,1,0:T(8,128)(2,1)} %bitcast.12), calls=%async_computation.4 | async-start | bytes 1048576 | tf_op jit(solution)/shard_map/all_to_all | solution.py:21
  222.2 0.0 copy-start.4
  222.3 0.0 copy-start.5
  222.3 0.9 constant_dynamic-slice_fusion
  223.2 1.9 collective-permute-start.2
  225.1 2.9 %collective-permute-start.3 = (f32[16,512]{1,0:T(8,128)S(1)}, f32[16,512]{1,0:T(8,128)S(1)}, u32[]{:S(2)}, u32[]{:S(2)}) collective-permute-start(f32[16,512]{1,0:T(8,128)S(1)} %get-tuple-element.45), channel_id=1, source_target_pairs={{0,128},{16,144},{128,0},{144,16},{1,129},{17,145},{129,1},{145,17... | collective-permute-start | bytes 98312 | tf_op jit(solution)/shard_map/ppermute | solution.py:147
  228.0 2.8 %collective-permute-start.4 = (f32[16,512]{1,0:T(8,128)S(1)}, f32[16,512]{1,0:T(8,128)S(1)}, u32[]{:S(2)}, u32[]{:S(2)}) collective-permute-start(f32[16,512]{1,0:T(8,128)S(1)} %get-tuple-element.44), channel_id=1, source_target_pairs={{0,16},{16,0},{128,144},{144,128},{1,17},{17,1},{129,145},{145,129... | collective-permute-start | bytes 98312 | tf_op jit(solution)/shard_map/ppermute | solution.py:147
  230.8 0.0 collective-permute-done.2
  230.8 0.3 collective-permute-done.3
  231.2 0.5 collective-permute-done.4
  231.6 0.8 select_select_fusion.3
  232.4 0.7 pad_maximum_fusion.2
  233.1 5.0 %all-to-all-done.3 = bf16[8,16,2048]{2,1,0:T(8,128)(2,1)S(1)} async-done(((bf16[8,16,2048]{2,1,0:T(8,128)(2,1)}), bf16[8,16,2048]{2,1,0:T(8,128)(2,1)S(1)}, u32[]{:S(2)}, u32[]{:S(2)}) %all-to-all-start.3) | async-done | bytes 524320 | tf_op jit(solution)/shard_map/all_to_all | solution.py:21
  238.1 0.5 fusion.17
  238.6 0.0 copy-done.4
  238.6 0.0 copy-done.5
  238.6 1.5 fusion.16
  240.0 0.9 fusion.32
  (9 shorter events, 0.2 us)
Async XLA Ops:
  8.0 2.5 %copy-start = (bf16[128,1024]{1,0:T(8,128)(2,1)S(1)}, bf16[128,1024]{1,0:T(8,128)(2,1)}, u32[]{:S(2)}) copy-start(bf16[128,1024]{1,0:T(8,128)(2,1)} %param.5) | copy-start | bytes 786436
  13.4 38.7 %all-to-all-start = ((bf16[8,24,3072]{2,1,0:T(8,128)(2,1)}), bf16[8,24,3072]{2,1,0:T(8,128)(2,1)S(1)}, u32[]{:S(2)}, u32[]{:S(2)}) async-start(bf16[8,24,3072]{2,1,0:T(8,128)(2,1)} %bitcast.2), calls=%async_computation | async-start | bytes 2359296 | tf_op jit(solution)/shard_map/all_to_all | solution.py:21
  21.4 25.7 %collective-permute-start = (bf16[64,2048]{1,0:T(8,128)(2,1)S(1)}, bf16[64,2048]{1,0:T(8,128)(2,1)S(1)}, u32[]{:S(2)}, u32[]{:S(2)}) collective-permute-start(bf16[64,2048]{1,0:T(8,128)(2,1)S(1)} %dynamic-slice_bitcast_fusion), channel_id=1, source_target_pairs={{0,1},{1,0},{2,3},{3,2},{4,5},{5,4},{6,7},{7,6},{8,9},{9,8},{10,11... | collective-permute-start | bytes 786440 | tf_op jit(solution)/shard_map/ppermute | solution.py:67
  53.1 1.9 copy-start.1
  55.0 74.9 %all-to-all-start.1 = ((bf16[16,160,768]{2,1,0:T(8,128)(2,1)}), bf16[16,160,768]{2,1,0:T(8,128)(2,1)}, u32[]{:S(2)}, u32[]{:S(2)}) async-start(bf16[16,160,768]{2,1,0:T(8,128)(2,1)} %copy-done.1), calls=%async_computation.1 | async-start | bytes 7864320 | tf_op jit(solution)/shard_map/all_to_all | solution.py:21
  72.5 103.2 %all-gather.2.cloned.1.call-start = ((), (), s32[]{:S(2)}) async-start(), calls=%async_computation.5 | async-start | bytes 4718592 | tf_op jit(solution)/shard_map/all_gather | solution.py:101
  72.5 51.4 %collective-permute-start.1 = (bf16[64,2048]{1,0:T(8,128)(2,1)S(1)}, bf16[64,2048]{1,0:T(8,128)(2,1)S(1)}, u32[]{:S(2)}, u32[]{:S(2)}) collective-permute-start(bf16[64,2048]{1,0:T(8,128)(2,1)S(1)} %collective-permute-done), channel_id=1, source_target_pairs={{0,128},{128,0},{1,129},{129,1},{2,130},{130,2},{3,131},{131,3},{4... | collective-permute-start | bytes 786440 | tf_op jit(solution)/shard_map/ppermute | solution.py:80
  131.3 3.5 %copy-start.2 = (bf16[1,1024,2048]{2,1,0:T(8,128)(2,1)S(1)}, bf16[1,1024,2048]{2,1,0:T(8,128)(2,1)}, u32[]{:S(2)}) copy-start(bf16[1,1024,2048]{2,1,0:T(8,128)(2,1)} %param.8) | copy-start | bytes 12582916
  144.8 25.3 %all-to-all-start.2 = ((bf16[8,16,2048]{2,1,0:T(8,128)(2,1)}), bf16[8,16,2048]{2,1,0:T(8,128)(2,1)S(1)}, u32[]{:S(2)}, u32[]{:S(2)}) async-start(bf16[8,16,2048]{2,1,0:T(8,128)(2,1)} %bitcast.7), calls=%async_computation.2 | async-start | bytes 1048576 | tf_op jit(solution)/shard_map/all_to_all | solution.py:21
  151.8 64.8 %reduce-scatter.2.cloned.1.call-start = ((), (), s32[]{:S(2)}) async-start(), calls=%async_computation.6 | async-start | bytes 1179648 | tf_op jit(solution)/shard_map/reduce_scatter | solution.py:109
  175.7 3.4 %copy-start.3 = (bf16[2,512,2048]{2,1,0:T(8,128)(2,1)S(1)}, bf16[2,512,2048]{2,1,0:T(8,128)(2,1)}, u32[]{:S(2)}) copy-start(bf16[2,512,2048]{2,1,0:T(8,128)(2,1)} %all-gather.2.cloned.1.call-done) | copy-start | bytes 12582916
  216.6 21.5 %all-to-all-start.3 = ((bf16[8,16,2048]{2,1,0:T(8,128)(2,1)}), bf16[8,16,2048]{2,1,0:T(8,128)(2,1)S(1)}, u32[]{:S(2)}, u32[]{:S(2)}) async-start(bf16[8,16,2048]{2,1,0:T(8,128)(2,1)} %bitcast.12), calls=%async_computation.4 | async-start | bytes 1048576 | tf_op jit(solution)/shard_map/all_to_all | solution.py:21
  222.2 16.3 %copy-start.4 = (bf16[128,2048]{1,0:T(8,128)(2,1)S(1)}, bf16[128,2048]{1,0:T(8,128)(2,1)}, u32[]{:S(2)}) copy-start(bf16[128,2048]{1,0:T(8,128)(2,1)} %param.9) | copy-start | bytes 1572868
  222.3 16.3 %copy-start.5 = (f32[128,1]{0,1:T(1,128)S(1)}, f32[128,1]{0,1:T(1,128)}, u32[]{:S(2)}) copy-start(f32[128,1]{0,1:T(1,128)} %param.7) | copy-start | bytes 1540
  223.2 7.6 %collective-permute-start.2 = (f32[16,512]{1,0:T(8,128)S(1)}, f32[16,512]{1,0:T(8,128)S(1)}, u32[]{:S(2)}, u32[]{:S(2)}) collective-permute-start(f32[16,512]{1,0:T(8,128)S(1)} %get-tuple-element.46), channel_id=1, source_target_pairs={{0,144},{16,128},{128,16},{144,0},{1,145},{17,129},{129,17},{145,1... | collective-permute-start | bytes 98312 | tf_op jit(solution)/shard_map/ppermute | solution.py:147
  225.1 6.1 %collective-permute-start.3 = (f32[16,512]{1,0:T(8,128)S(1)}, f32[16,512]{1,0:T(8,128)S(1)}, u32[]{:S(2)}, u32[]{:S(2)}) collective-permute-start(f32[16,512]{1,0:T(8,128)S(1)} %get-tuple-element.45), channel_id=1, source_target_pairs={{0,128},{16,144},{128,0},{144,16},{1,129},{17,145},{129,1},{145,17... | collective-permute-start | bytes 98312 | tf_op jit(solution)/shard_map/ppermute | solution.py:147
  228.0 3.6 %collective-permute-start.4 = (f32[16,512]{1,0:T(8,128)S(1)}, f32[16,512]{1,0:T(8,128)S(1)}, u32[]{:S(2)}, u32[]{:S(2)}) collective-permute-start(f32[16,512]{1,0:T(8,128)S(1)} %get-tuple-element.44), channel_id=1, source_target_pairs={{0,16},{16,0},{128,144},{144,128},{1,17},{17,1},{129,145},{145,129... | collective-permute-start | bytes 98312 | tf_op jit(solution)/shard_map/ppermute | solution.py:147
Sparse Core Ops, SparseCore 0:
  130.9 44.7 all-gather.1
Sparse Core Ops, SparseCore 1:
  155.6 60.8 reduce-scatter.1

commit v10 on v8

--- a/solution.py
+++ b/solution.py
@@ -44,6 +44,33 @@
             blocks[x * cs + c, :, quarter:] = kept[:, c * half : (c + 1) * half]
 
 
+def place_kernel(slots, ids, gates, hidden, out_grad, outgoing, ranks):
+    tall = outgoing.shape[0]
+    tok_rows, out_width = out_grad.shape
+    square = (tok_rows, tok_rows)
+    down, across = lax.broadcasted_iota(I32, square, 0), lax.broadcasted_iota(I32, square, 1)
+    experts = lax.broadcasted_iota(I32, (tall // slots, tok_rows), 0)
+    named = (experts == ids[...]).astype(F32)
+    before = dot(named.astype(BF16), (down < across).astype(BF16), ((1,), (0,)), F32)
+    rank = jnp.sum(named * before, axis=0, keepdims=True).astype(I32)
+    ranks[...] = rank
+    gate = jnp.sum(jnp.where(down == across, gates[...], 0.0), axis=1, keepdims=True)
+    grads = (gate * out_grad[...].astype(F32)).astype(BF16)
+    place = lax.broadcasted_iota(I32, (tall, tok_rows), 0)
+    placer = (place == ids[...] * slots + rank).astype(BF16)
+    outgoing[:, :out_width] = dot(placer, grads, ((1,), (0,)))
+    outgoing[:, out_width:] = dot(placer, hidden[...], ((1,), (0,)))
+
+
+def partial_kernel(capacity, halves, quarter, rows, partial):
+    tall = rows.shape[0]
+    expert = lax.broadcasted_iota(I32, (tall, quarter), 0) // capacity % halves
+    hid, grads = rows[:, :quarter].astype(F32), rows[:, quarter:]
+    for h in range(halves):
+        kept = jnp.where(expert == h, hid, 0.0).astype(BF16)
+        partial[h * quarter : (h + 1) * quarter, :] = dot(kept, grads, ((0,), (0,)), F32)
+
+
 def shards(hidden, expert_ids, gate_weights, down_weight, out_grad):
     tok_rows, hid_width = hidden.shape
     out_width = out_grad.shape[1]
@@ -64,14 +91,20 @@
     share = lax.ppermute(share, "zh", [(0, 1), (1, 0)])
 
     expert_list = expert_ids[:, 0]
-    onehot = (expert_list[:, None] == jnp.arange(experts, dtype=I32)[None, :]).astype(I32)
-    row_rank = jnp.sum(onehot * (jnp.cumsum(onehot, axis=0) - 1), axis=1)
-    slot_index = expert_list * slots + row_rank
-    placer = (jnp.arange(tall, dtype=I32)[:, None] == slot_index[None, :]).astype(BF16)
-    grad_rows = (gate_weights * out_grad.astype(F32)).astype(BF16)
-    outgoing = jnp.concatenate(
-        [dot(placer, grad_rows, ((1,), (0,))), dot(placer, hidden, ((1,), (0,)))], axis=1
-    )
+    outgoing, ranks = pl.pallas_call(
+        functools.partial(place_kernel, slots),
+        out_shape=(
+            jax.ShapeDtypeStruct((tall, out_width + hid_width), BF16),
+            jax.ShapeDtypeStruct((1, tok_rows), I32),
+        ),
+        compiler_params=pltpu.CompilerParams(vmem_limit_bytes=24 * 2**20),
+        cost_estimate=pl.CostEstimate(
+            flops=2 * tall * tok_rows * (hid_width + out_width),
+            bytes_accessed=3 * 2**20,
+            transcendentals=0,
+        ),
+    )(expert_ids.reshape(1, -1), gate_weights.reshape(1, -1), hidden, out_grad)
+    row_rank = ranks[0]
     arrived = exchange(outgoing.reshape(columns, block, -1), "y").reshape(tall, -1)
     arrived, share = lax.optimization_barrier((arrived, share))
     beside = lax.ppermute(share, "zp", [(0, 1), (1, 0)])
@@ -92,19 +125,6 @@
         )(arrived),
         NEAR,
     ).reshape(near * rows, -1)
-    near_rows, share, beside = lax.optimization_barrier((near_rows, share, beside))
-    even = lax.axis_index("zp") == 0
-    pair = jnp.stack([jnp.where(even, share, beside), jnp.where(even, beside, share)])
-    other_weight = lax.all_gather(pair, NEAR, axis=1, tiled=True).reshape(hid_width, -1)
-    hid_near, grad_near = near_rows[:, : hid_width // xs], near_rows[:, hid_width // xs :]
-    of_half = (jnp.arange(near * rows, dtype=I32) // capacity % halves)[:, None]
-    zero = jnp.zeros((), BF16)
-    by_half = jnp.concatenate(
-        [jnp.where(of_half == h, hid_near, zero) for h in range(halves)], axis=1
-    )
-    partial_grad = dot(by_half, grad_near, ((0,), (0,)), F32)
-    ring_sum = lax.psum_scatter(partial_grad, RING, scatter_dimension=0, tiled=True)
-
     full = jnp.arange(columns * capacity, dtype=I32)
     origin, rank = full // capacity, full % capacity
     odd = (rank % 2 == 1)[:, None]
@@ -126,7 +146,26 @@
         spread = (jnp.arange(short, dtype=I32)[:, None] == spots[None, :]).astype(BF16)
         return dot(spread, jnp.concatenate([proj, pairs], axis=0), ((1,), (0,)))
 
-    own_leaving, _ = lax.optimization_barrier((products(half, weight, arrived), partial_grad))
+    own_leaving = products(half, weight, arrived)
+    near_rows, share, beside, own_leaving = lax.optimization_barrier(
+        (near_rows, share, beside, own_leaving)
+    )
+    even = lax.axis_index("zp") == 0
+    pair = jnp.stack([jnp.where(even, share, beside), jnp.where(even, beside, share)])
+    other_weight = lax.all_gather(pair, NEAR, axis=1, tiled=True).reshape(hid_width, -1)
+    partial_grad = pl.pallas_call(
+        functools.partial(partial_kernel, capacity, halves, hid_width // xs),
+        out_shape=jax.ShapeDtypeStruct((halves * hid_width // xs, out_width // cs), F32),
+        compiler_params=pltpu.CompilerParams(vmem_limit_bytes=40 * 2**20),
+        cost_estimate=pl.CostEstimate(
+            flops=2 * near * rows * halves * (hid_width // xs) * (out_width // cs),
+            bytes_accessed=6 * 2**20,
+            transcendentals=0,
+        ),
+    )(near_rows)
+    ring_sum = lax.psum_scatter(partial_grad, RING, scatter_dimension=0, tiled=True)
+
+    own_leaving, _ = lax.optimization_barrier((own_leaving, partial_grad))
     own_back = exchange(own_leaving.reshape(columns, back_block, -1), "y").reshape(short, -1)
     arrived, own_back = lax.optimization_barrier((arrived, own_back))
     other_leaving = products(1 - half, other_weight, arrived)

time: 210 us -> 208 us (level)
  blocking collectives: 20 us -> 0 us
  waiting for transfers between devices: 84 us -> 99.9 us
  Pallas kernels: 1.04 us -> 7.79 us
  matrix products: 18.3 us -> 12.6 us
  other arithmetic: 9.5 us -> 4.07 us
  starting transfers between devices: 55.3 us -> 58.8 us
  local copies, waits for them, and re-layouts: 4.03 us -> 7.06 us
    all_to_all x1 -> x0, blocking collectives: 20 us -> none  [exchange(): return lax.all_to_all(blocks, axes, split_axis=0, concat_axis=0, tiled=True)]
    all_to_all x3 -> x4, waiting for transfers between devices: 21 us -> 38.4 us  [exchange(): return lax.all_to_all(blocks, axes, split_axis=0, concat_axis=0, tiled=True)]
    pallas_call x0 -> x2, Pallas kernels: none -> 6.74 us  [the longest x1 5.12 us: shards(): pl.pallas_call(functools.partial(partial_kernel, capacity, halves, hid_wi...]
    all_gather x1, waiting for transfers between devices: 20.2 us -> 26.3 us  [shards(): lax.all_gather(pair, NEAR, axis=1, tiled=True).reshape(hid_width, -1)]
    ppermute x1, waiting for transfers between devices: 6.6 us -> 0.55 us  [shards(): beside = lax.ppermute(share, 'zp', [(0, 1), (1, 0)])]
    dot_general x12 -> x9, matrix products: 18.3 us -> 12.6 us  [dot(): lax.dot_general(a, b, (dims, ((), ())), preferred_element_type=F32)]
    all_to_all x3 -> x4, starting transfers between devices: 18.8 us -> 22.4 us  [exchange(): return lax.all_to_all(blocks, axes, split_axis=0, concat_axis=0, tiled=True)]
    unnamed x14 -> x22, local copies, waits for them, and re-layouts: 2.22 us -> 5.25 us
  transfers between devices with their start and end apart: 8 -> 9, of which waited for: 6 -> 7; matrix products, arithmetic and copies ran while one was open for 11% -> 8% of each run, Pallas kernels for 0% -> 2%
where the time goes in v10:
time: 208 us; the launch traced here: 206 us
  waiting for transfers between devices  99.9 us (48%)
  starting transfers between devices  58.8 us (28%)
  between operations  15.7 us (8%)
  matrix products  12.6 us (6%)
  Pallas kernels  7.79 us (4%)
  local copies, waits for them, and re-layouts  7.06 us (3%)
  other arithmetic  4.07 us (2%)
    all_to_all x4, waiting for transfers between devices, exchange(): return lax.all_to_all(blocks, axes, split_axis=0, concat_axis=0, tiled=True)  38.4 us
    reduce_scatter x1, waiting for transfers between devices, shards(): lax.psum_scatter(partial_grad, RING, scatter_dimension=0, tiled=True)  28.3 us
    all_gather x1, waiting for transfers between devices, shards(): lax.all_gather(pair, NEAR, axis=1, tiled=True).reshape(hid_width, -1)  26.3 us
    all_to_all x4, starting transfers between devices, exchange(): return lax.all_to_all(blocks, axes, split_axis=0, concat_axis=0, tiled=True)  22.4 us
    ppermute x1, starting transfers between devices, shards(): share = lax.ppermute(share, 'zh', [(0, 1), (1, 0)])  19.4 us
    ppermute x1, starting transfers between devices, shards(): beside = lax.ppermute(share, 'zp', [(0, 1), (1, 0)])  15.1 us
    dot_general x9, matrix products, dot(): lax.dot_general(a, b, (dims, ((), ())), preferred_element_type=F32)  12.6 us
    ppermute x1, waiting for transfers between devices, shards(): share = lax.ppermute(share, 'zh', [(0, 1), (1, 0)])  6.31 us
  transfers between devices with their start and end apart: 9, of which 7 were waited for; matrix products, arithmetic and copies ran while one was open for 8% of the time, Pallas kernels for 2%

profile of v10, /device:TPU:6, one launch (start us, length us, event | category | flops | bytes accessed | tf_op | source)
XLA Modules:
  0.0 205.9 jit_solution(9893087876353753720)
XLA Ops:
  8.0 0.0 copy-start.1
  8.0 1.0 copy-done.1
  9.0 0.0 copy-start.3
  9.0 0.9 copy-done.3
  10.0 0.0 copy-start.4
  10.0 0.7 copy-done.4
  10.6 0.0 copy-start.6
  10.7 0.7 copy-done.6
  11.3 1.6 shard_map.84
  12.9 7.1 %all-to-all-start = ((bf16[8,24,3072]{2,1,0:T(8,128)(2,1)}), bf16[8,24,3072]{2,1,0:T(8,128)(2,1)S(1)}, u32[]{:S(2)}, u32[]{:S(2)}) async-start(bf16[8,24,3072]{2,1,0:T(8,128)(2,1)} %bitcast.5), calls=%async_computation | async-start | bytes 2359296 | tf_op jit(solution)/shard_map/all_to_all | solution.py:20
  20.0 1.0 dynamic-slice_bitcast_fusion
  21.0 19.4 %collective-permute-start = (bf16[64,2048]{1,0:T(8,128)(2,1)S(1)}, bf16[64,2048]{1,0:T(8,128)(2,1)S(1)}, u32[]{:S(2)}, u32[]{:S(2)}) collective-permute-start(bf16[64,2048]{1,0:T(8,128)(2,1)S(1)} %dynamic-slice_bitcast_fusion), channel_id=1, source_target_pairs={{0,1},{1,0},{2,3},{3,2},{4,5},{5,4},{6,7},{7,6},{8,9},{9,8},{10,11... | collective-permute-start | bytes 786440 | tf_op jit(solution)/shard_map/ppermute | solution.py:91
  40.4 6.3 %collective-permute-done = bf16[64,2048]{1,0:T(8,128)(2,1)S(1)} collective-permute-done((bf16[64,2048]{1,0:T(8,128)(2,1)S(1)}, bf16[64,2048]{1,0:T(8,128)(2,1)S(1)}, u32[]{:S(2)}, u32[]{:S(2)}) %collective-permute-start) | collective-permute-done | bytes 262176 | tf_op jit(solution)/shard_map/ppermute | solution.py:91
  46.7 4.9 %all-to-all-done = bf16[8,24,3072]{2,1,0:T(8,128)(2,1)S(1)} async-done(((bf16[8,24,3072]{2,1,0:T(8,128)(2,1)}), bf16[8,24,3072]{2,1,0:T(8,128)(2,1)S(1)}, u32[]{:S(2)}, u32[]{:S(2)}) %all-to-all-start) | async-done | bytes 1179680 | tf_op jit(solution)/shard_map/all_to_all | solution.py:20
  51.6 1.0 shard_map.85
  52.7 0.0 copy-start
  52.7 1.7 copy-done
  54.3 4.9 %all-to-all-start.1 = ((bf16[8,160,1280]{2,1,0:T(8,128)(2,1)}), bf16[8,160,1280]{2,1,0:T(8,128)(2,1)}, u32[]{:S(2)}, u32[]{:S(2)}) async-start(bf16[8,160,1280]{2,1,0:T(8,128)(2,1)} %copy-done), calls=%async_computation.1 | async-start | bytes 6553600 | tf_op jit(solution)/shard_map/all_to_all | solution.py:20
  59.2 0.0 all-gather.2.cloned.1.call-start
  59.3 0.1 pad_add_fusion.1
  59.4 15.1 %collective-permute-start.1 = (bf16[64,2048]{1,0:T(8,128)(2,1)S(1)}, bf16[64,2048]{1,0:T(8,128)(2,1)S(1)}, u32[]{:S(2)}, u32[]{:S(2)}) collective-permute-start(bf16[64,2048]{1,0:T(8,128)(2,1)S(1)} %collective-permute-done), channel_id=1, source_target_pairs={{0,128},{128,0},{1,129},{129,1},{2,130},{130,2},{3,131},{131,3},{4... | collective-permute-start | bytes 786440 | tf_op jit(solution)/shard_map/ppermute | solution.py:110
  74.5 0.3 convolution_convert_fusion.1
  74.8 0.0 copy-start.8
  74.9 3.7 %broadcast_select_fusion.3 = (bf16[80,1024]{1,0:T(8,128)(2,1)S(1)}, bf16[80,1024]{1,0:T(8,128)(2,1)S(1)}) fusion(pred[80]{0:T(512)(128)(4,1)S(1)} %fusion.35, bf16[1,1024,2048]{2,1,0:T(8,128)(2,1)} %param.8, bf16[80,3072]{1,0:T(8,128)(2,1)S(1)} %convolution_convert_fusion.1), kind=kOutput, calls=%fused_computation.42 | convolution fusion | flops 335790080 | bytes 4850176 | tf_op jit(solution)/shard_map/dot_general | solution.py:24
  78.6 0.0 copy-done.8
  78.6 0.8 fusion.4
  79.5 1.1 convolution_convert_fusion.3
  80.5 0.6 collective-permute-done.1
  81.1 16.0 %all-to-all-done.1 = bf16[8,160,1280]{2,1,0:T(8,128)(2,1)} async-done(((bf16[8,160,1280]{2,1,0:T(8,128)(2,1)}), bf16[8,160,1280]{2,1,0:T(8,128)(2,1)}, u32[]{:S(2)}, u32[]{:S(2)}) %all-to-all-start.1) | async-done | bytes 3276832 | tf_op jit(solution)/shard_map/all_to_all | solution.py:20
  97.1 0.8 pad_maximum_fusion
  98.0 0.0 all-gather.2.cloned.1.call-update
  98.0 0.0 reduce-scatter.2.cloned.1.call-start
  98.0 5.1 %shard_map.86 = f32[512,1024]{1,0:T(8,128)} custom-call(bf16[1280,1280]{1,0:T(8,128)(2,1)} %bitcast.8.rows), custom_call_target="tpu_custom_call" | custom-call | flops 1342177280 | bytes 6291456 | tf_op jit(solution)/shard_map/pallas_call | solution.py:156
  103.2 0.0 reduce-scatter.2.cloned.1.call-update
  103.2 3.5 %all-to-all-start.2 = ((bf16[8,16,2048]{2,1,0:T(8,128)(2,1)}), bf16[8,16,2048]{2,1,0:T(8,128)(2,1)S(1)}, u32[]{:S(2)}, u32[]{:S(2)}) async-start(bf16[8,16,2048]{2,1,0:T(8,128)(2,1)} %bitcast.10), calls=%async_computation.2 | async-start | bytes 1048576 | tf_op jit(solution)/shard_map/all_to_all | solution.py:20
  106.7 17.5 %all-to-all-done.2 = bf16[8,16,2048]{2,1,0:T(8,128)(2,1)S(1)} async-done(((bf16[8,16,2048]{2,1,0:T(8,128)(2,1)}), bf16[8,16,2048]{2,1,0:T(8,128)(2,1)S(1)}, u32[]{:S(2)}, u32[]{:S(2)}) %all-to-all-start.2) | async-done | bytes 524320 | tf_op jit(solution)/shard_map/all_to_all | solution.py:20
  124.2 0.4 convolution_convert_fusion
  124.6 26.3 %all-gather.2.cloned.1.call-done = bf16[2,512,2048]{2,1,0:T(8,128)(2,1)} async-done(((bf16[2,64,2048]{2,1,0:T(8,128)(2,1)}), bf16[2,512,2048]{2,1,0:T(8,128)(2,1)}) %all-gather.2.cloned.1.call-update) | async-done | bytes 4194320 | tf_op jit(solution)/shard_map/all_gather | solution.py:155
  150.8 0.0 copy-start.9
  150.9 3.2 %convolution_convert_fusion.4 = bf16[80,2048]{1,0:T(8,128)(2,1)S(1)} fusion(bf16[1024,2048]{1,0:T(8,128)(2,1)} %bitcast.73, bf16[80,3072]{1,0:T(8,128)(2,1)S(1)} %convolution_convert_fusion), kind=kOutput, calls=%fused_computation.9 | convolution fusion | flops 335708160 | bytes 4685824 | tf_op jit(solution)/shard_map/dot_general | solution.py:24
  154.1 0.3 copy-done.9
  154.3 1.4 broadcast_select_fusion.1
  155.7 0.0 copy-start.5
  155.8 1.1 convolution_convert_fusion.2
  156.8 0.0 copy-start.2
  156.9 0.0 copy-start.7
  156.9 6.9 %all-to-all-start.3 = ((bf16[8,16,2048]{2,1,0:T(8,128)(2,1)}), bf16[8,16,2048]{2,1,0:T(8,128)(2,1)S(1)}, u32[]{:S(2)}, u32[]{:S(2)}) async-start(bf16[8,16,2048]{2,1,0:T(8,128)(2,1)} %bitcast.15), calls=%async_computation.3 | async-start | bytes 1048576 | tf_op jit(solution)/shard_map/all_to_all | solution.py:20
  163.7 0.0 copy-done.5
  163.8 28.3 %reduce-scatter.2.cloned.1.call-done = f32[32,1024]{1,0:T(8,128)} async-done(((f32[512,1024]{1,0:T(8,128)}), f32[32,1024]{1,0:T(8,128)}) %reduce-scatter.2.cloned.1.call-update) | async-done | bytes 131088 | tf_op jit(solution)/shard_map/reduce_scatter | solution.py:166
  192.1 0.0 all-to-all-done.3
  192.1 0.8 constant_dynamic-slice_fusion
  193.0 1.9 collective-permute-start.2
  194.9 0.5 fusion.10
  195.4 0.0 copy-start.10
  195.4 0.0 copy-done.2
  195.4 0.0 copy-done.7
  195.4 1.5 multiply_reduce_fusion
  196.9 0.9 fusion.24
  197.7 0.0 collective-permute-done.2
  197.7 0.0 copy-done.10
  197.8 0.7 maximum_bitcast_fusion
  (10 shorter events, 0.2 us)
Async XLA Ops:
  8.0 1.0 copy-start.1
  9.0 0.9 copy-start.3
  10.0 0.7 copy-start.4
  10.6 0.7 copy-start.6
  12.9 38.7 %all-to-all-start = ((bf16[8,24,3072]{2,1,0:T(8,128)(2,1)}), bf16[8,24,3072]{2,1,0:T(8,128)(2,1)S(1)}, u32[]{:S(2)}, u32[]{:S(2)}) async-start(bf16[8,24,3072]{2,1,0:T(8,128)(2,1)} %bitcast.5), calls=%async_computation | async-start | bytes 2359296 | tf_op jit(solution)/shard_map/all_to_all | solution.py:20
  21.0 25.7 %collective-permute-start = (bf16[64,2048]{1,0:T(8,128)(2,1)S(1)}, bf16[64,2048]{1,0:T(8,128)(2,1)S(1)}, u32[]{:S(2)}, u32[]{:S(2)}) collective-permute-start(bf16[64,2048]{1,0:T(8,128)(2,1)S(1)} %dynamic-slice_bitcast_fusion), channel_id=1, source_target_pairs={{0,1},{1,0},{2,3},{3,2},{4,5},{5,4},{6,7},{7,6},{8,9},{9,8},{10,11... | collective-permute-start | bytes 786440 | tf_op jit(solution)/shard_map/ppermute | solution.py:91
  52.7 1.7 copy-start
  54.3 42.8 %all-to-all-start.1 = ((bf16[8,160,1280]{2,1,0:T(8,128)(2,1)}), bf16[8,160,1280]{2,1,0:T(8,128)(2,1)}, u32[]{:S(2)}, u32[]{:S(2)}) async-start(bf16[8,160,1280]{2,1,0:T(8,128)(2,1)} %copy-done), calls=%async_computation.1 | async-start | bytes 6553600 | tf_op jit(solution)/shard_map/all_to_all | solution.py:20
  59.2 91.6 %all-gather.2.cloned.1.call-start = ((), (), s32[]{:S(2)}) async-start(), calls=%async_computation.5 | async-start | bytes 4718592 | tf_op jit(solution)/shard_map/all_gather | solution.py:155
  59.4 21.7 %collective-permute-start.1 = (bf16[64,2048]{1,0:T(8,128)(2,1)S(1)}, bf16[64,2048]{1,0:T(8,128)(2,1)S(1)}, u32[]{:S(2)}, u32[]{:S(2)}) collective-permute-start(bf16[64,2048]{1,0:T(8,128)(2,1)S(1)} %collective-permute-done), channel_id=1, source_target_pairs={{0,128},{128,0},{1,129},{129,1},{2,130},{130,2},{3,131},{131,3},{4... | collective-permute-start | bytes 786440 | tf_op jit(solution)/shard_map/ppermute | solution.py:110
  74.8 3.8 %copy-start.8 = (bf16[1,1024,2048]{2,1,0:T(8,128)(2,1)S(1)}, bf16[1,1024,2048]{2,1,0:T(8,128)(2,1)}, u32[]{:S(2)}) copy-start(bf16[1,1024,2048]{2,1,0:T(8,128)(2,1)} %param.8) | copy-start | bytes 12582916
  98.0 94.1 %reduce-scatter.2.cloned.1.call-start = ((), (), s32[]{:S(2)}) async-start(), calls=%async_computation.6 | async-start | bytes 2228224 | tf_op jit(solution)/shard_map/reduce_scatter | solution.py:166
  103.2 21.0 %all-to-all-start.2 = ((bf16[8,16,2048]{2,1,0:T(8,128)(2,1)}), bf16[8,16,2048]{2,1,0:T(8,128)(2,1)S(1)}, u32[]{:S(2)}, u32[]{:S(2)}) async-start(bf16[8,16,2048]{2,1,0:T(8,128)(2,1)} %bitcast.10), calls=%async_computation.2 | async-start | bytes 1048576 | tf_op jit(solution)/shard_map/all_to_all | solution.py:20
  150.8 3.5 %copy-start.9 = (bf16[2,512,2048]{2,1,0:T(8,128)(2,1)S(1)}, bf16[2,512,2048]{2,1,0:T(8,128)(2,1)}, u32[]{:S(2)}) copy-start(bf16[2,512,2048]{2,1,0:T(8,128)(2,1)} %all-gather.2.cloned.1.call-done) | copy-start | bytes 12582916
  155.7 8.0 %copy-start.5 = (s32[128,1]{0,1:T(1,128)S(1)}, s32[128,1]{0,1:T(1,128)}, u32[]{:S(2)}) copy-start(s32[128,1]{0,1:T(1,128)} %param.6) | copy-start | bytes 1540
  156.8 38.5 %copy-start.2 = (bf16[128,2048]{1,0:T(8,128)(2,1)S(1)}, bf16[128,2048]{1,0:T(8,128)(2,1)}, u32[]{:S(2)}) copy-start(bf16[128,2048]{1,0:T(8,128)(2,1)} %out_grad.1) | copy-start | bytes 1572868
  156.9 38.5 %copy-start.7 = (f32[128,1]{0,1:T(1,128)S(1)}, f32[128,1]{0,1:T(1,128)}, u32[]{:S(2)}) copy-start(f32[128,1]{0,1:T(1,128)} %param.7) | copy-start | bytes 1540
  156.9 35.3 %all-to-all-start.3 = ((bf16[8,16,2048]{2,1,0:T(8,128)(2,1)}), bf16[8,16,2048]{2,1,0:T(8,128)(2,1)S(1)}, u32[]{:S(2)}, u32[]{:S(2)}) async-start(bf16[8,16,2048]{2,1,0:T(8,128)(2,1)} %bitcast.15), calls=%async_computation.3 | async-start | bytes 1048576 | tf_op jit(solution)/shard_map/all_to_all | solution.py:20
  193.0 4.8 %collective-permute-start.2 = (f32[16,1024]{1,0:T(8,128)S(1)}, f32[16,1024]{1,0:T(8,128)S(1)}, u32[]{:S(2)}, u32[]{:S(2)}) collective-permute-start(f32[16,1024]{1,0:T(8,128)S(1)} %constant_dynamic-slice_fusion), channel_id=1, source_target_pairs={{0,16},{16,0},{1,17},{17,1},{2,18},{18,2},{3,19},{19,3},{4,20},{20... | collective-permute-start | bytes 196616 | tf_op jit(solution)/shard_map/ppermute | solution.py:192
  195.4 2.4 %copy-start.10 = (f32[32,1024]{1,0:T(8,128)S(1)}, f32[32,1024]{1,0:T(8,128)}, u32[]{:S(2)}) copy-start(f32[32,1024]{1,0:T(8,128)} %reduce-scatter.2.cloned.1.call-done) | copy-start | bytes 393220
Sparse Core Ops, SparseCore 0:
  98.1 52.6 all-gather.1
Sparse Core Ops, SparseCore 1:
  103.3 88.8 reduce-scatter.1

commit v11 on v10

--- a/solution.py
+++ b/solution.py
@@ -27,21 +27,22 @@
 def pack_kernel(capacity, slots, strip, xs, cs, hid_width, arrived, blocks):
     tall, width = arrived.shape
     rows = blocks.shape[1]
-    quarter = hid_width // xs
-    half = (width - hid_width) // cs
+    half = hid_width // cs
+    quarter = (width - hid_width) // xs
     full = lax.broadcasted_iota(I32, (rows, tall), 0)
     wanted = full // capacity * slots + full % capacity
     compact = (wanted == lax.broadcasted_iota(I32, (rows, tall), 1)).astype(BF16)
     kept = dot(compact, arrived[...], ((1,), (0,)))
     group = cs * strip
     place = lax.broadcasted_iota(I32, (hid_width, hid_width), 0)
-    target = place // group % xs * quarter + place // (group * xs) * group + place % group
+    row = place // (group * xs) * (xs * strip) + place // group % xs * strip + place % strip
+    target = place // strip % cs * half + row
     sorter = (target == lax.broadcasted_iota(I32, (hid_width, hid_width), 1)).astype(BF16)
     hid = dot(kept[:, width - hid_width :], sorter, ((1,), (0,)))
     for x in range(xs):
         for c in range(cs):
-            blocks[x * cs + c, :, :quarter] = hid[:, x * quarter : (x + 1) * quarter]
-            blocks[x * cs + c, :, quarter:] = kept[:, c * half : (c + 1) * half]
+            blocks[x * cs + c, :, :half] = hid[:, c * half : (c + 1) * half]
+            blocks[x * cs + c, :, half:] = kept[:, x * quarter : (x + 1) * quarter]
 
 
 def place_kernel(slots, ids, gates, hidden, out_grad, outgoing, ranks):
@@ -114,7 +115,7 @@
         pl.pallas_call(
             functools.partial(pack_kernel, capacity, slots, strip, xs, cs, hid_width),
             out_shape=jax.ShapeDtypeStruct(
-                (near, rows, hid_width // xs + out_width // cs), BF16
+                (near, rows, hid_width // cs + out_width // xs), BF16
             ),
             compiler_params=pltpu.CompilerParams(vmem_limit_bytes=40 * 2**20),
             cost_estimate=pl.CostEstimate(
@@ -154,11 +155,11 @@
     pair = jnp.stack([jnp.where(even, share, beside), jnp.where(even, beside, share)])
     other_weight = lax.all_gather(pair, NEAR, axis=1, tiled=True).reshape(hid_width, -1)
     partial_grad = pl.pallas_call(
-        functools.partial(partial_kernel, capacity, halves, hid_width // xs),
-        out_shape=jax.ShapeDtypeStruct((halves * hid_width // xs, out_width // cs), F32),
+        functools.partial(partial_kernel, capacity, halves, hid_width // cs),
+        out_shape=jax.ShapeDtypeStruct((halves * hid_width // cs, out_width // xs), F32),
         compiler_params=pltpu.CompilerParams(vmem_limit_bytes=40 * 2**20),
         cost_estimate=pl.CostEstimate(
-            flops=2 * near * rows * halves * (hid_width // xs) * (out_width // cs),
+            flops=2 * near * rows * halves * (hid_width // cs) * (out_width // xs),
             bytes_accessed=6 * 2**20,
             transcendentals=0,
         ),
@@ -185,14 +186,20 @@
     layer_out = (gate_weights * projected).astype(BF16)
     gate_grad = jnp.sum(out_grad.astype(F32) * projected, axis=1, keepdims=True)
 
-    core = lax.axis_index("c")
-    first = core == 0
-    kept = lax.dynamic_slice_in_dim(ring_sum, core * strip, strip, axis=0)
-    given = lax.dynamic_slice_in_dim(ring_sum, (1 - core) * strip, strip, axis=0)
-    taken = lax.ppermute(given, "c", [(0, 1), (1, 0)])
-    weight_grad = jnp.concatenate(
-        [jnp.where(first, kept, taken), jnp.where(first, taken, kept)], axis=1
-    )
+    mine = lax.axis_index("x")
+    held = [
+        lax.dynamic_slice_in_dim(ring_sum, (mine ^ k) * strip, strip, axis=0) for k in range(xs)
+    ]
+    held = [held[0]] + [
+        lax.ppermute(held[k], "x", [(i, i ^ k) for i in range(xs)]) for k in range(1, xs)
+    ]
+    quarters = []
+    for p in range(xs):
+        chosen = held[0]
+        for k in range(1, xs):
+            chosen = jnp.where((mine ^ k) == p, held[k], chosen)
+        quarters.append(chosen)
+    weight_grad = jnp.concatenate(quarters, axis=1)
     return (layer_out, hidden_grad, gate_grad, weight_grad[None])
 
 

time: 208 us -> 208 us (level)
  starting transfers between devices: 58.8 us -> 66.6 us
  waiting for transfers between devices: 99.9 us -> 93.1 us
    ppermute x1 -> x3, starting transfers between devices: 1.91 us -> 9.81 us  [shards(): lax.ppermute(held[k], 'x', [(i, i ^ k) for i in range(xs)])]
    all_to_all x4, waiting for transfers between devices: 38.4 us -> 31.4 us  [exchange(): return lax.all_to_all(blocks, axes, split_axis=0, concat_axis=0, tiled=True)]
    unnamed x22 -> x20, local copies, waits for them, and re-layouts: 5.25 us -> 5.08 us
  transfers between devices with their start and end apart: 9 -> 11, of which waited for: 7 -> 8; matrix products, arithmetic and copies ran while one was open for 8% -> 8% of each run, Pallas kernels for 2% -> 2%
where the time goes in v11:
time: 208 us; the launch traced here: 207 us
  waiting for transfers between devices  93.1 us (45%)
  starting transfers between devices  66.6 us (32%)
  between operations  15.7 us (8%)
  matrix products  12.6 us (6%)
  Pallas kernels  7.43 us (4%)
  local copies, waits for them, and re-layouts  6.84 us (3%)
  other arithmetic  4.84 us (2%)
    all_to_all x4, waiting for transfers between devices, exchange(): return lax.all_to_all(blocks, axes, split_axis=0, concat_axis=0, tiled=True)  31.4 us
    reduce_scatter x1, waiting for transfers between devices, shards(): lax.psum_scatter(partial_grad, RING, scatter_dimension=0, tiled=True)  27.9 us
    all_gather x1, waiting for transfers between devices, shards(): lax.all_gather(pair, NEAR, axis=1, tiled=True).reshape(hid_width, -1)  26.7 us
    all_to_all x4, starting transfers between devices, exchange(): return lax.all_to_all(blocks, axes, split_axis=0, concat_axis=0, tiled=True)  22.3 us
    ppermute x1, starting transfers between devices, shards(): share = lax.ppermute(share, 'zh', [(0, 1), (1, 0)])  19.4 us
    ppermute x1, starting transfers between devices, shards(): beside = lax.ppermute(share, 'zp', [(0, 1), (1, 0)])  15.1 us
    dot_general x9, matrix products, dot(): lax.dot_general(a, b, (dims, ((), ())), preferred_element_type=F32)  12.6 us
    ppermute x3, starting transfers between devices, shards(): lax.ppermute(held[k], 'x', [(i, i ^ k) for i in range(xs)])  9.81 us
  transfers between devices with their start and end apart: 11, of which 8 were waited for; matrix products, arithmetic and copies ran while one was open for 8% of the time, Pallas kernels for 2%

profile of v11, /device:TPU:6, one launch (start us, length us, event | category | flops | bytes accessed | tf_op | source)
XLA Modules:
  0.0 207.2 jit_solution(10190796976413721790)
XLA Ops:
  8.0 0.0 copy-start.1
  8.0 1.0 copy-done.1
  9.0 0.0 copy-start.3
  9.0 0.9 copy-done.3
  10.0 0.0 copy-start.4
  10.0 0.7 copy-done.4
  10.6 0.0 copy-start.6
  10.7 0.7 copy-done.6
  11.3 1.6 shard_map.84
  12.9 7.1 %all-to-all-start = ((bf16[8,24,3072]{2,1,0:T(8,128)(2,1)}), bf16[8,24,3072]{2,1,0:T(8,128)(2,1)S(1)}, u32[]{:S(2)}, u32[]{:S(2)}) async-start(bf16[8,24,3072]{2,1,0:T(8,128)(2,1)} %bitcast.5), calls=%async_computation | async-start | bytes 2359296 | tf_op jit(solution)/shard_map/all_to_all | solution.py:20
  20.0 1.0 dynamic-slice_bitcast_fusion
  21.0 19.4 %collective-permute-start = (bf16[64,2048]{1,0:T(8,128)(2,1)S(1)}, bf16[64,2048]{1,0:T(8,128)(2,1)S(1)}, u32[]{:S(2)}, u32[]{:S(2)}) collective-permute-start(bf16[64,2048]{1,0:T(8,128)(2,1)S(1)} %dynamic-slice_bitcast_fusion), channel_id=1, source_target_pairs={{0,1},{1,0},{2,3},{3,2},{4,5},{5,4},{6,7},{7,6},{8,9},{9,8},{10,11... | collective-permute-start | bytes 786440 | tf_op jit(solution)/shard_map/ppermute | solution.py:92
  40.4 6.3 %collective-permute-done = bf16[64,2048]{1,0:T(8,128)(2,1)S(1)} collective-permute-done((bf16[64,2048]{1,0:T(8,128)(2,1)S(1)}, bf16[64,2048]{1,0:T(8,128)(2,1)S(1)}, u32[]{:S(2)}, u32[]{:S(2)}) %collective-permute-start) | collective-permute-done | bytes 262176 | tf_op jit(solution)/shard_map/ppermute | solution.py:92
  46.7 4.9 %all-to-all-done = bf16[8,24,3072]{2,1,0:T(8,128)(2,1)S(1)} async-done(((bf16[8,24,3072]{2,1,0:T(8,128)(2,1)}), bf16[8,24,3072]{2,1,0:T(8,128)(2,1)S(1)}, u32[]{:S(2)}, u32[]{:S(2)}) %all-to-all-start) | async-done | bytes 1179680 | tf_op jit(solution)/shard_map/all_to_all | solution.py:20
  51.6 1.1 shard_map.85
  52.7 0.0 copy-start
  52.7 1.5 copy-done
  54.2 4.8 %all-to-all-start.1 = ((bf16[8,160,1024]{2,1,0:T(8,128)(2,1)}), bf16[8,160,1024]{2,1,0:T(8,128)(2,1)}, u32[]{:S(2)}, u32[]{:S(2)}) async-start(bf16[8,160,1024]{2,1,0:T(8,128)(2,1)} %copy-done), calls=%async_computation.1 | async-start | bytes 5242880 | tf_op jit(solution)/shard_map/all_to_all | solution.py:20
  59.0 0.0 all-gather.2.cloned.1.call-start
  59.1 0.1 pad_add_fusion.1
  59.2 15.1 %collective-permute-start.1 = (bf16[64,2048]{1,0:T(8,128)(2,1)S(1)}, bf16[64,2048]{1,0:T(8,128)(2,1)S(1)}, u32[]{:S(2)}, u32[]{:S(2)}) collective-permute-start(bf16[64,2048]{1,0:T(8,128)(2,1)S(1)} %collective-permute-done), channel_id=1, source_target_pairs={{0,128},{128,0},{1,129},{129,1},{2,130},{130,2},{3,131},{131,3},{4... | collective-permute-start | bytes 786440 | tf_op jit(solution)/shard_map/ppermute | solution.py:111
  74.3 0.4 convolution_convert_fusion.1
  74.7 0.0 copy-start.8
  74.7 3.7 %broadcast_select_fusion.3 = (bf16[80,1024]{1,0:T(8,128)(2,1)S(1)}, bf16[80,1024]{1,0:T(8,128)(2,1)S(1)}) fusion(pred[80]{0:T(512)(128)(4,1)S(1)} %fusion.35, bf16[1,1024,2048]{2,1,0:T(8,128)(2,1)} %param.8, bf16[80,3072]{1,0:T(8,128)(2,1)S(1)} %convolution_convert_fusion.1), kind=kOutput, calls=%fused_computation.42 | convolution fusion | flops 335790080 | bytes 4850176 | tf_op jit(solution)/shard_map/dot_general | solution.py:24
  78.4 0.0 copy-done.8
  78.4 0.8 fusion.4
  79.3 1.1 convolution_convert_fusion.3
  80.4 0.5 collective-permute-done.1
  80.9 9.0 %all-to-all-done.1 = bf16[8,160,1024]{2,1,0:T(8,128)(2,1)} async-done(((bf16[8,160,1024]{2,1,0:T(8,128)(2,1)}), bf16[8,160,1024]{2,1,0:T(8,128)(2,1)}, u32[]{:S(2)}, u32[]{:S(2)}) %all-to-all-start.1) | async-done | bytes 2621472 | tf_op jit(solution)/shard_map/all_to_all | solution.py:20
  89.9 0.8 pad_maximum_fusion
  90.7 0.0 all-gather.2.cloned.1.call-update
  90.8 0.0 reduce-scatter.2.cloned.1.call-start
  90.8 4.8 %shard_map.86 = f32[1024,512]{1,0:T(8,128)} custom-call(bf16[1280,1024]{1,0:T(8,128)(2,1)} %bitcast.8.rows), custom_call_target="tpu_custom_call" | custom-call | flops 1342177280 | bytes 6291456 | tf_op jit(solution)/shard_map/pallas_call | solution.py:157
  95.6 0.0 reduce-scatter.2.cloned.1.call-update
  95.6 3.5 %all-to-all-start.2 = ((bf16[8,16,2048]{2,1,0:T(8,128)(2,1)}), bf16[8,16,2048]{2,1,0:T(8,128)(2,1)S(1)}, u32[]{:S(2)}, u32[]{:S(2)}) async-start(bf16[8,16,2048]{2,1,0:T(8,128)(2,1)} %bitcast.10), calls=%async_computation.2 | async-start | bytes 1048576 | tf_op jit(solution)/shard_map/all_to_all | solution.py:20
  99.1 17.5 %all-to-all-done.2 = bf16[8,16,2048]{2,1,0:T(8,128)(2,1)S(1)} async-done(((bf16[8,16,2048]{2,1,0:T(8,128)(2,1)}), bf16[8,16,2048]{2,1,0:T(8,128)(2,1)S(1)}, u32[]{:S(2)}, u32[]{:S(2)}) %all-to-all-start.2) | async-done | bytes 524320 | tf_op jit(solution)/shard_map/all_to_all | solution.py:20
  116.6 0.3 convolution_convert_fusion
  117.0 26.7 %all-gather.2.cloned.1.call-done = bf16[2,512,2048]{2,1,0:T(8,128)(2,1)} async-done(((bf16[2,64,2048]{2,1,0:T(8,128)(2,1)}), bf16[2,512,2048]{2,1,0:T(8,128)(2,1)}) %all-gather.2.cloned.1.call-update) | async-done | bytes 4194320 | tf_op jit(solution)/shard_map/all_gather | solution.py:156
  143.6 0.0 copy-start.9
  143.6 3.2 %convolution_convert_fusion.4 = bf16[80,2048]{1,0:T(8,128)(2,1)S(1)} fusion(bf16[1024,2048]{1,0:T(8,128)(2,1)} %bitcast.73, bf16[80,3072]{1,0:T(8,128)(2,1)S(1)} %convolution_convert_fusion), kind=kOutput, calls=%fused_computation.9 | convolution fusion | flops 335708160 | bytes 4685824 | tf_op jit(solution)/shard_map/dot_general | solution.py:24
  146.8 0.3 copy-done.9
  147.1 1.4 broadcast_select_fusion.1
  148.5 0.0 copy-start.5
  148.5 1.1 convolution_convert_fusion.2
  149.6 0.0 copy-start.2
  149.6 0.0 copy-start.7
  149.6 6.9 %all-to-all-start.3 = ((bf16[8,16,2048]{2,1,0:T(8,128)(2,1)}), bf16[8,16,2048]{2,1,0:T(8,128)(2,1)S(1)}, u32[]{:S(2)}, u32[]{:S(2)}) async-start(bf16[8,16,2048]{2,1,0:T(8,128)(2,1)} %bitcast.15), calls=%async_computation.3 | async-start | bytes 1048576 | tf_op jit(solution)/shard_map/all_to_all | solution.py:20
  156.5 0.0 copy-done.5
  156.6 27.9 %reduce-scatter.2.cloned.1.call-done = f32[64,512]{1,0:T(8,128)} async-done(((f32[1024,512]{1,0:T(8,128)}), f32[64,512]{1,0:T(8,128)}) %reduce-scatter.2.cloned.1.call-update) | async-done | bytes 131088 | tf_op jit(solution)/shard_map/reduce_scatter | solution.py:167
  184.4 0.0 all-to-all-done.3
  184.4 0.8 constant_dynamic-slice_fusion
  185.2 2.5 %collective-permute-start.2 = (f32[16,512]{1,0:T(8,128)S(1)}, f32[16,512]{1,0:T(8,128)S(1)}, u32[]{:S(2)}, u32[]{:S(2)}) collective-permute-start(f32[16,512]{1,0:T(8,128)S(1)} %get-tuple-element.46), channel_id=1, source_target_pairs={{0,96},{32,64},{64,32},{96,0},{1,97},{33,65},{65,33},{97,1},{2,98}... | collective-permute-start | bytes 98312 | tf_op jit(solution)/shard_map/ppermute | solution.py:194
  187.8 4.7 %collective-permute-start.3 = (f32[16,512]{1,0:T(8,128)S(1)}, f32[16,512]{1,0:T(8,128)S(1)}, u32[]{:S(2)}, u32[]{:S(2)}) collective-permute-start(f32[16,512]{1,0:T(8,128)S(1)} %get-tuple-element.45), channel_id=1, source_target_pairs={{0,64},{32,96},{64,0},{96,32},{1,65},{33,97},{65,1},{97,33},{2,66}... | collective-permute-start | bytes 98312 | tf_op jit(solution)/shard_map/ppermute | solution.py:194
  192.5 2.6 %collective-permute-start.4 = (f32[16,512]{1,0:T(8,128)S(1)}, f32[16,512]{1,0:T(8,128)S(1)}, u32[]{:S(2)}, u32[]{:S(2)}) collective-permute-start(f32[16,512]{1,0:T(8,128)S(1)} %get-tuple-element.44), channel_id=1, source_target_pairs={{0,32},{32,0},{64,96},{96,64},{1,33},{33,1},{65,97},{97,65},{2,34}... | collective-permute-start | bytes 98312 | tf_op jit(solution)/shard_map/ppermute | solution.py:194
  195.1 0.5 fusion.10
  195.6 0.0 copy-done.2
  195.6 0.0 copy-done.7
  195.6 1.5 multiply_reduce_fusion
  197.0 0.9 fusion.24
  197.9 0.0 collective-permute-done.2
  197.9 0.0 collective-permute-done.3
  197.9 0.4 collective-permute-done.4
  198.3 0.8 select_select_fusion.3
  199.1 0.7 maximum_bitcast_fusion
  (9 shorter events, 0.1 us)
Async XLA Ops:
  8.0 1.0 copy-start.1
  9.0 0.9 copy-start.3
  10.0 0.7 copy-start.4
  10.6 0.7 copy-start.6
  12.9 38.7 %all-to-all-start = ((bf16[8,24,3072]{2,1,0:T(8,128)(2,1)}), bf16[8,24,3072]{2,1,0:T(8,128)(2,1)S(1)}, u32[]{:S(2)}, u32[]{:S(2)}) async-start(bf16[8,24,3072]{2,1,0:T(8,128)(2,1)} %bitcast.5), calls=%async_computation | async-start | bytes 2359296 | tf_op jit(solution)/shard_map/all_to_all | solution.py:20
  21.0 25.7 %collective-permute-start = (bf16[64,2048]{1,0:T(8,128)(2,1)S(1)}, bf16[64,2048]{1,0:T(8,128)(2,1)S(1)}, u32[]{:S(2)}, u32[]{:S(2)}) collective-permute-start(bf16[64,2048]{1,0:T(8,128)(2,1)S(1)} %dynamic-slice_bitcast_fusion), channel_id=1, source_target_pairs={{0,1},{1,0},{2,3},{3,2},{4,5},{5,4},{6,7},{7,6},{8,9},{9,8},{10,11... | collective-permute-start | bytes 786440 | tf_op jit(solution)/shard_map/ppermute | solution.py:92
  52.7 1.5 copy-start
  54.2 35.7 %all-to-all-start.1 = ((bf16[8,160,1024]{2,1,0:T(8,128)(2,1)}), bf16[8,160,1024]{2,1,0:T(8,128)(2,1)}, u32[]{:S(2)}, u32[]{:S(2)}) async-start(bf16[8,160,1024]{2,1,0:T(8,128)(2,1)} %copy-done), calls=%async_computation.1 | async-start | bytes 5242880 | tf_op jit(solution)/shard_map/all_to_all | solution.py:20
  59.0 84.6 %all-gather.2.cloned.1.call-start = ((), (), s32[]{:S(2)}) async-start(), calls=%async_computation.5 | async-start | bytes 4718592 | tf_op jit(solution)/shard_map/all_gather | solution.py:156
  59.2 21.7 %collective-permute-start.1 = (bf16[64,2048]{1,0:T(8,128)(2,1)S(1)}, bf16[64,2048]{1,0:T(8,128)(2,1)S(1)}, u32[]{:S(2)}, u32[]{:S(2)}) collective-permute-start(bf16[64,2048]{1,0:T(8,128)(2,1)S(1)} %collective-permute-done), channel_id=1, source_target_pairs={{0,128},{128,0},{1,129},{129,1},{2,130},{130,2},{3,131},{131,3},{4... | collective-permute-start | bytes 786440 | tf_op jit(solution)/shard_map/ppermute | solution.py:111
  74.7 3.8 %copy-start.8 = (bf16[1,1024,2048]{2,1,0:T(8,128)(2,1)S(1)}, bf16[1,1024,2048]{2,1,0:T(8,128)(2,1)}, u32[]{:S(2)}) copy-start(bf16[1,1024,2048]{2,1,0:T(8,128)(2,1)} %param.8) | copy-start | bytes 12582916
  90.8 93.7 %reduce-scatter.2.cloned.1.call-start = ((), (), s32[]{:S(2)}) async-start(), calls=%async_computation.6 | async-start | bytes 2228224 | tf_op jit(solution)/shard_map/reduce_scatter | solution.py:167
  95.6 21.0 %all-to-all-start.2 = ((bf16[8,16,2048]{2,1,0:T(8,128)(2,1)}), bf16[8,16,2048]{2,1,0:T(8,128)(2,1)S(1)}, u32[]{:S(2)}, u32[]{:S(2)}) async-start(bf16[8,16,2048]{2,1,0:T(8,128)(2,1)} %bitcast.10), calls=%async_computation.2 | async-start | bytes 1048576 | tf_op jit(solution)/shard_map/all_to_all | solution.py:20
  143.6 3.5 %copy-start.9 = (bf16[2,512,2048]{2,1,0:T(8,128)(2,1)S(1)}, bf16[2,512,2048]{2,1,0:T(8,128)(2,1)}, u32[]{:S(2)}) copy-start(bf16[2,512,2048]{2,1,0:T(8,128)(2,1)} %all-gather.2.cloned.1.call-done) | copy-start | bytes 12582916
  148.5 8.0 %copy-start.5 = (s32[128,1]{0,1:T(1,128)S(1)}, s32[128,1]{0,1:T(1,128)}, u32[]{:S(2)}) copy-start(s32[128,1]{0,1:T(1,128)} %param.6) | copy-start | bytes 1540
  149.6 45.9 %copy-start.2 = (bf16[128,2048]{1,0:T(8,128)(2,1)S(1)}, bf16[128,2048]{1,0:T(8,128)(2,1)}, u32[]{:S(2)}) copy-start(bf16[128,2048]{1,0:T(8,128)(2,1)} %out_grad.1) | copy-start | bytes 1572868
  149.6 46.0 %copy-start.7 = (f32[128,1]{0,1:T(1,128)S(1)}, f32[128,1]{0,1:T(1,128)}, u32[]{:S(2)}) copy-start(f32[128,1]{0,1:T(1,128)} %param.7) | copy-start | bytes 1540
  149.6 34.8 %all-to-all-start.3 = ((bf16[8,16,2048]{2,1,0:T(8,128)(2,1)}), bf16[8,16,2048]{2,1,0:T(8,128)(2,1)S(1)}, u32[]{:S(2)}, u32[]{:S(2)}) async-start(bf16[8,16,2048]{2,1,0:T(8,128)(2,1)} %bitcast.15), calls=%async_computation.3 | async-start | bytes 1048576 | tf_op jit(solution)/shard_map/all_to_all | solution.py:20
  185.2 12.7 %collective-permute-start.2 = (f32[16,512]{1,0:T(8,128)S(1)}, f32[16,512]{1,0:T(8,128)S(1)}, u32[]{:S(2)}, u32[]{:S(2)}) collective-permute-start(f32[16,512]{1,0:T(8,128)S(1)} %get-tuple-element.46), channel_id=1, source_target_pairs={{0,96},{32,64},{64,32},{96,0},{1,97},{33,65},{65,33},{97,1},{2,98}... | collective-permute-start | bytes 98312 | tf_op jit(solution)/shard_map/ppermute | solution.py:194
  187.8 10.1 %collective-permute-start.3 = (f32[16,512]{1,0:T(8,128)S(1)}, f32[16,512]{1,0:T(8,128)S(1)}, u32[]{:S(2)}, u32[]{:S(2)}) collective-permute-start(f32[16,512]{1,0:T(8,128)S(1)} %get-tuple-element.45), channel_id=1, source_target_pairs={{0,64},{32,96},{64,0},{96,32},{1,65},{33,97},{65,1},{97,33},{2,66}... | collective-permute-start | bytes 98312 | tf_op jit(solution)/shard_map/ppermute | solution.py:194
  192.5 5.8 %collective-permute-start.4 = (f32[16,512]{1,0:T(8,128)S(1)}, f32[16,512]{1,0:T(8,128)S(1)}, u32[]{:S(2)}, u32[]{:S(2)}) collective-permute-start(f32[16,512]{1,0:T(8,128)S(1)} %get-tuple-element.44), channel_id=1, source_target_pairs={{0,32},{32,0},{64,96},{96,64},{1,33},{33,1},{65,97},{97,65},{2,34}... | collective-permute-start | bytes 98312 | tf_op jit(solution)/shard_map/ppermute | solution.py:194
Sparse Core Ops, SparseCore 0:
  90.9 52.6 all-gather.1
Sparse Core Ops, SparseCore 1:
  95.7 88.7 reduce-scatter.1
